TPU v7x, 512 devices: a whole 4x8x8 slice. The times are simulated.
512 devices in a mesh: shard: 32 (over y, x), grp: 16 (over z, core).
Axes of the slice: x: 4, y: 8, z: 8, core: 2. Of those that a mesh axis runs over, the one named last changes fastest.
Arguments:
- embeddings: bfloat16 [262144, 768], P(('shard', 'grp'))
- cluster_ids: int32 [512], P(('shard', 'grp')), may hold values from 0 to 73, as said below
Outputs:
- max_sim: float32 [262144], P(('shard', 'grp'))
- log_mass: float32 [262144], P(('shard', 'grp'))
- centroid_cos: float32 [262144], P(('shard', 'grp'))
Inputs may be any that keep to these rules, and one draw needn't show every extreme that they name: `cluster_ids`: cluster ids begin at 0 on the first block, never fall along the blocks and rise by one from each cluster to the next; every cluster holds 6 to 8 consecutive blocks, and some cluster holds exactly 8.
All inputs are finite; a program needn't handle non-finite values.
Results may differ from a plain program's by a relative error of at most 0.00053.
Values may be sent and summed in bfloat16 or wider, within the bound.
No kernel may reach another device: no remote copies, remote signals or barrier semaphores. Data moves between devices by JAX's collectives and lax.ppermute only.
A program may use at most 64 MiB of HBM per device.

v0:
```python
import math

import jax
import jax.numpy as jnp
from jax import lax
from jax.sharding import PartitionSpec as P

CMAX = 8


TAU = 0.05


def passed_along(value, axis, steps):
    count = lax.axis_size(axis)
    leading, last = (max(0, -steps), min(count, count - steps))
    return lax.ppermute(value, axis, [(source, source + steps) for source in range(leading, last)])


def unit_rows(values):
    floats = values.astype(jnp.float32)
    scale = lax.rsqrt(jnp.mean(floats * floats, axis=-1, keepdims=True) + 1e-06) / math.sqrt(
        floats.shape[-1]
    )
    return (floats * scale).astype(jnp.bfloat16)


def tile_stats(left, right, keep, diagonal):
    rows = left.shape[0]

    def compute(unused):
        sims = jnp.dot(left, right.T, preferred_element_type=jnp.float32)
        weights = jnp.exp(sims / TAU)
        if diagonal:
            same = jnp.arange(rows)[:, None] == jnp.arange(rows)[None, :]
            sims = jnp.where(same, -2.0, sims)
            weights = jnp.where(same, 0.0, weights)
        return (
            jnp.max(sims, axis=1),
            jnp.sum(weights, axis=1),
            jnp.max(sims, axis=0),
            jnp.sum(weights, axis=0),
        )

    def empty(unused):
        low = jnp.full((rows,), -2.0, jnp.float32)
        nothing = jnp.zeros((rows,), jnp.float32)
        return (low, nothing, low, nothing)

    return lax.cond(keep, compute, empty, 0)


def per_device(embeddings, cluster_ids):
    width = embeddings.shape[1]
    unit = unit_rows(embeddings)
    marker = (cluster_ids + 1).astype(jnp.bfloat16)
    own_mark = marker.astype(jnp.float32)[0]
    rmax, rsum, cmax, csum = tile_stats(unit, unit, jnp.bool_(True), True)
    row_max = rmax
    row_sum = rsum
    partners = []
    for offset in range(1, CMAX):
        partners.append(passed_along((unit, marker), ("shard", "grp"), -offset))
    column_parts = []
    for offset in range(1, CMAX):
        block, pmark = partners[offset - 1]
        keep = pmark.astype(jnp.float32)[0] == own_mark
        rmax, rsum, cmax, csum = tile_stats(unit, block, keep, False)
        row_max = jnp.maximum(row_max, rmax)
        row_sum = row_sum + rsum
        column_parts.append((cmax + 2.0, csum))
    for offset in range(1, CMAX):
        lifted, moved = passed_along(column_parts[offset - 1], ("shard", "grp"), offset)
        row_max = jnp.maximum(row_max, lifted - 2.0)
        row_sum = row_sum + moved
    unit_float = unit.astype(jnp.float32)
    block_sum = jnp.sum(unit_float, axis=0)
    tag_float = cluster_ids.astype(jnp.float32)
    total = block_sum
    for offset in range(-(CMAX - 1), CMAX):
        if offset != 0:
            vector, tag = passed_along((block_sum, tag_float), ("shard", "grp"), offset)
            total = total + vector * jnp.where(tag[0] == tag_float[0], 1.0, 0.0)
    centre = total * lax.rsqrt(jnp.mean(total * total) + 1e-06) / math.sqrt(width)
    cosines = jnp.sum(unit_float * centre[None, :], axis=-1)
    return (row_max, jnp.log(row_sum), cosines)


def solution(mesh):
    in_specs = (P(("shard", "grp"), None), P(("shard", "grp")))
    out_specs = (P(("shard", "grp")), P(("shard", "grp")), P(("shard", "grp")))
    return jax.shard_map(
        per_device, mesh=mesh, in_specs=in_specs, out_specs=out_specs, check_vma=False
    )
```

profile of v0, /device:TPU:82, one launch (start us, length us, event | category | flops | bytes accessed | tf_op | source)
XLA Modules:
  0.0 497.5 jit_solution(14885834558202859404)
XLA Ops:
  2.4 1.9 collective-permute-start.1
  4.3 10.1 %collective-permute-start.28 = (f32[768]{0:T(1024)S(1)}, f32[768]{0:T(1024)S(1)}, u32[]{:S(2)}, u32[]{:S(2)}) collective-permute-start(f32[768]{0:T(1024)S(1)} %get-tuple-element.133), channel_id=1, source_target_pairs={{7,0},{8,1},{9,2},{10,3},{11,4},{12,5},{13,6},{14,7},{15,8},{16,9}... | collective-permute-start | bytes 9224 | tf_op jit(solution)/shard_map/ppermute | solution.py:17
  14.4 1.9 collective-permute-start.30
  17.0 3.5 collective-permute-start
  20.4 5.1 %collective-permute-start.2 = (bf16[1]{0:T(256)(128)(2,1)}, bf16[1]{0:T(256)(128)(2,1)}, u32[]{:S(2)}, u32[]{:S(2)}) collective-permute-start(bf16[1]{0:T(256)(128)(2,1)} %convert_element_type.83), channel_id=1, source_target_pairs={{2,0},{3,1},{4,2},{5,3},{6,4},{7,5},{8,6},{9,7},{10,8},{11,9},{12,... | collective-permute-start | bytes 14 | tf_op jit(solution)/shard_map/ppermute | solution.py:17
  25.6 8.5 %collective-permute-start.4 = (bf16[1]{0:T(256)(128)(2,1)}, bf16[1]{0:T(256)(128)(2,1)}, u32[]{:S(2)}, u32[]{:S(2)}) collective-permute-start(bf16[1]{0:T(256)(128)(2,1)} %convert_element_type.83), channel_id=1, source_target_pairs={{3,0},{4,1},{5,2},{6,3},{7,4},{8,5},{9,6},{10,7},{11,8},{12,9},{13... | collective-permute-start | bytes 14 | tf_op jit(solution)/shard_map/ppermute | solution.py:17
  34.0 4.7 collective-permute-start.6
  38.7 3.7 collective-permute-start.8
  42.4 7.2 %collective-permute-start.10 = (bf16[1]{0:T(256)(128)(2,1)}, bf16[1]{0:T(256)(128)(2,1)}, u32[]{:S(2)}, u32[]{:S(2)}) collective-permute-start(bf16[1]{0:T(256)(128)(2,1)} %convert_element_type.83), channel_id=1, source_target_pairs={{6,0},{7,1},{8,2},{9,3},{10,4},{11,5},{12,6},{13,7},{14,8},{15,9},... | collective-permute-start | bytes 14 | tf_op jit(solution)/shard_map/ppermute | solution.py:17
  49.6 3.3 collective-permute-start.12
  52.9 6.0 %collective-permute-start.35 = (f32[1]{0:T(128)}, f32[1]{0:T(128)}, u32[]{:S(2)}, u32[]{:S(2)}) collective-permute-start(f32[1]{0:T(128)} %convert_element_type.107), channel_id=1, source_target_pairs={{4,0},{5,1},{6,2},{7,3},{8,4},{9,5},{10,6},{11,7},{12,8},{13,9},{1... | collective-permute-start | bytes 20 | tf_op jit(solution)/shard_map/ppermute | solution.py:17
  58.9 7.0 %collective-permute-start.37 = (f32[1]{0:T(128)}, f32[1]{0:T(128)}, u32[]{:S(2)}, u32[]{:S(2)}) collective-permute-start(f32[1]{0:T(128)} %convert_element_type.107), channel_id=1, source_target_pairs={{3,0},{4,1},{5,2},{6,3},{7,4},{8,5},{9,6},{10,7},{11,8},{12,9},{13... | collective-permute-start | bytes 20 | tf_op jit(solution)/shard_map/ppermute | solution.py:17
  65.9 3.2 collective-permute-start.39
  69.1 3.2 collective-permute-start.41
  72.3 2.9 collective-permute-start.43
  75.2 5.2 %collective-permute-start.45 = (f32[1]{0:T(128)}, f32[1]{0:T(128)}, u32[]{:S(2)}, u32[]{:S(2)}) collective-permute-start(f32[1]{0:T(128)} %convert_element_type.107), channel_id=1, source_target_pairs={{0,2},{1,3},{2,4},{3,5},{4,6},{5,7},{6,8},{7,9},{8,10},{9,11},{10,... | collective-permute-start | bytes 20 | tf_op jit(solution)/shard_map/ppermute | solution.py:17
  80.4 3.2 collective-permute-start.47
  83.6 3.9 collective-permute-start.49
  88.4 3.6 collective-permute-start.51
  92.0 4.8 collective-permute-start.53
  97.2 4.7 collective-permute-start.55
  101.9 7.6 %collective-permute-start.29 = (f32[1]{0:T(128)}, f32[1]{0:T(128)}, u32[]{:S(2)}, u32[]{:S(2)}) collective-permute-start(f32[1]{0:T(128)} %convert_element_type.107), channel_id=1, source_target_pairs={{7,0},{8,1},{9,2},{10,3},{11,4},{12,5},{13,6},{14,7},{15,8},{16,9}... | collective-permute-start | bytes 20 | tf_op jit(solution)/shard_map/ppermute | solution.py:17
  109.6 7.9 %collective-permute-start.31 = (f32[1]{0:T(128)}, f32[1]{0:T(128)}, u32[]{:S(2)}, u32[]{:S(2)}) collective-permute-start(f32[1]{0:T(128)} %convert_element_type.107), channel_id=1, source_target_pairs={{6,0},{7,1},{8,2},{9,3},{10,4},{11,5},{12,6},{13,7},{14,8},{15,9},... | collective-permute-start | bytes 20 | tf_op jit(solution)/shard_map/ppermute | solution.py:17
  117.5 8.3 %collective-permute-start.33 = (f32[1]{0:T(128)}, f32[1]{0:T(128)}, u32[]{:S(2)}, u32[]{:S(2)}) collective-permute-start(f32[1]{0:T(128)} %convert_element_type.107), channel_id=1, source_target_pairs={{5,0},{6,1},{7,2},{8,3},{9,4},{10,5},{11,6},{12,7},{13,8},{14,9},{... | collective-permute-start | bytes 20 | tf_op jit(solution)/shard_map/ppermute | solution.py:17
  125.8 5.4 %collective-permute-start.32 = (f32[768]{0:T(1024)S(1)}, f32[768]{0:T(1024)S(1)}, u32[]{:S(2)}, u32[]{:S(2)}) collective-permute-start(f32[768]{0:T(1024)S(1)} %get-tuple-element.133), channel_id=1, source_target_pairs={{5,0},{6,1},{7,2},{8,3},{9,4},{10,5},{11,6},{12,7},{13,8},{14,9},{... | collective-permute-start | bytes 9224 | tf_op jit(solution)/shard_map/ppermute | solution.py:17
  131.2 1.9 collective-permute-start.34
  133.2 7.2 %collective-permute-start.36 = (f32[768]{0:T(1024)S(1)}, f32[768]{0:T(1024)S(1)}, u32[]{:S(2)}, u32[]{:S(2)}) collective-permute-start(f32[768]{0:T(1024)S(1)} %get-tuple-element.133), channel_id=1, source_target_pairs={{3,0},{4,1},{5,2},{6,3},{7,4},{8,5},{9,6},{10,7},{11,8},{12,9},{13... | collective-permute-start | bytes 9224 | tf_op jit(solution)/shard_map/ppermute | solution.py:17
  140.4 1.9 collective-permute-start.38
  142.4 2.8 collective-permute-start.40
  145.2 2.0 collective-permute-start.42
  147.3 3.5 collective-permute-start.44
  150.8 4.8 collective-permute-start.46
  155.7 3.4 collective-permute-start.48
  159.0 1.9 collective-permute-start.50
  161.0 1.9 collective-permute-start.52
  162.9 2.2 collective-permute-start.54
  165.1 3.4 collective-permute-start.3
  168.5 6.1 %collective-permute-start.5 = (bf16[512,768]{1,0:T(8,128)(2,1)S(1)}, bf16[512,768]{1,0:T(8,128)(2,1)}, u32[]{:S(2)}, u32[]{:S(2)}) collective-permute-start(bf16[512,768]{1,0:T(8,128)(2,1)S(1)} %get-tuple-element.134), channel_id=1, source_target_pairs={{3,0},{4,1},{5,2},{6,3},{7,4},{8,5},{9,6},{10,7},{11,8},{12,9},{13... | collective-permute-start | bytes 2359304 | tf_op jit(solution)/shard_map/ppermute | solution.py:17
  174.6 4.5 collective-permute-start.7
  179.2 5.8 %collective-permute-start.9 = (bf16[512,768]{1,0:T(8,128)(2,1)S(1)}, bf16[512,768]{1,0:T(8,128)(2,1)S(1)}, u32[]{:S(2)}, u32[]{:S(2)}) collective-permute-start(bf16[512,768]{1,0:T(8,128)(2,1)S(1)} %get-tuple-element.134), channel_id=1, source_target_pairs={{5,0},{6,1},{7,2},{8,3},{9,4},{10,5},{11,6},{12,7},{13,8},{14,9},{... | collective-permute-start | bytes 2359304 | tf_op jit(solution)/shard_map/ppermute | solution.py:17
  200.3 9.7 %collective-permute-start.11 = (bf16[512,768]{1,0:T(8,128)(2,1)S(1)}, bf16[512,768]{1,0:T(8,128)(2,1)}, u32[]{:S(2)}, u32[]{:S(2)}) collective-permute-start(bf16[512,768]{1,0:T(8,128)(2,1)S(1)} %get-tuple-element.134), channel_id=1, source_target_pairs={{6,0},{7,1},{8,2},{9,3},{10,4},{11,5},{12,6},{13,7},{14,8},{15,9},... | collective-permute-start | bytes 2359304 | tf_op jit(solution)/shard_map/ppermute | solution.py:17
  211.6 2.3 collective-permute-start.13
  213.9 2.0 conditional.8
  213.9 1.9 fusion.2
  215.9 1.9 collective-permute-start.21
  217.8 2.0 conditional.9
  217.8 1.9 fusion.4
  219.8 13.3 %collective-permute-done.7 = bf16[512,768]{1,0:T(8,128)(2,1)S(1)} collective-permute-done((bf16[512,768]{1,0:T(8,128)(2,1)S(1)}, bf16[512,768]{1,0:T(8,128)(2,1)S(1)}, u32[]{:S(2)}, u32[]{:S(2)}) %collective-permute-start.7) | collective-permute-done | bytes 786464 | tf_op jit(solution)/shard_map/ppermute | solution.py:17
  233.0 23.3 %collective-permute-start.22 = (f32[512]{0:T(512)S(1)}, f32[512]{0:T(512)S(1)}, u32[]{:S(2)}, u32[]{:S(2)}) collective-permute-start(f32[512]{0:T(512)S(1)} %get-tuple-element.95), channel_id=1, source_target_pairs={{0,2},{1,3},{2,4},{3,5},{4,6},{5,7},{6,8},{7,9},{8,10},{9,11},{10,... | collective-permute-start | bytes 6152 | tf_op jit(solution)/shard_map/ppermute | solution.py:17
  257.2 31.7 %collective-permute-done.9 = bf16[512,768]{1,0:T(8,128)(2,1)S(1)} collective-permute-done((bf16[512,768]{1,0:T(8,128)(2,1)S(1)}, bf16[512,768]{1,0:T(8,128)(2,1)S(1)}, u32[]{:S(2)}, u32[]{:S(2)}) %collective-permute-start.9) | collective-permute-done | bytes 786464 | tf_op jit(solution)/shard_map/ppermute | solution.py:17
  288.9 7.2 %collective-permute-start.23 = (f32[512]{0:T(512)S(1)}, f32[512]{0:T(512)S(1)}, u32[]{:S(2)}, u32[]{:S(2)}) collective-permute-start(f32[512]{0:T(512)S(1)} %get-tuple-element.96), channel_id=1, source_target_pairs={{0,3},{1,4},{2,5},{3,6},{4,7},{5,8},{6,9},{7,10},{8,11},{9,12},{10... | collective-permute-start | bytes 6152 | tf_op jit(solution)/shard_map/ppermute | solution.py:17
  297.0 49.6 %collective-permute-done.11 = bf16[512,768]{1,0:T(8,128)(2,1)} collective-permute-done((bf16[512,768]{1,0:T(8,128)(2,1)S(1)}, bf16[512,768]{1,0:T(8,128)(2,1)}, u32[]{:S(2)}, u32[]{:S(2)}) %collective-permute-start.11) | collective-permute-done | bytes 786464 | tf_op jit(solution)/shard_map/ppermute | solution.py:17
  348.5 2.0 conditional.12
  348.6 1.9 fusion.10
  350.6 33.5 %collective-permute-done.13 = bf16[512,768]{1,0:T(8,128)(2,1)} collective-permute-done((bf16[512,768]{1,0:T(8,128)(2,1)S(1)}, bf16[512,768]{1,0:T(8,128)(2,1)}, u32[]{:S(2)}, u32[]{:S(2)}) %collective-permute-start.13) | collective-permute-done | bytes 786464 | tf_op jit(solution)/shard_map/ppermute | solution.py:17
  384.1 6.1 %collective-permute-start.25 = (f32[512]{0:T(512)S(1)}, f32[512]{0:T(512)S(1)}, u32[]{:S(2)}, u32[]{:S(2)}) collective-permute-start(f32[512]{0:T(512)S(1)} %get-tuple-element.98), channel_id=1, source_target_pairs={{0,5},{1,6},{2,7},{3,8},{4,9},{5,10},{6,11},{7,12},{8,13},{9,14},{... | collective-permute-start | bytes 6152 | tf_op jit(solution)/shard_map/ppermute | solution.py:17
  390.2 2.2 collective-permute-start.26
  392.4 8.5 %collective-permute-start.27 = (f32[512]{0:T(512)S(1)}, f32[512]{0:T(512)S(1)}, u32[]{:S(2)}, u32[]{:S(2)}) collective-permute-start(f32[512]{0:T(512)S(1)} %get-tuple-element.100), channel_id=1, source_target_pairs={{0,7},{1,8},{2,9},{3,10},{4,11},{5,12},{6,13},{7,14},{8,15},{9,16}... | collective-permute-start | bytes 6152 | tf_op jit(solution)/shard_map/ppermute | solution.py:17
  400.9 2.3 collective-permute-start.14
  403.2 6.3 %collective-permute-start.15 = (f32[512]{0:T(512)S(1)}, f32[512]{0:T(512)S(1)}, u32[]{:S(2)}, u32[]{:S(2)}) collective-permute-start(f32[512]{0:T(512)S(1)} %broadcast_add_fusion.5), channel_id=1, source_target_pairs={{0,2},{1,3},{2,4},{3,5},{4,6},{5,7},{6,8},{7,9},{8,10},{9,11},{10,... | collective-permute-start | bytes 6152 | tf_op jit(solution)/shard_map/ppermute | solution.py:17
  409.6 6.5 %collective-permute-start.16 = (f32[512]{0:T(512)S(1)}, f32[512]{0:T(512)S(1)}, u32[]{:S(2)}, u32[]{:S(2)}) collective-permute-start(f32[512]{0:T(512)S(1)} %broadcast_add_fusion.4), channel_id=1, source_target_pairs={{0,3},{1,4},{2,5},{3,6},{4,7},{5,8},{6,9},{7,10},{8,11},{9,12},{10... | collective-permute-start | bytes 6152 | tf_op jit(solution)/shard_map/ppermute | solution.py:17
  416.1 1.9 collective-permute-start.17
  420.0 67.2 %collective-permute-start.19 = (f32[512]{0:T(512)S(1)}, f32[512]{0:T(512)S(1)}, u32[]{:S(2)}, u32[]{:S(2)}) collective-permute-start(f32[512]{0:T(512)S(1)} %broadcast_add_fusion.1), channel_id=1, source_target_pairs={{0,6},{1,7},{2,8},{3,9},{4,10},{5,11},{6,12},{7,13},{8,14},{9,15},... | collective-permute-start | bytes 6152 | tf_op jit(solution)/shard_map/ppermute | solution.py:17
  489.7 7.2 %collective-permute-done.20 = f32[512]{0:T(512)S(1)} collective-permute-done((f32[512]{0:T(512)S(1)}, f32[512]{0:T(512)S(1)}, u32[]{:S(2)}, u32[]{:S(2)}) %collective-permute-start.20) | collective-permute-done | bytes 2080 | tf_op jit(solution)/shard_map/ppermute | solution.py:17
  (83 shorter events, 17.3 us)
Async XLA Ops:
  0.6 1.5 copy-start
  2.4 197.9 %collective-permute-start.1 = (bf16[512,768]{1,0:T(8,128)(2,1)S(1)}, bf16[512,768]{1,0:T(8,128)(2,1)S(1)}, u32[]{:S(2)}, u32[]{:S(2)}) collective-permute-start(bf16[512,768]{1,0:T(8,128)(2,1)S(1)} %get-tuple-element.134), channel_id=1, source_target_pairs={{1,0},{2,1},{3,2},{4,3},{5,4},{6,5},{7,6},{8,7},{9,8},{10,9},{11,1... | collective-permute-start | bytes 2359304 | tf_op jit(solution)/shard_map/ppermute | solution.py:17
  4.3 128.9 %collective-permute-start.28 = (f32[768]{0:T(1024)S(1)}, f32[768]{0:T(1024)S(1)}, u32[]{:S(2)}, u32[]{:S(2)}) collective-permute-start(f32[768]{0:T(1024)S(1)} %get-tuple-element.133), channel_id=1, source_target_pairs={{7,0},{8,1},{9,2},{10,3},{11,4},{12,5},{13,6},{14,7},{15,8},{16,9}... | collective-permute-start | bytes 9224 | tf_op jit(solution)/shard_map/ppermute | solution.py:17
  14.4 126.0 %collective-permute-start.30 = (f32[768]{0:T(1024)S(1)}, f32[768]{0:T(1024)S(1)}, u32[]{:S(2)}, u32[]{:S(2)}) collective-permute-start(f32[768]{0:T(1024)S(1)} %get-tuple-element.133), channel_id=1, source_target_pairs={{6,0},{7,1},{8,2},{9,3},{10,4},{11,5},{12,6},{13,7},{14,8},{15,9},... | collective-permute-start | bytes 9224 | tf_op jit(solution)/shard_map/ppermute | solution.py:17
  17.0 8.6 %collective-permute-start = (bf16[1]{0:T(256)(128)(2,1)}, bf16[1]{0:T(256)(128)(2,1)}, u32[]{:S(2)}, u32[]{:S(2)}) collective-permute-start(bf16[1]{0:T(256)(128)(2,1)} %convert_element_type.83), channel_id=1, source_target_pairs={{1,0},{2,1},{3,2},{4,3},{5,4},{6,5},{7,6},{8,7},{9,8},{10,9},{11,1... | collective-permute-start | bytes 14 | tf_op jit(solution)/shard_map/ppermute | solution.py:17
  20.4 13.6 %collective-permute-start.2 = (bf16[1]{0:T(256)(128)(2,1)}, bf16[1]{0:T(256)(128)(2,1)}, u32[]{:S(2)}, u32[]{:S(2)}) collective-permute-start(bf16[1]{0:T(256)(128)(2,1)} %convert_element_type.83), channel_id=1, source_target_pairs={{2,0},{3,1},{4,2},{5,3},{6,4},{7,5},{8,6},{9,7},{10,8},{11,9},{12,... | collective-permute-start | bytes 14 | tf_op jit(solution)/shard_map/ppermute | solution.py:17
  25.6 13.2 %collective-permute-start.4 = (bf16[1]{0:T(256)(128)(2,1)}, bf16[1]{0:T(256)(128)(2,1)}, u32[]{:S(2)}, u32[]{:S(2)}) collective-permute-start(bf16[1]{0:T(256)(128)(2,1)} %convert_element_type.83), channel_id=1, source_target_pairs={{3,0},{4,1},{5,2},{6,3},{7,4},{8,5},{9,6},{10,7},{11,8},{12,9},{13... | collective-permute-start | bytes 14 | tf_op jit(solution)/shard_map/ppermute | solution.py:17
  34.0 8.4 %collective-permute-start.6 = (bf16[1]{0:T(256)(128)(2,1)}, bf16[1]{0:T(256)(128)(2,1)}, u32[]{:S(2)}, u32[]{:S(2)}) collective-permute-start(bf16[1]{0:T(256)(128)(2,1)} %convert_element_type.83), channel_id=1, source_target_pairs={{4,0},{5,1},{6,2},{7,3},{8,4},{9,5},{10,6},{11,7},{12,8},{13,9},{1... | collective-permute-start | bytes 14 | tf_op jit(solution)/shard_map/ppermute | solution.py:17
  38.7 10.9 %collective-permute-start.8 = (bf16[1]{0:T(256)(128)(2,1)}, bf16[1]{0:T(256)(128)(2,1)}, u32[]{:S(2)}, u32[]{:S(2)}) collective-permute-start(bf16[1]{0:T(256)(128)(2,1)} %convert_element_type.83), channel_id=1, source_target_pairs={{5,0},{6,1},{7,2},{8,3},{9,4},{10,5},{11,6},{12,7},{13,8},{14,9},{... | collective-permute-start | bytes 14 | tf_op jit(solution)/shard_map/ppermute | solution.py:17
  42.4 10.5 %collective-permute-start.10 = (bf16[1]{0:T(256)(128)(2,1)}, bf16[1]{0:T(256)(128)(2,1)}, u32[]{:S(2)}, u32[]{:S(2)}) collective-permute-start(bf16[1]{0:T(256)(128)(2,1)} %convert_element_type.83), channel_id=1, source_target_pairs={{6,0},{7,1},{8,2},{9,3},{10,4},{11,5},{12,6},{13,7},{14,8},{15,9},... | collective-permute-start | bytes 14 | tf_op jit(solution)/shard_map/ppermute | solution.py:17
  49.6 9.3 %collective-permute-start.12 = (bf16[1]{0:T(256)(128)(2,1)}, bf16[1]{0:T(256)(128)(2,1)}, u32[]{:S(2)}, u32[]{:S(2)}) collective-permute-start(bf16[1]{0:T(256)(128)(2,1)} %convert_element_type.83), channel_id=1, source_target_pairs={{7,0},{8,1},{9,2},{10,3},{11,4},{12,5},{13,6},{14,7},{15,8},{16,9}... | collective-permute-start | bytes 14 | tf_op jit(solution)/shard_map/ppermute | solution.py:17
  52.9 13.0 %collective-permute-start.35 = (f32[1]{0:T(128)}, f32[1]{0:T(128)}, u32[]{:S(2)}, u32[]{:S(2)}) collective-permute-start(f32[1]{0:T(128)} %convert_element_type.107), channel_id=1, source_target_pairs={{4,0},{5,1},{6,2},{7,3},{8,4},{9,5},{10,6},{11,7},{12,8},{13,9},{1... | collective-permute-start | bytes 20 | tf_op jit(solution)/shard_map/ppermute | solution.py:17
  58.9 10.2 %collective-permute-start.37 = (f32[1]{0:T(128)}, f32[1]{0:T(128)}, u32[]{:S(2)}, u32[]{:S(2)}) collective-permute-start(f32[1]{0:T(128)} %convert_element_type.107), channel_id=1, source_target_pairs={{3,0},{4,1},{5,2},{6,3},{7,4},{8,5},{9,6},{10,7},{11,8},{12,9},{13... | collective-permute-start | bytes 20 | tf_op jit(solution)/shard_map/ppermute | solution.py:17
  65.9 6.4 %collective-permute-start.39 = (f32[1]{0:T(128)}, f32[1]{0:T(128)}, u32[]{:S(2)}, u32[]{:S(2)}) collective-permute-start(f32[1]{0:T(128)} %convert_element_type.107), channel_id=1, source_target_pairs={{2,0},{3,1},{4,2},{5,3},{6,4},{7,5},{8,6},{9,7},{10,8},{11,9},{12,... | collective-permute-start | bytes 20 | tf_op jit(solution)/shard_map/ppermute | solution.py:17
  69.1 6.1 %collective-permute-start.41 = (f32[1]{0:T(128)}, f32[1]{0:T(128)}, u32[]{:S(2)}, u32[]{:S(2)}) collective-permute-start(f32[1]{0:T(128)} %convert_element_type.107), channel_id=1, source_target_pairs={{1,0},{2,1},{3,2},{4,3},{5,4},{6,5},{7,6},{8,7},{9,8},{10,9},{11,1... | collective-permute-start | bytes 20 | tf_op jit(solution)/shard_map/ppermute | solution.py:17
  72.3 8.1 %collective-permute-start.43 = (f32[1]{0:T(128)}, f32[1]{0:T(128)}, u32[]{:S(2)}, u32[]{:S(2)}) collective-permute-start(f32[1]{0:T(128)} %convert_element_type.107), channel_id=1, source_target_pairs={{0,1},{1,2},{2,3},{3,4},{4,5},{5,6},{6,7},{7,8},{8,9},{9,10},{10,1... | collective-permute-start | bytes 20 | tf_op jit(solution)/shard_map/ppermute | solution.py:17
  75.2 8.4 %collective-permute-start.45 = (f32[1]{0:T(128)}, f32[1]{0:T(128)}, u32[]{:S(2)}, u32[]{:S(2)}) collective-permute-start(f32[1]{0:T(128)} %convert_element_type.107), channel_id=1, source_target_pairs={{0,2},{1,3},{2,4},{3,5},{4,6},{5,7},{6,8},{7,9},{8,10},{9,11},{10,... | collective-permute-start | bytes 20 | tf_op jit(solution)/shard_map/ppermute | solution.py:17
  80.4 8.0 %collective-permute-start.47 = (f32[1]{0:T(128)}, f32[1]{0:T(128)}, u32[]{:S(2)}, u32[]{:S(2)}) collective-permute-start(f32[1]{0:T(128)} %convert_element_type.107), channel_id=1, source_target_pairs={{0,3},{1,4},{2,5},{3,6},{4,7},{5,8},{6,9},{7,10},{8,11},{9,12},{10... | collective-permute-start | bytes 20 | tf_op jit(solution)/shard_map/ppermute | solution.py:17
  83.6 8.4 %collective-permute-start.49 = (f32[1]{0:T(128)}, f32[1]{0:T(128)}, u32[]{:S(2)}, u32[]{:S(2)}) collective-permute-start(f32[1]{0:T(128)} %convert_element_type.107), channel_id=1, source_target_pairs={{0,4},{1,5},{2,6},{3,7},{4,8},{5,9},{6,10},{7,11},{8,12},{9,13},{1... | collective-permute-start | bytes 20 | tf_op jit(solution)/shard_map/ppermute | solution.py:17
  88.4 8.9 %collective-permute-start.51 = (f32[1]{0:T(128)}, f32[1]{0:T(128)}, u32[]{:S(2)}, u32[]{:S(2)}) collective-permute-start(f32[1]{0:T(128)} %convert_element_type.107), channel_id=1, source_target_pairs={{0,5},{1,6},{2,7},{3,8},{4,9},{5,10},{6,11},{7,12},{8,13},{9,14},{... | collective-permute-start | bytes 20 | tf_op jit(solution)/shard_map/ppermute | solution.py:17
  92.0 10.0 %collective-permute-start.53 = (f32[1]{0:T(128)}, f32[1]{0:T(128)}, u32[]{:S(2)}, u32[]{:S(2)}) collective-permute-start(f32[1]{0:T(128)} %convert_element_type.107), channel_id=1, source_target_pairs={{0,6},{1,7},{2,8},{3,9},{4,10},{5,11},{6,12},{7,13},{8,14},{9,15},... | collective-permute-start | bytes 20 | tf_op jit(solution)/shard_map/ppermute | solution.py:17
  97.2 12.3 %collective-permute-start.55 = (f32[1]{0:T(128)}, f32[1]{0:T(128)}, u32[]{:S(2)}, u32[]{:S(2)}) collective-permute-start(f32[1]{0:T(128)} %convert_element_type.107), channel_id=1, source_target_pairs={{0,7},{1,8},{2,9},{3,10},{4,11},{5,12},{6,13},{7,14},{8,15},{9,16}... | collective-permute-start | bytes 20 | tf_op jit(solution)/shard_map/ppermute | solution.py:17
  101.9 15.5 %collective-permute-start.29 = (f32[1]{0:T(128)}, f32[1]{0:T(128)}, u32[]{:S(2)}, u32[]{:S(2)}) collective-permute-start(f32[1]{0:T(128)} %convert_element_type.107), channel_id=1, source_target_pairs={{7,0},{8,1},{9,2},{10,3},{11,4},{12,5},{13,6},{14,7},{15,8},{16,9}... | collective-permute-start | bytes 20 | tf_op jit(solution)/shard_map/ppermute | solution.py:17
  109.6 16.3 %collective-permute-start.31 = (f32[1]{0:T(128)}, f32[1]{0:T(128)}, u32[]{:S(2)}, u32[]{:S(2)}) collective-permute-start(f32[1]{0:T(128)} %convert_element_type.107), channel_id=1, source_target_pairs={{6,0},{7,1},{8,2},{9,3},{10,4},{11,5},{12,6},{13,7},{14,8},{15,9},... | collective-permute-start | bytes 20 | tf_op jit(solution)/shard_map/ppermute | solution.py:17
  117.5 13.8 %collective-permute-start.33 = (f32[1]{0:T(128)}, f32[1]{0:T(128)}, u32[]{:S(2)}, u32[]{:S(2)}) collective-permute-start(f32[1]{0:T(128)} %convert_element_type.107), channel_id=1, source_target_pairs={{5,0},{6,1},{7,2},{8,3},{9,4},{10,5},{11,6},{12,7},{13,8},{14,9},{... | collective-permute-start | bytes 20 | tf_op jit(solution)/shard_map/ppermute | solution.py:17
  125.8 16.6 %collective-permute-start.32 = (f32[768]{0:T(1024)S(1)}, f32[768]{0:T(1024)S(1)}, u32[]{:S(2)}, u32[]{:S(2)}) collective-permute-start(f32[768]{0:T(1024)S(1)} %get-tuple-element.133), channel_id=1, source_target_pairs={{5,0},{6,1},{7,2},{8,3},{9,4},{10,5},{11,6},{12,7},{13,8},{14,9},{... | collective-permute-start | bytes 9224 | tf_op jit(solution)/shard_map/ppermute | solution.py:17
  131.2 14.0 %collective-permute-start.34 = (f32[768]{0:T(1024)S(1)}, f32[768]{0:T(1024)S(1)}, u32[]{:S(2)}, u32[]{:S(2)}) collective-permute-start(f32[768]{0:T(1024)S(1)} %get-tuple-element.133), channel_id=1, source_target_pairs={{4,0},{5,1},{6,2},{7,3},{8,4},{9,5},{10,6},{11,7},{12,8},{13,9},{1... | collective-permute-start | bytes 9224 | tf_op jit(solution)/shard_map/ppermute | solution.py:17
  133.2 14.1 %collective-permute-start.36 = (f32[768]{0:T(1024)S(1)}, f32[768]{0:T(1024)S(1)}, u32[]{:S(2)}, u32[]{:S(2)}) collective-permute-start(f32[768]{0:T(1024)S(1)} %get-tuple-element.133), channel_id=1, source_target_pairs={{3,0},{4,1},{5,2},{6,3},{7,4},{8,5},{9,6},{10,7},{11,8},{12,9},{13... | collective-permute-start | bytes 9224 | tf_op jit(solution)/shard_map/ppermute | solution.py:17
  140.4 10.4 %collective-permute-start.38 = (f32[768]{0:T(1024)S(1)}, f32[768]{0:T(1024)S(1)}, u32[]{:S(2)}, u32[]{:S(2)}) collective-permute-start(f32[768]{0:T(1024)S(1)} %get-tuple-element.133), channel_id=1, source_target_pairs={{2,0},{3,1},{4,2},{5,3},{6,4},{7,5},{8,6},{9,7},{10,8},{11,9},{12,... | collective-permute-start | bytes 9224 | tf_op jit(solution)/shard_map/ppermute | solution.py:17
  142.4 13.3 %collective-permute-start.40 = (f32[768]{0:T(1024)S(1)}, f32[768]{0:T(1024)S(1)}, u32[]{:S(2)}, u32[]{:S(2)}) collective-permute-start(f32[768]{0:T(1024)S(1)} %get-tuple-element.133), channel_id=1, source_target_pairs={{1,0},{2,1},{3,2},{4,3},{5,4},{6,5},{7,6},{8,7},{9,8},{10,9},{11,1... | collective-permute-start | bytes 9224 | tf_op jit(solution)/shard_map/ppermute | solution.py:17
  145.2 13.8 %collective-permute-start.42 = (f32[768]{0:T(1024)S(1)}, f32[768]{0:T(1024)S(1)}, u32[]{:S(2)}, u32[]{:S(2)}) collective-permute-start(f32[768]{0:T(1024)S(1)} %get-tuple-element.133), channel_id=1, source_target_pairs={{0,1},{1,2},{2,3},{3,4},{4,5},{5,6},{6,7},{7,8},{8,9},{9,10},{10,1... | collective-permute-start | bytes 9224 | tf_op jit(solution)/shard_map/ppermute | solution.py:17
  147.3 13.7 %collective-permute-start.44 = (f32[768]{0:T(1024)S(1)}, f32[768]{0:T(1024)S(1)}, u32[]{:S(2)}, u32[]{:S(2)}) collective-permute-start(f32[768]{0:T(1024)S(1)} %get-tuple-element.133), channel_id=1, source_target_pairs={{0,2},{1,3},{2,4},{3,5},{4,6},{5,7},{6,8},{7,9},{8,10},{9,11},{10,... | collective-permute-start | bytes 9224 | tf_op jit(solution)/shard_map/ppermute | solution.py:17
  150.8 12.1 %collective-permute-start.46 = (f32[768]{0:T(1024)S(1)}, f32[768]{0:T(1024)S(1)}, u32[]{:S(2)}, u32[]{:S(2)}) collective-permute-start(f32[768]{0:T(1024)S(1)} %get-tuple-element.133), channel_id=1, source_target_pairs={{0,3},{1,4},{2,5},{3,6},{4,7},{5,8},{6,9},{7,10},{8,11},{9,12},{10... | collective-permute-start | bytes 9224 | tf_op jit(solution)/shard_map/ppermute | solution.py:17
  155.7 9.5 %collective-permute-start.48 = (f32[768]{0:T(1024)S(1)}, f32[768]{0:T(1024)S(1)}, u32[]{:S(2)}, u32[]{:S(2)}) collective-permute-start(f32[768]{0:T(1024)S(1)} %get-tuple-element.133), channel_id=1, source_target_pairs={{0,4},{1,5},{2,6},{3,7},{4,8},{5,9},{6,10},{7,11},{8,12},{9,13},{1... | collective-permute-start | bytes 9224 | tf_op jit(solution)/shard_map/ppermute | solution.py:17
  159.0 9.5 %collective-permute-start.50 = (f32[768]{0:T(1024)S(1)}, f32[768]{0:T(1024)S(1)}, u32[]{:S(2)}, u32[]{:S(2)}) collective-permute-start(f32[768]{0:T(1024)S(1)} %get-tuple-element.133), channel_id=1, source_target_pairs={{0,5},{1,6},{2,7},{3,8},{4,9},{5,10},{6,11},{7,12},{8,13},{9,14},{... | collective-permute-start | bytes 9224 | tf_op jit(solution)/shard_map/ppermute | solution.py:17
  161.0 13.7 %collective-permute-start.52 = (f32[768]{0:T(1024)S(1)}, f32[768]{0:T(1024)S(1)}, u32[]{:S(2)}, u32[]{:S(2)}) collective-permute-start(f32[768]{0:T(1024)S(1)} %get-tuple-element.133), channel_id=1, source_target_pairs={{0,6},{1,7},{2,8},{3,9},{4,10},{5,11},{6,12},{7,13},{8,14},{9,15},... | collective-permute-start | bytes 9224 | tf_op jit(solution)/shard_map/ppermute | solution.py:17
  162.9 16.3 %collective-permute-start.54 = (f32[768]{0:T(1024)S(1)}, f32[768]{0:T(1024)S(1)}, u32[]{:S(2)}, u32[]{:S(2)}) collective-permute-start(f32[768]{0:T(1024)S(1)} %get-tuple-element.133), channel_id=1, source_target_pairs={{0,7},{1,8},{2,9},{3,10},{4,11},{5,12},{6,13},{7,14},{8,15},{9,16}... | collective-permute-start | bytes 9224 | tf_op jit(solution)/shard_map/ppermute | solution.py:17
  165.1 46.5 %collective-permute-start.3 = (bf16[512,768]{1,0:T(8,128)(2,1)S(1)}, bf16[512,768]{1,0:T(8,128)(2,1)}, u32[]{:S(2)}, u32[]{:S(2)}) collective-permute-start(bf16[512,768]{1,0:T(8,128)(2,1)S(1)} %get-tuple-element.134), channel_id=1, source_target_pairs={{2,0},{3,1},{4,2},{5,3},{6,4},{7,5},{8,6},{9,7},{10,8},{11,9},{12,... | collective-permute-start | bytes 2359304 | tf_op jit(solution)/shard_map/ppermute | solution.py:17
  168.5 47.3 %collective-permute-start.5 = (bf16[512,768]{1,0:T(8,128)(2,1)S(1)}, bf16[512,768]{1,0:T(8,128)(2,1)}, u32[]{:S(2)}, u32[]{:S(2)}) collective-permute-start(bf16[512,768]{1,0:T(8,128)(2,1)S(1)} %get-tuple-element.134), channel_id=1, source_target_pairs={{3,0},{4,1},{5,2},{6,3},{7,4},{8,5},{9,6},{10,7},{11,8},{12,9},{13... | collective-permute-start | bytes 2359304 | tf_op jit(solution)/shard_map/ppermute | solution.py:17
  174.6 58.4 %collective-permute-start.7 = (bf16[512,768]{1,0:T(8,128)(2,1)S(1)}, bf16[512,768]{1,0:T(8,128)(2,1)S(1)}, u32[]{:S(2)}, u32[]{:S(2)}) collective-permute-start(bf16[512,768]{1,0:T(8,128)(2,1)S(1)} %get-tuple-element.134), channel_id=1, source_target_pairs={{4,0},{5,1},{6,2},{7,3},{8,4},{9,5},{10,6},{11,7},{12,8},{13,9},{1... | collective-permute-start | bytes 2359304 | tf_op jit(solution)/shard_map/ppermute | solution.py:17
  179.2 109.7 %collective-permute-start.9 = (bf16[512,768]{1,0:T(8,128)(2,1)S(1)}, bf16[512,768]{1,0:T(8,128)(2,1)S(1)}, u32[]{:S(2)}, u32[]{:S(2)}) collective-permute-start(bf16[512,768]{1,0:T(8,128)(2,1)S(1)} %get-tuple-element.134), channel_id=1, source_target_pairs={{5,0},{6,1},{7,2},{8,3},{9,4},{10,5},{11,6},{12,7},{13,8},{14,9},{... | collective-permute-start | bytes 2359304 | tf_op jit(solution)/shard_map/ppermute | solution.py:17
  200.3 146.3 %collective-permute-start.11 = (bf16[512,768]{1,0:T(8,128)(2,1)S(1)}, bf16[512,768]{1,0:T(8,128)(2,1)}, u32[]{:S(2)}, u32[]{:S(2)}) collective-permute-start(bf16[512,768]{1,0:T(8,128)(2,1)S(1)} %get-tuple-element.134), channel_id=1, source_target_pairs={{6,0},{7,1},{8,2},{9,3},{10,4},{11,5},{12,6},{13,7},{14,8},{15,9},... | collective-permute-start | bytes 2359304 | tf_op jit(solution)/shard_map/ppermute | solution.py:17
  211.6 172.5 %collective-permute-start.13 = (bf16[512,768]{1,0:T(8,128)(2,1)S(1)}, bf16[512,768]{1,0:T(8,128)(2,1)}, u32[]{:S(2)}, u32[]{:S(2)}) collective-permute-start(bf16[512,768]{1,0:T(8,128)(2,1)S(1)} %get-tuple-element.134), channel_id=1, source_target_pairs={{7,0},{8,1},{9,2},{10,3},{11,4},{12,5},{13,6},{14,7},{15,8},{16,9}... | collective-permute-start | bytes 2359304 | tf_op jit(solution)/shard_map/ppermute | solution.py:17
  215.9 174.4 %collective-permute-start.21 = (f32[512]{0:T(512)S(1)}, f32[512]{0:T(512)S(1)}, u32[]{:S(2)}, u32[]{:S(2)}) collective-permute-start(f32[512]{0:T(512)S(1)} %get-tuple-element.94), channel_id=1, source_target_pairs={{0,1},{1,2},{2,3},{3,4},{4,5},{5,6},{6,7},{7,8},{8,9},{9,10},{10,1... | collective-permute-start | bytes 6152 | tf_op jit(solution)/shard_map/ppermute | solution.py:17
  233.0 159.4 %collective-permute-start.22 = (f32[512]{0:T(512)S(1)}, f32[512]{0:T(512)S(1)}, u32[]{:S(2)}, u32[]{:S(2)}) collective-permute-start(f32[512]{0:T(512)S(1)} %get-tuple-element.95), channel_id=1, source_target_pairs={{0,2},{1,3},{2,4},{3,5},{4,6},{5,7},{6,8},{7,9},{8,10},{9,11},{10,... | collective-permute-start | bytes 6152 | tf_op jit(solution)/shard_map/ppermute | solution.py:17
  288.9 112.0 %collective-permute-start.23 = (f32[512]{0:T(512)S(1)}, f32[512]{0:T(512)S(1)}, u32[]{:S(2)}, u32[]{:S(2)}) collective-permute-start(f32[512]{0:T(512)S(1)} %get-tuple-element.96), channel_id=1, source_target_pairs={{0,3},{1,4},{2,5},{3,6},{4,7},{5,8},{6,9},{7,10},{8,11},{9,12},{10... | collective-permute-start | bytes 6152 | tf_op jit(solution)/shard_map/ppermute | solution.py:17
  346.6 56.6 %collective-permute-start.24 = (f32[512]{0:T(512)S(1)}, f32[512]{0:T(512)S(1)}, u32[]{:S(2)}, u32[]{:S(2)}) collective-permute-start(f32[512]{0:T(512)S(1)} %get-tuple-element.97), channel_id=1, source_target_pairs={{0,4},{1,5},{2,6},{3,7},{4,8},{5,9},{6,10},{7,11},{8,12},{9,13},{1... | collective-permute-start | bytes 6152 | tf_op jit(solution)/shard_map/ppermute | solution.py:17
  384.1 25.5 %collective-permute-start.25 = (f32[512]{0:T(512)S(1)}, f32[512]{0:T(512)S(1)}, u32[]{:S(2)}, u32[]{:S(2)}) collective-permute-start(f32[512]{0:T(512)S(1)} %get-tuple-element.98), channel_id=1, source_target_pairs={{0,5},{1,6},{2,7},{3,8},{4,9},{5,10},{6,11},{7,12},{8,13},{9,14},{... | collective-permute-start | bytes 6152 | tf_op jit(solution)/shard_map/ppermute | solution.py:17
  390.2 25.9 %collective-permute-start.26 = (f32[512]{0:T(512)S(1)}, f32[512]{0:T(512)S(1)}, u32[]{:S(2)}, u32[]{:S(2)}) collective-permute-start(f32[512]{0:T(512)S(1)} %get-tuple-element.99), channel_id=1, source_target_pairs={{0,6},{1,7},{2,8},{3,9},{4,10},{5,11},{6,12},{7,13},{8,14},{9,15},... | collective-permute-start | bytes 6152 | tf_op jit(solution)/shard_map/ppermute | solution.py:17
  392.4 25.6 %collective-permute-start.27 = (f32[512]{0:T(512)S(1)}, f32[512]{0:T(512)S(1)}, u32[]{:S(2)}, u32[]{:S(2)}) collective-permute-start(f32[512]{0:T(512)S(1)} %get-tuple-element.100), channel_id=1, source_target_pairs={{0,7},{1,8},{2,9},{3,10},{4,11},{5,12},{6,13},{7,14},{8,15},{9,16}... | collective-permute-start | bytes 6152 | tf_op jit(solution)/shard_map/ppermute | solution.py:17
  400.9 19.1 %collective-permute-start.14 = (f32[512]{0:T(512)S(1)}, f32[512]{0:T(512)S(1)}, u32[]{:S(2)}, u32[]{:S(2)}) collective-permute-start(f32[512]{0:T(512)S(1)} %broadcast_add_fusion.6), channel_id=1, source_target_pairs={{0,1},{1,2},{2,3},{3,4},{4,5},{5,6},{6,7},{7,8},{8,9},{9,10},{10,1... | collective-permute-start | bytes 6152 | tf_op jit(solution)/shard_map/ppermute | solution.py:17
  403.2 83.9 %collective-permute-start.15 = (f32[512]{0:T(512)S(1)}, f32[512]{0:T(512)S(1)}, u32[]{:S(2)}, u32[]{:S(2)}) collective-permute-start(f32[512]{0:T(512)S(1)} %broadcast_add_fusion.5), channel_id=1, source_target_pairs={{0,2},{1,3},{2,4},{3,5},{4,6},{5,7},{6,8},{7,9},{8,10},{9,11},{10,... | collective-permute-start | bytes 6152 | tf_op jit(solution)/shard_map/ppermute | solution.py:17
  409.6 80.1 %collective-permute-start.16 = (f32[512]{0:T(512)S(1)}, f32[512]{0:T(512)S(1)}, u32[]{:S(2)}, u32[]{:S(2)}) collective-permute-start(f32[512]{0:T(512)S(1)} %broadcast_add_fusion.4), channel_id=1, source_target_pairs={{0,3},{1,4},{2,5},{3,6},{4,7},{5,8},{6,9},{7,10},{8,11},{9,12},{10... | collective-permute-start | bytes 6152 | tf_op jit(solution)/shard_map/ppermute | solution.py:17
  416.1 73.6 %collective-permute-start.17 = (f32[512]{0:T(512)S(1)}, f32[512]{0:T(512)S(1)}, u32[]{:S(2)}, u32[]{:S(2)}) collective-permute-start(f32[512]{0:T(512)S(1)} %broadcast_add_fusion.3), channel_id=1, source_target_pairs={{0,4},{1,5},{2,6},{3,7},{4,8},{5,9},{6,10},{7,11},{8,12},{9,13},{1... | collective-permute-start | bytes 6152 | tf_op jit(solution)/shard_map/ppermute | solution.py:17
  418.1 71.7 %collective-permute-start.18 = (f32[512]{0:T(512)S(1)}, f32[512]{0:T(512)S(1)}, u32[]{:S(2)}, u32[]{:S(2)}) collective-permute-start(f32[512]{0:T(512)S(1)} %broadcast_add_fusion.2), channel_id=1, source_target_pairs={{0,5},{1,6},{2,7},{3,8},{4,9},{5,10},{6,11},{7,12},{8,13},{9,14},{... | collective-permute-start | bytes 6152 | tf_op jit(solution)/shard_map/ppermute | solution.py:17
  420.0 69.7 %collective-permute-start.19 = (f32[512]{0:T(512)S(1)}, f32[512]{0:T(512)S(1)}, u32[]{:S(2)}, u32[]{:S(2)}) collective-permute-start(f32[512]{0:T(512)S(1)} %broadcast_add_fusion.1), channel_id=1, source_target_pairs={{0,6},{1,7},{2,8},{3,9},{4,10},{5,11},{6,12},{7,13},{8,14},{9,15},... | collective-permute-start | bytes 6152 | tf_op jit(solution)/shard_map/ppermute | solution.py:17
  487.2 9.7 %collective-permute-start.20 = (f32[512]{0:T(512)S(1)}, f32[512]{0:T(512)S(1)}, u32[]{:S(2)}, u32[]{:S(2)}) collective-permute-start(f32[512]{0:T(512)S(1)} %broadcast_add_fusion), channel_id=1, source_target_pairs={{0,7},{1,8},{2,9},{3,10},{4,11},{5,12},{6,13},{7,14},{8,15},{9,16}... | collective-permute-start | bytes 6152 | tf_op jit(solution)/shard_map/ppermute | solution.py:17
where the time goes:
time: 500 us; the launch traced here: 497 us
  starting transfers between devices  331 us (66%)
  waiting for transfers between devices  137 us (27%)
  between operations  15.9 us (3%)
  matrix products  8.99 us (2%)
    ppermute x56, starting transfers between devices, passed_along(): lax.ppermute(value, axis, [(source, source + steps) for source in range(l...  331 us
    ppermute x56, waiting for transfers between devices, passed_along(): lax.ppermute(value, axis, [(source, source + steps) for source in range(l...  137 us
  transfers between devices with their start and end apart: 56, of which 7 were waited for; matrix products, arithmetic and copies ran while one was open for 2% of the time, Pallas kernels for 0%

commit v1 on v0

v1 whole, which is shorter than its diff:
```python
import functools
import math

import jax
import jax.numpy as jnp
from jax import lax
from jax.experimental import pallas as pl
from jax.experimental.pallas import tpu as pltpu
from jax.sharding import PartitionSpec as P

TAU = 0.05
LOW = -2.0
TO_EXP2 = math.log2(math.e) / TAU
AXES = ("shard", "grp")
VMEM = pl.BlockSpec(memory_space=pltpu.VMEM)
F32 = jnp.float32
BF16 = jnp.bfloat16


def shape(*dims, dtype=F32):
    return jax.ShapeDtypeStruct(dims, dtype)


def call(kernel, outs, *args, flops=0, limit=24):
    single = not isinstance(outs, (list, tuple))
    size = sum(a.size * a.dtype.itemsize for a in args)
    return pl.pallas_call(
        kernel,
        out_shape=outs,
        in_specs=[VMEM] * len(args),
        out_specs=VMEM if single else [VMEM] * len(outs),
        compiler_params=pltpu.CompilerParams(vmem_limit_bytes=limit << 20),
        cost_estimate=pl.CostEstimate(flops=flops, bytes_accessed=size, transcendentals=0),
    )(*args)


def blocks_moved(value, steps, core=None, closed=False):
    count = lax.axis_size(AXES)
    sources = [i for i in range(count) if core in (None, i % 2) and (closed or 0 <= i + steps < count)]
    pairs = [(i, (i + steps) % count) for i in sources]
    return lax.ppermute(value, AXES, pairs)


def cores_swapped(value):
    return lax.ppermute(value, AXES, [(i, i ^ 1) for i in range(lax.axis_size(AXES))])


def after(value, *others):
    return lax.optimization_barrier((value, *others))[0]


def unit_kernel(emb_ref, tag_ref, unit_ref, info_ref):
    rows, width = emb_ref.shape
    floats = emb_ref[...].astype(F32)
    mean = jnp.sum(floats * floats, axis=1, keepdims=True) / width
    unit = (floats * (lax.rsqrt(mean + 1e-06) / math.sqrt(width))).astype(BF16)
    unit_ref[...] = unit
    ones = jnp.ones((8, rows), BF16)
    total = jnp.dot(ones, unit, preferred_element_type=F32)
    info_ref[0:1, :] = total[0:1, :]
    info_ref[1:2, :] = jnp.broadcast_to(tag_ref[...], (1, width))


def window_kernel(mine_ref, left_ref, here_ref, right_ref, suffix_ref, prefix_ref, window_ref):
    refs = (left_ref, here_ref, right_ref)
    sums = [ref[2 * core : 2 * core + 1, :] for ref in refs for core in range(2)]
    tags = [ref[2 * core + 1 : 2 * core + 2, :] for ref in refs for core in range(2)]

    def sum_of(tag):
        return functools.reduce(
            jnp.add, [jnp.where(other == tag, value, 0.0) for value, other in zip(sums, tags)]
        )

    suffix_ref[0:1, :] = sum_of(tags[-1])
    suffix_ref[1:2, :] = tags[-1]
    prefix_ref[0:1, :] = sum_of(tags[0])
    prefix_ref[1:2, :] = tags[0]
    prefix_ref[2:3, :] = tags[1]
    prefix_ref[3:4, :] = tags[1]
    window_ref[...] = sum_of(mine_ref[1:2, :])


def centre_kernel(mine_ref, here_ref, left_ref, window_ref, suffix_ref, prefix_ref, unit_ref, core_ref, cos_ref, flag_ref):
    rows, width = unit_ref.shape
    tag = mine_ref[1:2, :]
    total = window_ref[...]
    total += jnp.where(suffix_ref[1:2, :] == tag, suffix_ref[0:1, :], 0.0)
    total += jnp.where(prefix_ref[1:2, :] == tag, prefix_ref[0:1, :], 0.0)
    mean = jnp.sum(total * total, axis=1, keepdims=True) / width
    centre = total * (lax.rsqrt(mean + 1e-06) / math.sqrt(width))
    high = centre.astype(BF16)
    rest = centre - high.astype(F32)
    middle = rest.astype(BF16)
    low = (rest - middle.astype(F32)).astype(BF16)
    cosines = jnp.zeros((8, rows), F32)
    for part in (low, middle, high):
        cosines += lax.dot_general(
            jnp.broadcast_to(part, (8, width)), unit_ref[...], (((1,), (1,)), ((), ())), preferred_element_type=F32
        )
    cos_ref[...] = cosines[0:1, :]

    lead = slice(0, rows)
    core = core_ref[0:1, lead] > 0.5
    tag = tag[:, lead]
    pair = lambda ref, which: ref[2 * which + 1 : 2 * which + 2, lead]
    other = jnp.where(core, pair(here_ref, 0), pair(here_ref, 1))
    near = jnp.where(core, pair(left_ref, 1), pair(left_ref, 0))
    near_x = jnp.where(core, pair(left_ref, 0), pair(left_ref, 1))
    far = jnp.where(core, prefix_ref[2:3, lead], prefix_ref[1:2, lead])
    back = suffix_ref[1:2, lead]
    one = lambda same: jnp.where(same, 1.0, 0.0)
    flags = (
        one(near == tag),
        one(near == other),
        one(far == tag),
        one(far == other),
        one(far == near),
        one(far == near_x),
        jnp.where(core, one(tag == other), one(far == back)),
        one(core),
    )
    for at, flag in enumerate(flags):
        flag_ref[at : at + 1, :] = flag


def tile(left, right):
    return lax.dot_general(left, right, (((1,), (1,)), ((), ())), preferred_element_type=F32)


def lane_groups(value, combine):
    return functools.reduce(combine, [value[:, at : at + 128] for at in range(0, value.shape[1], 128)])


def rows_done(value, combine):
    return combine(value.T, axis=0, keepdims=True)


class Columns:
    def __init__(self, rows):
        self.top = jnp.full((1, rows), LOW, F32)
        self.mass = jnp.zeros((1, rows), F32)

    def add(self, top, mass, flag=None):
        if flag is not None:
            top = jnp.where(flag, top, LOW)
            mass = jnp.where(flag, mass, 0.0)
        self.top = jnp.maximum(self.top, top)
        self.mass = self.mass + mass

    def merge(self, ref, at):
        self.add(ref[at : at + 1, :], ref[at + 1 : at + 2, :])

    def store(self, ref, at):
        ref[at : at + 1, :] = self.top
        ref[at + 1 : at + 2, :] = self.mass


def strip(rows_value, others, flags, outs, out_rows):
    row_top = row_mass = None
    for other, flag, out in zip(others, flags, outs):
        sims = tile(rows_value, other)
        weights = jnp.exp2(sims * TO_EXP2)
        out.add(jnp.max(sims, axis=0, keepdims=True), jnp.sum(weights, axis=0, keepdims=True), flag)
        top = jnp.where(flag[:, :128], lane_groups(sims, jnp.maximum), LOW)
        mass = jnp.where(flag[:, :128], lane_groups(weights, jnp.add), 0.0)
        row_top = top if row_top is None else jnp.maximum(row_top, top)
        row_mass = mass if row_mass is None else row_mass + mass
    out_rows.append((rows_done(row_top, jnp.max), rows_done(row_mass, jnp.sum)))


STRIP = 256


def near_kernel(unit_ref, other_ref, near_ref, flag_ref, out_ref):
    rows = unit_ref.shape[0]
    flags = flag_ref[...] > 0.5
    unit, other = unit_ref[...], other_ref[...]
    mine, across, near = Columns(rows), Columns(rows), []
    for at in range(0, rows, STRIP):
        sims = tile(unit_ref[at : at + STRIP, :], unit)
        row = lax.broadcasted_iota(jnp.int32, sims.shape, 0) + at
        same = row == lax.broadcasted_iota(jnp.int32, sims.shape, 1)
        weights = jnp.where(same, 0.0, jnp.exp2(sims * TO_EXP2))
        sims = jnp.where(same, LOW, sims)
        mine.add(jnp.max(sims, axis=0, keepdims=True), jnp.sum(weights, axis=0, keepdims=True))
        strip(near_ref[at : at + STRIP, :], (unit, other), (flags[0:1], flags[1:2]), (mine, across), near)
    mine.store(out_ref, 0)
    across.store(out_ref, 2)
    for at, (top, mass) in enumerate(near):
        out_ref[4:5, at * STRIP : (at + 1) * STRIP] = top
        out_ref[5:6, at * STRIP : (at + 1) * STRIP] = mass
    out_ref[6:8, :] = jnp.zeros((2, rows), F32)


def far_kernel(far_ref, unit_ref, other_ref, near_ref, near_x_ref, flag_ref, out_ref):
    rows = unit_ref.shape[0]
    flags = flag_ref[...] > 0.5
    columns = [Columns(rows) for _ in range(4)]
    far = []
    blocks = (unit_ref[...], other_ref[...], near_ref[...], near_x_ref[...])
    strip(far_ref[...], blocks, [flags[at : at + 1] for at in range(2, 6)], columns, far)
    for at, column in enumerate(columns):
        column.store(out_ref, 2 * at)
    count = far_ref.shape[0]
    out_ref[8:9, :count] = far[0][0]
    out_ref[9:10, :count] = far[0][1]
    out_ref[8:10, count:] = jnp.zeros((2, rows - count), F32)
    out_ref[10:16, :] = jnp.zeros((6, rows), F32)


def last_kernel(
    far_a_ref, far_b_ref, unit_ref, other_ref, near_ref, near_x_ref, back_ref, flag_ref, stats_near_ref, stats_far_ref,
    mine_ref, swap_ref, near_out_ref, far_out_ref, back_out_ref,
):
    rows = unit_ref.shape[0]
    flags = flag_ref[...] > 0.5
    mine, across, near, near_x = columns = [Columns(rows) for _ in range(4)]
    far = [(stats_far_ref[8:9, :STRIP], stats_far_ref[9:10, :STRIP])]
    blocks = (unit_ref[...], other_ref[...], near_ref[...], near_x_ref[...])
    strip(far_b_ref[...], blocks, [flags[at : at + 1] for at in range(2, 6)], columns, far)
    second = jnp.max(flag_ref[7:8, 0:1]) > 0.5
    flag = flags[6:7]
    last, extra = Columns(rows), []
    rows_a = jnp.where(second, unit_ref[:STRIP, :], far_a_ref[...])
    rows_b = jnp.where(second, unit_ref[STRIP:, :], far_b_ref[...])
    block = jnp.where(second, other_ref[...], back_ref[...])
    for value in (rows_a, rows_b):
        strip(value, (block,), (flag,), (last,), extra)
    none = Columns(rows)
    whole = lambda parts: [jnp.concatenate([part[which] for part in parts], axis=1) for which in range(2)]
    extra, far = whole(extra), whole(far)
    core = flags[7:8]
    mine.add(extra[0], extra[1], core)
    across.add(last.top, last.mass, core)
    far_top = jnp.maximum(far[0], jnp.where(core, LOW, extra[0]))
    far_mass = far[1] + jnp.where(core, 0.0, extra[1])
    none.add(last.top, last.mass, jnp.logical_not(core))
    mine.merge(stats_near_ref, 0)
    mine.merge(stats_far_ref, 0)
    across.merge(stats_near_ref, 2)
    across.merge(stats_far_ref, 2)
    near.merge(stats_near_ref, 4)
    near.merge(stats_far_ref, 4)
    near_x.merge(stats_far_ref, 6)
    mine.store(mine_ref, 0)
    across.store(swap_ref, 0)
    near_x.store(swap_ref, 2)
    near.store(near_out_ref, 0)
    far_out_ref[0:1, :] = far_top
    far_out_ref[1:2, :] = far_mass
    none.store(back_out_ref, 0)


def merged(columns, ref, at):
    mass = ref[at + 1 : at + 2, :]
    columns.add(ref[at : at + 1, :], mass, mass > 0.0)


def near_sum_kernel(near_ref, swap_ref, out_ref):
    near = Columns(near_ref.shape[1])
    near.merge(near_ref, 0)
    near.merge(swap_ref, 2)
    near.store(out_ref, 0)


def final_kernel(mine_ref, swap_ref, far_ref, back_ref, near_ref, top_ref, log_ref):
    mine = Columns(mine_ref.shape[1])
    mine.merge(mine_ref, 0)
    for ref in (swap_ref, far_ref, back_ref, near_ref):
        merged(mine, ref, 0)
    top_ref[...] = mine.top
    log_ref[...] = jnp.log(mine.mass)


def per_device(embeddings, cluster_ids):
    rows, width = embeddings.shape
    tile_flops = 2 * rows * rows * width
    core = lax.axis_index("grp") % 2
    tag = (cluster_ids + 1).astype(F32).reshape(1, 1)
    unit, info = call(unit_kernel, [shape(rows, width, dtype=BF16), shape(2, width)], embeddings, tag)

    near = blocks_moved(unit, 2)
    far_a = blocks_moved(unit[:STRIP], -4)
    info_x = cores_swapped(info)
    other = cores_swapped(unit)
    pair = jnp.where(core == 0, jnp.concatenate([info, info_x]), jnp.concatenate([info_x, info]))
    pair_left = blocks_moved(pair, 2, closed=True)
    pair_right = blocks_moved(pair, -2, closed=True)
    suffix, prefix, window = call(
        window_kernel, [shape(2, width), shape(4, width), shape(1, width)], info, pair_left, pair, pair_right
    )
    left_suffix = blocks_moved(suffix, 6, closed=True)
    right_prefix = blocks_moved(prefix, -6, closed=True)
    far_b = blocks_moved(after(unit[STRIP:], near), -4)
    near_x = cores_swapped(near)
    back = blocks_moved(after(unit, near), 3, core=1)
    cores = jnp.full((1, rows), core, F32)
    cosines, flags = call(
        centre_kernel,
        [shape(1, rows), shape(8, rows)],
        info, pair, pair_left, window, left_suffix, right_prefix, unit, cores,
    )
    stats_near = call(near_kernel, shape(8, rows), unit, other, near, flags, flops=3 * tile_flops)
    stats_far = call(far_kernel, shape(16, rows), far_a, unit, other, near, near_x, flags, flops=2 * tile_flops)
    mine, swap, near_out, far_out, back_out = call(
        last_kernel,
        [shape(2, rows), shape(4, rows), shape(2, rows), shape(2, rows), shape(2, rows)],
        far_a, far_b, unit, other, near, near_x, back, flags, stats_near, stats_far,
        flops=3 * tile_flops,
    )
    swap_in = cores_swapped(swap)
    far_in = blocks_moved(far_out, 4)
    back_in = blocks_moved(back_out, -3, core=0)
    near_in = blocks_moved(call(near_sum_kernel, shape(2, rows), near_out, swap_in), -2)
    top, log_mass = call(final_kernel, [shape(1, rows), shape(1, rows)], mine, swap_in, far_in, back_in, near_in)
    return top.reshape(rows), log_mass.reshape(rows), cosines.reshape(rows)


def solution(mesh):
    in_specs = (P(AXES, None), P(AXES))
    out_specs = (P(AXES), P(AXES), P(AXES))
    return jax.shard_map(per_device, mesh=mesh, in_specs=in_specs, out_specs=out_specs, check_vma=False)
```

time: 500 us -> 141 us (0.28)
  the two profiles are of different devices: /device:TPU:82 before, /device:TPU:24 now
where the time goes in v1:
time: 141 us; the launch traced here: 140 us
  waiting for transfers between devices  63.2 us (45%)
  starting transfers between devices  59.6 us (42%)
  Pallas kernels  8.2 us (6%)
  local copies, waits for them, and re-layouts  6.68 us (5%)
  between operations  1.53 us (1%)
    ppermute x11, waiting for transfers between devices, blocks_moved(): return lax.ppermute(value, AXES, pairs)  63.2 us
    ppermute x11, starting transfers between devices, blocks_moved(): return lax.ppermute(value, AXES, pairs)  50.9 us
    ppermute x4, starting transfers between devices, cores_swapped(): lax.ppermute(value, AXES, [(i, i ^ 1) for i in range(lax.axis_size(AXES))])  8.65 us
    pallas_call x8, Pallas kernels, call(): pl.pallas_call(kernel, out_shape=outs, in_specs=[VMEM] * len(args), out_s...  8.2 us
    unnamed x20, local copies, waits for them, and re-layouts  5.68 us
  transfers between devices with their start and end apart: 15, of which 7 were waited for; matrix products, arithmetic and copies ran while one was open for 1% of the time, Pallas kernels for 3%

profile of v1, /device:TPU:24, one launch (start us, length us, event | category | flops | bytes accessed | tf_op | source)
XLA Modules:
  0.0 139.9 jit_solution(10778252879493834324)
XLA Ops:
  1.3 0.0 copy-start
  1.3 1.1 copy-done
  2.4 0.5 shard_map.49
  2.9 0.0 copy-start.1
  2.9 4.3 %collective-permute-start.1 = (bf16[512,768]{1,0:T(8,128)(2,1)S(1)}, bf16[512,768]{1,0:T(8,128)(2,1)S(1)}, u32[]{:S(2)}, u32[]{:S(2)}) collective-permute-start(bf16[512,768]{1,0:T(8,128)(2,1)S(1)} %get-tuple-element.21.unit_ref), channel_id=1, source_target_pairs={{0,2},{1,3},{2,4},{3,5},{4,6},{5,7},{6,8},{7,9},{8,10},{9,11},{10,... | collective-permute-start | bytes 2359304 | tf_op jit(solution)/shard_map/ppermute | solution.py:41
  7.2 1.9 %collective-permute-start.3 = (bf16[512,768]{1,0:T(8,128)(2,1)S(1)}, bf16[512,768]{1,0:T(8,128)(2,1)S(1)}, u32[]{:S(2)}, u32[]{:S(2)}) collective-permute-start(bf16[512,768]{1,0:T(8,128)(2,1)S(1)} %get-tuple-element.21.unit_ref), channel_id=1, source_target_pairs={{0,1},{1,0},{2,3},{3,2},{4,5},{5,4},{6,7},{7,6},{8,9},{9,8},{10,11... | collective-permute-start | bytes 2359304 | tf_op jit(solution)/shard_map/ppermute | solution.py:45
  9.1 24.3 %collective-permute-done.1.near_ref = bf16[512,768]{1,0:T(8,128)(2,1)S(1)} collective-permute-done((bf16[512,768]{1,0:T(8,128)(2,1)S(1)}, bf16[512,768]{1,0:T(8,128)(2,1)S(1)}, u32[]{:S(2)}, u32[]{:S(2)}) %collective-permute-start.1) | collective-permute-done | bytes 786464 | tf_op jit(solution)/shard_map/ppermute | solution.py:41
  33.4 1.9 %collective-permute-start.4 = (bf16[512,768]{1,0:T(8,128)(2,1)S(1)}, bf16[512,768]{1,0:T(8,128)(2,1)S(1)}, u32[]{:S(2)}, u32[]{:S(2)}) collective-permute-start(bf16[512,768]{1,0:T(8,128)(2,1)S(1)} %collective-permute-done.1.near_ref), channel_id=1, source_target_pairs={{0,1},{1,0},{2,3},{3,2},{4,5},{5,4},{6,7},{7,6},{8,9},{9,8},{10,11... | collective-permute-start | bytes 2359304 | tf_op jit(solution)/shard_map/ppermute | solution.py:45
  35.4 2.4 %collective-permute-start.6 = (f32[2,768]{1,0:T(2,128)S(1)}, f32[2,768]{1,0:T(2,128)}, u32[]{:S(2)}, u32[]{:S(2)}) collective-permute-start(f32[2,768]{1,0:T(2,128)S(1)} %get-tuple-element.22.mine_ref), channel_id=1, source_target_pairs={{0,1},{1,0},{2,3},{3,2},{4,5},{5,4},{6,7},{7,6},{8,9},{9,8},{10,11... | collective-permute-start | bytes 18440 | tf_op jit(solution)/shard_map/ppermute | solution.py:45
  37.8 1.3 collective-permute-start.5
  39.1 1.0 fusion
  40.1 0.0 copy-done.1
  40.1 3.6 %collective-permute-start = (bf16[256,768]{1,0:T(8,128)(2,1)}, bf16[256,768]{1,0:T(8,128)(2,1)S(1)}, u32[]{:S(2)}, u32[]{:S(2)}) collective-permute-start(bf16[256,768]{1,0:T(8,128)(2,1)} %get-tuple-element.36), channel_id=1, source_target_pairs={{4,0},{5,1},{6,2},{7,3},{8,4},{9,5},{10,6},{11,7},{12,8},{13,9},{1... | collective-permute-start | bytes 1179656 | tf_op jit(solution)/shard_map/ppermute | solution.py:41
  43.7 0.0 copy-start.2
  43.7 0.0 collective-permute-done.6
  43.7 0.8 maximum_select_fusion.here_ref
  44.5 2.5 %collective-permute-start.8 = (f32[4,768]{1,0:T(4,128)S(1)}, f32[4,768]{1,0:T(4,128)S(1)}, u32[]{:S(2)}, u32[]{:S(2)}) collective-permute-start(f32[4,768]{1,0:T(4,128)S(1)} %maximum_select_fusion.here_ref), channel_id=1, source_target_pairs={{0,510},{1,511},{2,0},{3,1},{4,2},{5,3},{6,4},{7,5},{8,6},{9,7},{1... | collective-permute-start | bytes 36872 | tf_op jit(solution)/shard_map/ppermute | solution.py:41
  47.0 6.2 %collective-permute-done.8.right_ref = f32[4,768]{1,0:T(4,128)S(1)} collective-permute-done((f32[4,768]{1,0:T(4,128)S(1)}, f32[4,768]{1,0:T(4,128)S(1)}, u32[]{:S(2)}, u32[]{:S(2)}) %collective-permute-start.8) | collective-permute-done | bytes 12320 | tf_op jit(solution)/shard_map/ppermute | solution.py:41
  53.2 15.5 %collective-permute-start.7 = (f32[4,768]{1,0:T(4,128)S(1)}, f32[4,768]{1,0:T(4,128)S(1)}, u32[]{:S(2)}, u32[]{:S(2)}) collective-permute-start(f32[4,768]{1,0:T(4,128)S(1)} %maximum_select_fusion.here_ref), channel_id=1, source_target_pairs={{0,2},{1,3},{2,4},{3,5},{4,6},{5,7},{6,8},{7,9},{8,10},{9,11},{10,... | collective-permute-start | bytes 36872 | tf_op jit(solution)/shard_map/ppermute | solution.py:41
  68.7 1.4 collective-permute-done.7.left_ref
  70.0 0.0 copy-done.2
  70.0 0.0 copy-start.4
  70.1 0.6 copy-done.4
  70.6 2.6 %collective-permute-start.9 = (f32[2,768]{1,0:T(2,128)S(1)}, f32[2,768]{1,0:T(2,128)S(1)}, u32[]{:S(2)}, u32[]{:S(2)}) collective-permute-start(f32[2,768]{1,0:T(2,128)S(1)} %get-tuple-element.24), channel_id=1, source_target_pairs={{0,6},{1,7},{2,8},{3,9},{4,10},{5,11},{6,12},{7,13},{8,14},{9,15},... | collective-permute-start | bytes 18440 | tf_op jit(solution)/shard_map/ppermute | solution.py:41
  73.3 8.9 %collective-permute-done.9.suffix_ref = f32[2,768]{1,0:T(2,128)S(1)} collective-permute-done((f32[2,768]{1,0:T(2,128)S(1)}, f32[2,768]{1,0:T(2,128)S(1)}, u32[]{:S(2)}, u32[]{:S(2)}) %collective-permute-start.9) | collective-permute-done | bytes 6176 | tf_op jit(solution)/shard_map/ppermute | solution.py:41
  82.2 0.0 copy-start.8
  82.2 0.6 copy-done.8
  82.7 1.9 %collective-permute-start.10 = (f32[4,768]{1,0:T(4,128)S(1)}, f32[4,768]{1,0:T(4,128)S(1)}, u32[]{:S(2)}, u32[]{:S(2)}) collective-permute-start(f32[4,768]{1,0:T(4,128)S(1)} %get-tuple-element.25), channel_id=1, source_target_pairs={{0,506},{1,507},{2,508},{3,509},{4,510},{5,511},{6,0},{7,1},{8,2},... | collective-permute-start | bytes 36872 | tf_op jit(solution)/shard_map/ppermute | solution.py:41
  84.7 5.5 %collective-permute-done.10.prefix_ref = f32[4,768]{1,0:T(4,128)S(1)} collective-permute-done((f32[4,768]{1,0:T(4,128)S(1)}, f32[4,768]{1,0:T(4,128)S(1)}, u32[]{:S(2)}, u32[]{:S(2)}) %collective-permute-start.10) | collective-permute-done | bytes 12320 | tf_op jit(solution)/shard_map/ppermute | solution.py:41
  90.2 0.0 copy-start.6
  90.2 0.6 copy-done.6
  90.8 7.0 %collective-permute-start.2 = (bf16[256,768]{1,0:T(8,128)(2,1)}, bf16[256,768]{1,0:T(8,128)(2,1)}, u32[]{:S(2)}, u32[]{:S(2)}) collective-permute-start(bf16[256,768]{1,0:T(8,128)(2,1)} %get-tuple-element.20), channel_id=1, source_target_pairs={{4,0},{5,1},{6,2},{7,3},{8,4},{9,5},{10,6},{11,7},{12,8},{13,9},{1... | collective-permute-start | bytes 1179656 | tf_op jit(solution)/shard_map/ppermute | solution.py:41
  97.8 0.0 copy-start.3
  97.8 0.7 copy-done.3
  98.5 0.0 copy-start.5
  98.5 0.7 copy-done.5
  99.2 0.0 copy-start.7
  99.2 0.7 copy-done.7
  99.9 0.0 copy-start.9
  99.9 0.7 copy-done.9
  100.6 1.3 shard_map.51
  102.0 0.0 collective-permute-done.3.other_ref
  102.0 1.6 %shard_map.52.stats_near_ref = f32[8,512]{1,0:T(8,128)S(1)} custom-call(bf16[512,768]{1,0:T(8,128)(2,1)S(1)} %get-tuple-element.21.unit_ref, bf16[512,768]{1,0:T(8,128)(2,1)S(1)} %collective-permute-done.3.other_ref, bf16[512,768]{1,0:T(8,128)(2,1)S(1)} %collective-permute-done.1.near_ref, f32[8,512]{1,0:T(8,128)S(1)} %get-tuple-element.26.flag_ref), custom_call_target="tpu_custom_call" | custom-call | flops 1207959552 | bytes 2375680 | tf_op jit(solution)/shard_map/pallas_call | solution.py:27
  103.6 0.0 collective-permute-done.far_ref.far_a_ref
  103.6 0.0 collective-permute-done.4.near_x_ref
  103.6 1.2 shard_map.53.stats_far_ref
  104.8 13.3 %collective-permute-done.2.far_b_ref = bf16[256,768]{1,0:T(8,128)(2,1)} collective-permute-done((bf16[256,768]{1,0:T(8,128)(2,1)}, bf16[256,768]{1,0:T(8,128)(2,1)}, u32[]{:S(2)}, u32[]{:S(2)}) %collective-permute-start.2) | collective-permute-done | bytes 393248 | tf_op jit(solution)/shard_map/ppermute | solution.py:41
  118.1 0.0 collective-permute-done.5.back_ref
  118.1 3.0 %shard_map.54 = (f32[2,512]{1,0:T(2,128)S(1)}, f32[4,512]{1,0:T(4,128)S(1)}, f32[2,512]{1,0:T(2,128)S(1)}, f32[2,512]{1,0:T(2,128)S(1)}, f32[2,512]{1,0:T(2,128)S(1)}) custom-call(bf16[256,768]{1,0:T(8,128)(2,1)S(1)} %collective-permute-done.far_ref.far_a_ref, bf16[256,768]{1,0:T(8,128)(2,1)} %collective-permute-done.2.far_b_ref, ...), custom_call_target="tpu_custom_call" | custom-call | flops 1207959552 | bytes 4784128 | tf_op jit(solution)/shard_map/pallas_call | solution.py:27
  121.1 2.4 %collective-permute-start.11 = (f32[4,512]{1,0:T(4,128)S(1)}, f32[4,512]{1,0:T(4,128)S(1)}, u32[]{:S(2)}, u32[]{:S(2)}) collective-permute-start(f32[4,512]{1,0:T(4,128)S(1)} %get-tuple-element.28), channel_id=1, source_target_pairs={{0,1},{1,0},{2,3},{3,2},{4,5},{5,4},{6,7},{7,6},{8,9},{9,8},{10,11... | collective-permute-start | bytes 24584 | tf_op jit(solution)/shard_map/ppermute | solution.py:45
  123.5 1.9 %collective-permute-start.12 = (f32[2,512]{1,0:T(2,128)S(1)}, f32[2,512]{1,0:T(2,128)S(1)}, u32[]{:S(2)}, u32[]{:S(2)}) collective-permute-start(f32[2,512]{1,0:T(2,128)S(1)} %get-tuple-element.29), channel_id=1, source_target_pairs={{0,4},{1,5},{2,6},{3,7},{4,8},{5,9},{6,10},{7,11},{8,12},{9,13},{1... | collective-permute-start | bytes 12296 | tf_op jit(solution)/shard_map/ppermute | solution.py:41
  125.4 8.4 %collective-permute-start.13 = (f32[2,512]{1,0:T(2,128)S(1)}, f32[2,512]{1,0:T(2,128)S(1)}, u32[]{:S(2)}, u32[]{:S(2)}) collective-permute-start(f32[2,512]{1,0:T(2,128)S(1)} %get-tuple-element.30), channel_id=1, source_target_pairs={{4,1},{6,3},{8,5},{10,7},{12,9},{14,11},{16,13},{18,15},{20,17},{2... | collective-permute-start | bytes 12296 | tf_op jit(solution)/shard_map/ppermute | solution.py:41
  133.8 0.0 collective-permute-done.11.swap_ref
  133.8 1.9 %collective-permute-start.14 = (f32[2,512]{1,0:T(2,128)S(1)}, f32[2,512]{1,0:T(2,128)S(1)}, u32[]{:S(2)}, u32[]{:S(2)}) collective-permute-start(f32[2,512]{1,0:T(2,128)S(1)} %shard_map.55), channel_id=1, source_target_pairs={{2,0},{3,1},{4,2},{5,3},{6,4},{7,5},{8,6},{9,7},{10,8},{11,9},{12,... | collective-permute-start | bytes 12296 | tf_op jit(solution)/shard_map/ppermute | solution.py:41
  135.8 0.0 collective-permute-done.12.far_ref
  135.8 0.0 collective-permute-done.13.back_ref
  135.8 3.6 %collective-permute-done.14.near_ref = f32[2,512]{1,0:T(2,128)S(1)} collective-permute-done((f32[2,512]{1,0:T(2,128)S(1)}, f32[2,512]{1,0:T(2,128)S(1)}, u32[]{:S(2)}, u32[]{:S(2)}) %collective-permute-start.14) | collective-permute-done | bytes 4128 | tf_op jit(solution)/shard_map/ppermute | solution.py:41
  139.3 0.6 shard_map.56
  (3 shorter events, 0.0 us)
Async XLA Ops:
  1.3 1.1 copy-start
  2.9 37.2 %copy-start.1 = (f32[2,768]{1,0:T(2,128)}, f32[2,768]{1,0:T(2,128)S(1)}, u32[]{:S(2)}) copy-start(f32[2,768]{1,0:T(2,128)S(1)} %get-tuple-element.22.mine_ref) | copy-start | bytes 18436
  2.9 30.6 %collective-permute-start.1 = (bf16[512,768]{1,0:T(8,128)(2,1)S(1)}, bf16[512,768]{1,0:T(8,128)(2,1)S(1)}, u32[]{:S(2)}, u32[]{:S(2)}) collective-permute-start(bf16[512,768]{1,0:T(8,128)(2,1)S(1)} %get-tuple-element.21.unit_ref), channel_id=1, source_target_pairs={{0,2},{1,3},{2,4},{3,5},{4,6},{5,7},{6,8},{7,9},{8,10},{9,11},{10,... | collective-permute-start | bytes 2359304 | tf_op jit(solution)/shard_map/ppermute | solution.py:41
  7.2 94.8 %collective-permute-start.3 = (bf16[512,768]{1,0:T(8,128)(2,1)S(1)}, bf16[512,768]{1,0:T(8,128)(2,1)S(1)}, u32[]{:S(2)}, u32[]{:S(2)}) collective-permute-start(bf16[512,768]{1,0:T(8,128)(2,1)S(1)} %get-tuple-element.21.unit_ref), channel_id=1, source_target_pairs={{0,1},{1,0},{2,3},{3,2},{4,5},{5,4},{6,7},{7,6},{8,9},{9,8},{10,11... | collective-permute-start | bytes 2359304 | tf_op jit(solution)/shard_map/ppermute | solution.py:45
  33.4 70.2 %collective-permute-start.4 = (bf16[512,768]{1,0:T(8,128)(2,1)S(1)}, bf16[512,768]{1,0:T(8,128)(2,1)S(1)}, u32[]{:S(2)}, u32[]{:S(2)}) collective-permute-start(bf16[512,768]{1,0:T(8,128)(2,1)S(1)} %collective-permute-done.1.near_ref), channel_id=1, source_target_pairs={{0,1},{1,0},{2,3},{3,2},{4,5},{5,4},{6,7},{7,6},{8,9},{9,8},{10,11... | collective-permute-start | bytes 2359304 | tf_op jit(solution)/shard_map/ppermute | solution.py:45
  35.4 8.4 %collective-permute-start.6 = (f32[2,768]{1,0:T(2,128)S(1)}, f32[2,768]{1,0:T(2,128)}, u32[]{:S(2)}, u32[]{:S(2)}) collective-permute-start(f32[2,768]{1,0:T(2,128)S(1)} %get-tuple-element.22.mine_ref), channel_id=1, source_target_pairs={{0,1},{1,0},{2,3},{3,2},{4,5},{5,4},{6,7},{7,6},{8,9},{9,8},{10,11... | collective-permute-start | bytes 18440 | tf_op jit(solution)/shard_map/ppermute | solution.py:45
  37.8 80.3 %collective-permute-start.5 = (bf16[512,768]{1,0:T(8,128)(2,1)S(1)}, bf16[512,768]{1,0:T(8,128)(2,1)}, u32[]{:S(2)}, u32[]{:S(2)}) collective-permute-start(bf16[512,768]{1,0:T(8,128)(2,1)S(1)} %get-tuple-element.21.unit_ref), channel_id=1, source_target_pairs={{1,4},{3,6},{5,8},{7,10},{9,12},{11,14},{13,16},{15,18},{17,20},{1... | collective-permute-start | bytes 2359304 | tf_op jit(solution)/shard_map/ppermute | solution.py:41
  40.1 63.5 %collective-permute-start = (bf16[256,768]{1,0:T(8,128)(2,1)}, bf16[256,768]{1,0:T(8,128)(2,1)S(1)}, u32[]{:S(2)}, u32[]{:S(2)}) collective-permute-start(bf16[256,768]{1,0:T(8,128)(2,1)} %get-tuple-element.36), channel_id=1, source_target_pairs={{4,0},{5,1},{6,2},{7,3},{8,4},{9,5},{10,6},{11,7},{12,8},{13,9},{1... | collective-permute-start | bytes 1179656 | tf_op jit(solution)/shard_map/ppermute | solution.py:41
  43.7 26.3 %copy-start.2 = (f32[2,768]{1,0:T(2,128)S(1)}, f32[2,768]{1,0:T(2,128)}, u32[]{:S(2)}) copy-start(f32[2,768]{1,0:T(2,128)} %copy-done.1) | copy-start | bytes 18436
  44.5 8.6 %collective-permute-start.8 = (f32[4,768]{1,0:T(4,128)S(1)}, f32[4,768]{1,0:T(4,128)S(1)}, u32[]{:S(2)}, u32[]{:S(2)}) collective-permute-start(f32[4,768]{1,0:T(4,128)S(1)} %maximum_select_fusion.here_ref), channel_id=1, source_target_pairs={{0,510},{1,511},{2,0},{3,1},{4,2},{5,3},{6,4},{7,5},{8,6},{9,7},{1... | collective-permute-start | bytes 36872 | tf_op jit(solution)/shard_map/ppermute | solution.py:41
  53.2 16.9 %collective-permute-start.7 = (f32[4,768]{1,0:T(4,128)S(1)}, f32[4,768]{1,0:T(4,128)S(1)}, u32[]{:S(2)}, u32[]{:S(2)}) collective-permute-start(f32[4,768]{1,0:T(4,128)S(1)} %maximum_select_fusion.here_ref), channel_id=1, source_target_pairs={{0,2},{1,3},{2,4},{3,5},{4,6},{5,7},{6,8},{7,9},{8,10},{9,11},{10,... | collective-permute-start | bytes 36872 | tf_op jit(solution)/shard_map/ppermute | solution.py:41
  70.0 0.6 copy-start.4
  70.6 11.5 %collective-permute-start.9 = (f32[2,768]{1,0:T(2,128)S(1)}, f32[2,768]{1,0:T(2,128)S(1)}, u32[]{:S(2)}, u32[]{:S(2)}) collective-permute-start(f32[2,768]{1,0:T(2,128)S(1)} %get-tuple-element.24), channel_id=1, source_target_pairs={{0,6},{1,7},{2,8},{3,9},{4,10},{5,11},{6,12},{7,13},{8,14},{9,15},... | collective-permute-start | bytes 18440 | tf_op jit(solution)/shard_map/ppermute | solution.py:41
  82.2 0.6 copy-start.8
  82.7 7.4 %collective-permute-start.10 = (f32[4,768]{1,0:T(4,128)S(1)}, f32[4,768]{1,0:T(4,128)S(1)}, u32[]{:S(2)}, u32[]{:S(2)}) collective-permute-start(f32[4,768]{1,0:T(4,128)S(1)} %get-tuple-element.25), channel_id=1, source_target_pairs={{0,506},{1,507},{2,508},{3,509},{4,510},{5,511},{6,0},{7,1},{8,2},... | collective-permute-start | bytes 36872 | tf_op jit(solution)/shard_map/ppermute | solution.py:41
  90.2 0.6 copy-start.6
  90.8 27.3 %collective-permute-start.2 = (bf16[256,768]{1,0:T(8,128)(2,1)}, bf16[256,768]{1,0:T(8,128)(2,1)}, u32[]{:S(2)}, u32[]{:S(2)}) collective-permute-start(bf16[256,768]{1,0:T(8,128)(2,1)} %get-tuple-element.20), channel_id=1, source_target_pairs={{4,0},{5,1},{6,2},{7,3},{8,4},{9,5},{10,6},{11,7},{12,8},{13,9},{1... | collective-permute-start | bytes 1179656 | tf_op jit(solution)/shard_map/ppermute | solution.py:41
  97.8 0.7 copy-start.3
  98.5 0.7 copy-start.5
  99.2 0.7 copy-start.7
  99.9 0.7 copy-start.9
  121.1 12.7 %collective-permute-start.11 = (f32[4,512]{1,0:T(4,128)S(1)}, f32[4,512]{1,0:T(4,128)S(1)}, u32[]{:S(2)}, u32[]{:S(2)}) collective-permute-start(f32[4,512]{1,0:T(4,128)S(1)} %get-tuple-element.28), channel_id=1, source_target_pairs={{0,1},{1,0},{2,3},{3,2},{4,5},{5,4},{6,7},{7,6},{8,9},{9,8},{10,11... | collective-permute-start | bytes 24584 | tf_op jit(solution)/shard_map/ppermute | solution.py:45
  123.5 12.3 %collective-permute-start.12 = (f32[2,512]{1,0:T(2,128)S(1)}, f32[2,512]{1,0:T(2,128)S(1)}, u32[]{:S(2)}, u32[]{:S(2)}) collective-permute-start(f32[2,512]{1,0:T(2,128)S(1)} %get-tuple-element.29), channel_id=1, source_target_pairs={{0,4},{1,5},{2,6},{3,7},{4,8},{5,9},{6,10},{7,11},{8,12},{9,13},{1... | collective-permute-start | bytes 12296 | tf_op jit(solution)/shard_map/ppermute | solution.py:41
  125.4 10.3 %collective-permute-start.13 = (f32[2,512]{1,0:T(2,128)S(1)}, f32[2,512]{1,0:T(2,128)S(1)}, u32[]{:S(2)}, u32[]{:S(2)}) collective-permute-start(f32[2,512]{1,0:T(2,128)S(1)} %get-tuple-element.30), channel_id=1, source_target_pairs={{4,1},{6,3},{8,5},{10,7},{12,9},{14,11},{16,13},{18,15},{20,17},{2... | collective-permute-start | bytes 12296 | tf_op jit(solution)/shard_map/ppermute | solution.py:41
  133.8 5.5 %collective-permute-start.14 = (f32[2,512]{1,0:T(2,128)S(1)}, f32[2,512]{1,0:T(2,128)S(1)}, u32[]{:S(2)}, u32[]{:S(2)}) collective-permute-start(f32[2,512]{1,0:T(2,128)S(1)} %shard_map.55), channel_id=1, source_target_pairs={{2,0},{3,1},{4,2},{5,3},{6,4},{7,5},{8,6},{9,7},{10,8},{11,9},{12,... | collective-permute-start | bytes 12296 | tf_op jit(solution)/shard_map/ppermute | solution.py:41

commit v2 on v0

v2 whole, which is shorter than its diff:
```python
import functools
import math

import jax
import jax.numpy as jnp
from jax import lax
from jax.experimental import pallas as pl
from jax.experimental.pallas import tpu as pltpu
from jax.sharding import PartitionSpec as P

TAU = 0.05
LOW = -2.0
TO_EXP2 = math.log2(math.e) / TAU
AXES = ("shard", "grp")
VMEM = pl.BlockSpec(memory_space=pltpu.VMEM)
F32 = jnp.float32
BF16 = jnp.bfloat16
LANES = 128
TAIL = 16
STRIP = 256


def shape(*dims, dtype=F32):
    return jax.ShapeDtypeStruct(dims, dtype)


def call(kernel, outs, *args, flops=0, limit=16):
    single = not isinstance(outs, (list, tuple))
    size = sum(a.size * a.dtype.itemsize for a in args)
    return pl.pallas_call(
        kernel,
        out_shape=outs,
        in_specs=[VMEM] * len(args),
        out_specs=VMEM if single else [VMEM] * len(outs),
        compiler_params=pltpu.CompilerParams(vmem_limit_bytes=limit << 20),
        cost_estimate=pl.CostEstimate(flops=flops, bytes_accessed=size, transcendentals=0),
    )(*args)


def blocks_moved(value, steps, core=None):
    count = lax.axis_size(AXES)
    pairs = [(i, i + steps) for i in range(count) if core in (None, i % 2) and 0 <= i + steps < count]
    return lax.ppermute(value, AXES, pairs)


def cores_swapped(value):
    return lax.ppermute(value, AXES, [(i, i ^ 1) for i in range(lax.axis_size(AXES))])


def after(value, *others):
    return lax.optimization_barrier((value, *others))[0]


def parts_of(value):
    high = value.astype(BF16)
    rest = value - high.astype(F32)
    middle = rest.astype(BF16)
    return high, middle, (rest - middle.astype(F32)).astype(BF16)


def unit_kernel(id_ref, emb_ref, block_ref):
    rows, width = emb_ref.shape
    total = jnp.zeros((8, width), F32)
    for at in range(0, rows, STRIP // 2):
        strip_rows = slice(at, at + STRIP // 2)
        floats = emb_ref[strip_rows, :].astype(F32)
        mean = jnp.sum(floats * floats, axis=1, keepdims=True) / width
        unit = (floats * (lax.rsqrt(mean + 1e-06) / math.sqrt(width))).astype(BF16)
        block_ref[strip_rows, :] = unit
        total += jnp.dot(jnp.ones((8, STRIP // 2), BF16), unit, preferred_element_type=F32)
    parts = [part.astype(F32) for part in parts_of(total[0:1, :])]
    tag = jnp.full((1, width), (id_ref[0] + 1).astype(F32))
    block_ref[rows:, :] = jnp.concatenate(parts + [tag, jnp.zeros((TAIL - 4, width), F32)]).astype(BF16)


def unit_block(embeddings, cluster_ids):
    rows, width = embeddings.shape
    return pl.pallas_call(
        unit_kernel,
        out_shape=shape(rows + TAIL, width, dtype=BF16),
        in_specs=[pl.BlockSpec(memory_space=pltpu.SMEM), VMEM],
        out_specs=VMEM,
        compiler_params=pltpu.CompilerParams(vmem_limit_bytes=16 << 20),
    )(cluster_ids, embeddings)


def this_core():
    return lax.rem(lax.axis_index("grp"), 2)


def rows_of(ref):
    return ref[: ref.shape[0] - TAIL, :]


def tail_of(ref):
    tail = ref[ref.shape[0] - TAIL :, :].astype(F32)
    return tail[0:1, :] + (tail[1:2, :] + tail[2:3, :]), tail[3:4, :]


def tile(left, right):
    return lax.dot_general(left, right, (((1,), (1,)), ((), ())), preferred_element_type=F32)


def lane_groups(value, combine):
    return functools.reduce(combine, [value[:, at : at + 128] for at in range(0, value.shape[1], 128)])


def rows_done(value, combine):
    return combine(value.T, axis=0, keepdims=True)


class Columns:
    def __init__(self, rows, width=0):
        self.top = jnp.full((1, rows), LOW, F32)
        self.mass = jnp.zeros((1, rows), F32)
        self.total = jnp.zeros((1, width), F32)

    def add(self, top, mass, flag=None):
        if flag is not None:
            top = jnp.where(flag, top, LOW)
            mass = jnp.where(flag, mass, 0.0)
        self.top = jnp.maximum(self.top, top)
        self.mass = self.mass + mass

    def meet(self, total, flag=None):
        self.total = self.total + (total if flag is None else jnp.where(flag, total, 0.0))

    def load(self, ref, at):
        rows = self.top.shape[1]
        self.add(ref[at : at + 1, :rows], ref[at + 1 : at + 2, :rows])

    def store(self, ref, at):
        rows = self.top.shape[1]
        ref[at : at + 1, :rows] = self.top
        ref[at + 1 : at + 2, :rows] = self.mass
        if self.total.size:
            ref[at : at + 2, rows:] = jnp.zeros((2, ref.shape[1] - rows), F32)
            ref[at + 2 : at + 3, :] = self.total

    def receive(self, ref, at):
        rows = self.top.shape[1]
        mass = ref[at + 1 : at + 2, :rows]
        self.add(ref[at : at + 1, :rows], mass, mass > 0.0)
        self.meet(ref[at + 2 : at + 3, :])


def strip(rows_value, others, flags, outs, out_rows):
    row_top = row_mass = None
    for other, flag, out in zip(others, flags, outs):
        sims = tile(rows_value, other)
        weights = jnp.exp2(sims * TO_EXP2)
        out.add(jnp.max(sims, axis=0, keepdims=True), jnp.sum(weights, axis=0, keepdims=True), flag[:, : sims.shape[1]])
        top = jnp.where(flag[:, :LANES], lane_groups(sims, jnp.maximum), LOW)
        mass = jnp.where(flag[:, :LANES], lane_groups(weights, jnp.add), 0.0)
        row_top = top if row_top is None else jnp.maximum(row_top, top)
        row_mass = mass if row_mass is None else row_mass + mass
    out_rows.append((rows_done(row_top, jnp.max), rows_done(row_mass, jnp.sum)))


def whole(parts):
    return [jnp.concatenate([part[which] for part in parts], axis=1) for which in range(2)]


def near_kernel(unit_ref, other_ref, near_ref, out_ref):
    unit, other = rows_of(unit_ref), rows_of(other_ref)
    rows = unit.shape[0]
    (_, tag), (_, tag_other), (_, tag_near) = [tail_of(ref) for ref in (unit_ref, other_ref, near_ref)]
    mine, across, near, parts = Columns(rows), Columns(rows), Columns(rows), []
    for at in range(0, rows, STRIP):
        sims = tile(unit_ref[at : at + STRIP, :], unit)
        row = lax.broadcasted_iota(jnp.int32, sims.shape, 0) + at
        same = row == lax.broadcasted_iota(jnp.int32, sims.shape, 1)
        weights = jnp.where(same, 0.0, jnp.exp2(sims * TO_EXP2))
        sims = jnp.where(same, LOW, sims)
        mine.add(jnp.max(sims, axis=0, keepdims=True), jnp.sum(weights, axis=0, keepdims=True))
        strip(near_ref[at : at + STRIP, :], (unit, other), (tag_near == tag, tag_near == tag_other), (mine, across), parts)
    near.add(*whole(parts))
    for at, columns in ((0, mine), (2, across), (4, near)):
        columns.store(out_ref, at)
    out_ref[6:8, :] = jnp.zeros((2, rows), F32)


def far_kernel(
    far_ref, unit_ref, other_ref, near_ref, near_x_ref, back_ref, stats_ref,
    mine_ref, swap_ref, near_out_ref, far_out_ref, back_out_ref,
):
    unit, other = rows_of(unit_ref), rows_of(other_ref)
    rows, width = unit.shape
    second = this_core() == 1
    mine, across, near, near_x = columns = [Columns(rows, width) for _ in range(4)]
    theirs, beyond, last = Columns(rows, width), Columns(rows, width), Columns(rows)
    blocks = (unit, other, rows_of(near_ref), rows_of(near_x_ref))
    tails = [tail_of(ref) for ref in (unit_ref, other_ref, near_ref, near_x_ref)]
    far_tail, back_tail = tail_of(far_ref), tail_of(back_ref)
    last_block = jnp.where(second, other, rows_of(back_ref))
    last_flag = jnp.where(second, tails[0][1], far_tail[1]) == jnp.where(second, tails[1][1], back_tail[1])
    flags = [tag == far_tail[1] for _, tag in tails]
    far, extra = [], []
    for at in range(0, rows, STRIP):
        far_rows = far_ref[at : at + STRIP, :]
        strip(far_rows, blocks, flags, columns, far)
        last_rows = jnp.where(second, unit_ref[at : at + STRIP, :], far_rows)
        strip(last_rows, (last_block,), (last_flag,), (last,), extra)
    mine.meet(tails[0][0])
    for (total, tag), owner in zip(tails[:2], (mine, across)):
        near.meet(total, tag == tails[2][1])
        owner.meet(tails[2][0], tag == tails[2][1])
    for (total, _), flag, owner in zip(tails, flags, columns):
        theirs.meet(total, flag)
        owner.meet(far_tail[0], flag)
    on = jnp.logical_and(last_flag, second)
    off = jnp.logical_and(last_flag, jnp.logical_not(second))
    across.meet(tails[0][0], on)
    mine.meet(tails[1][0], on)
    beyond.meet(far_tail[0], off)
    theirs.meet(back_tail[0], off)
    extra = whole(extra)
    theirs.add(*whole(far))
    theirs.add(*extra, off[:, :rows])
    mine.add(*extra, on[:, :rows])
    across.add(last.top, last.mass, on[:, :rows])
    beyond.add(last.top, last.mass, off[:, :rows])
    mine.load(stats_ref, 0)
    across.load(stats_ref, 2)
    near.load(stats_ref, 4)
    mine.store(mine_ref, 0)
    across.store(swap_ref, 0)
    near_x.store(swap_ref, 3)
    near.store(near_out_ref, 0)
    theirs.store(far_out_ref, 0)
    beyond.store(back_out_ref, 0)


def near_sum_kernel(near_ref, swap_ref, out_ref, *, rows):
    near = Columns(rows, near_ref.shape[1])
    near.receive(near_ref, 0)
    near.receive(swap_ref, 3)
    near.store(out_ref, 0)


def final_kernel(unit_ref, mine_ref, swap_ref, far_ref, back_ref, near_ref, top_ref, log_ref, cos_ref):
    unit = rows_of(unit_ref)
    rows, width = unit.shape
    mine = Columns(rows, width)
    for ref in (mine_ref, swap_ref, far_ref, back_ref, near_ref):
        mine.receive(ref, 0)
    top_ref[...] = mine.top
    log_ref[...] = jnp.log(mine.mass)
    mean = jnp.sum(mine.total * mine.total, axis=1, keepdims=True) / width
    centre = mine.total * (lax.rsqrt(mean + 1e-06) / math.sqrt(width))
    cosines = jnp.zeros((8, rows), F32)
    for part in parts_of(centre)[::-1]:
        cosines += tile(jnp.broadcast_to(part, (8, width)), unit)
    cos_ref[...] = cosines[0:1, :]


def per_device(embeddings, cluster_ids):
    rows, width = embeddings.shape
    block = unit_block(embeddings, cluster_ids)

    near = blocks_moved(block, 2)
    far = blocks_moved(block, -4)
    other = cores_swapped(block)
    back = blocks_moved(near, 1, core=1)
    near_x = cores_swapped(near)
    stats = call(near_kernel, shape(8, rows), block, other, near)
    mine, swap, near_out, far_out, back_out = call(
        far_kernel,
        [shape(3, width), shape(6, width), shape(3, width), shape(3, width), shape(3, width)],
        far, block, other, near, near_x, back, stats,
    )
    swap_in = cores_swapped(swap)
    far_in = blocks_moved(far_out, 4)
    back_in = blocks_moved(back_out, -3, core=0)
    near_all = call(functools.partial(near_sum_kernel, rows=rows), shape(3, width), near_out, swap_in)
    near_in = blocks_moved(near_all, -2)
    outs = call(final_kernel, [shape(1, rows)] * 3, block, mine, swap_in, far_in, back_in, near_in)
    return tuple(out.reshape(rows) for out in outs)


def solution(mesh):
    in_specs = (P(AXES, None), P(AXES))
    out_specs = (P(AXES), P(AXES), P(AXES))
    return jax.shard_map(per_device, mesh=mesh, in_specs=in_specs, out_specs=out_specs, check_vma=False)
```

time: 500 us -> 80.9 us (0.16)
  the two profiles are of different devices: /device:TPU:82 before, /device:TPU:32 now
where the time goes in v2:
time: 80.9 us; the launch traced here: 80.5 us
  starting transfers between devices  42 us (52%)
  waiting for transfers between devices  29.6 us (37%)
  Pallas kernels  6.38 us (8%)
  between operations  1.41 us (2%)
  local copies, waits for them, and re-layouts  1.13 us (1%)
    ppermute x6, starting transfers between devices, blocks_moved(): return lax.ppermute(value, AXES, pairs)  36.3 us
    ppermute x6, waiting for transfers between devices, blocks_moved(): return lax.ppermute(value, AXES, pairs)  29.6 us
    pallas_call x4, Pallas kernels, call(): pl.pallas_call(kernel, out_shape=outs, in_specs=[VMEM] * len(args), out_s...  5.93 us
    ppermute x3, starting transfers between devices, cores_swapped(): lax.ppermute(value, AXES, [(i, i ^ 1) for i in range(lax.axis_size(AXES))])  5.76 us
  transfers between devices with their start and end apart: 9, of which 3 were waited for; matrix products, arithmetic and copies ran while one was open for 0% of the time, Pallas kernels for 2%

profile of v2, /device:TPU:32, one launch (start us, length us, event | category | flops | bytes accessed | tf_op | source)
XLA Modules:
  0.0 80.5 jit_solution(5272233105892857009)
XLA Ops:
  1.3 0.0 copy-start
  1.3 1.1 %copy-done = bf16[512,768]{1,0:T(8,128)(2,1)S(1)} copy-done((bf16[512,768]{1,0:T(8,128)(2,1)S(1)}, bf16[512,768]{1,0:T(8,128)(2,1)}, u32[]{:S(2)}) %copy-start) | copy-done | bytes 786456
  2.4 0.4 shard_map.49.unit_ref
  2.9 4.3 %collective-permute-start.2 = (bf16[528,768]{1,0:T(8,128)(2,1)S(1)}, bf16[528,768]{1,0:T(8,128)(2,1)S(1)}, u32[]{:S(2)}, u32[]{:S(2)}) collective-permute-start(bf16[528,768]{1,0:T(8,128)(2,1)S(1)} %shard_map.49.unit_ref), channel_id=1, source_target_pairs={{0,2},{1,3},{2,4},{3,5},{4,6},{5,7},{6,8},{7,9},{8,10},{9,11},{10,... | collective-permute-start | bytes 2433032 | tf_op jit(solution)/shard_map/ppermute | solution.py:43
  7.2 1.9 %collective-permute-start.1 = (bf16[528,768]{1,0:T(8,128)(2,1)S(1)}, bf16[528,768]{1,0:T(8,128)(2,1)S(1)}, u32[]{:S(2)}, u32[]{:S(2)}) collective-permute-start(bf16[528,768]{1,0:T(8,128)(2,1)S(1)} %shard_map.49.unit_ref), channel_id=1, source_target_pairs={{0,1},{1,0},{2,3},{3,2},{4,5},{5,4},{6,7},{7,6},{8,9},{9,8},{10,11... | collective-permute-start | bytes 2433032 | tf_op jit(solution)/shard_map/ppermute | solution.py:47
  9.1 12.1 %collective-permute-start = (bf16[528,768]{1,0:T(8,128)(2,1)S(1)}, bf16[528,768]{1,0:T(8,128)(2,1)S(1)}, u32[]{:S(2)}, u32[]{:S(2)}) collective-permute-start(bf16[528,768]{1,0:T(8,128)(2,1)S(1)} %shard_map.49.unit_ref), channel_id=1, source_target_pairs={{4,0},{5,1},{6,2},{7,3},{8,4},{9,5},{10,6},{11,7},{12,8},{13,9},{1... | collective-permute-start | bytes 2433032 | tf_op jit(solution)/shard_map/ppermute | solution.py:43
  21.2 12.7 %collective-permute-done.2.near_ref = bf16[528,768]{1,0:T(8,128)(2,1)S(1)} collective-permute-done((bf16[528,768]{1,0:T(8,128)(2,1)S(1)}, bf16[528,768]{1,0:T(8,128)(2,1)S(1)}, u32[]{:S(2)}, u32[]{:S(2)}) %collective-permute-start.2) | collective-permute-done | bytes 811040 | tf_op jit(solution)/shard_map/ppermute | solution.py:43
  34.0 1.3 %collective-permute-start.4 = (bf16[528,768]{1,0:T(8,128)(2,1)S(1)}, bf16[528,768]{1,0:T(8,128)(2,1)S(1)}, u32[]{:S(2)}, u32[]{:S(2)}) collective-permute-start(bf16[528,768]{1,0:T(8,128)(2,1)S(1)} %collective-permute-done.2.near_ref), channel_id=1, source_target_pairs={{1,2},{3,4},{5,6},{7,8},{9,10},{11,12},{13,14},{15,16},{17,18},{19... | collective-permute-start | bytes 2433032 | tf_op jit(solution)/shard_map/ppermute | solution.py:43
  35.2 1.9 %collective-permute-start.3 = (bf16[528,768]{1,0:T(8,128)(2,1)S(1)}, bf16[528,768]{1,0:T(8,128)(2,1)S(1)}, u32[]{:S(2)}, u32[]{:S(2)}) collective-permute-start(bf16[528,768]{1,0:T(8,128)(2,1)S(1)} %collective-permute-done.2.near_ref), channel_id=1, source_target_pairs={{0,1},{1,0},{2,3},{3,2},{4,5},{5,4},{6,7},{7,6},{8,9},{9,8},{10,11... | collective-permute-start | bytes 2433032 | tf_op jit(solution)/shard_map/ppermute | solution.py:47
  37.2 0.0 collective-permute-done.1.other_ref
  37.2 1.6 %shard_map.50.stats_ref = f32[8,512]{1,0:T(8,128)S(1)} custom-call(bf16[528,768]{1,0:T(8,128)(2,1)S(1)} %shard_map.49.unit_ref, bf16[528,768]{1,0:T(8,128)(2,1)S(1)} %collective-permute-done.1.other_ref, bf16[528,768]{1,0:T(8,128)(2,1)S(1)} %collective-permute-done.2.near_ref), custom_call_target="tpu_custom_call" | custom-call | bytes 2433024 | tf_op jit(solution)/shard_map/pallas_call | solution.py:30
  38.8 15.0 %collective-permute-done.far_ref = bf16[528,768]{1,0:T(8,128)(2,1)S(1)} collective-permute-done((bf16[528,768]{1,0:T(8,128)(2,1)S(1)}, bf16[528,768]{1,0:T(8,128)(2,1)S(1)}, u32[]{:S(2)}, u32[]{:S(2)}) %collective-permute-start) | collective-permute-done | bytes 811040 | tf_op jit(solution)/shard_map/ppermute | solution.py:43
  53.8 0.0 collective-permute-done.4.back_ref
  53.8 0.0 collective-permute-done.3.near_x_ref
  53.8 2.9 %shard_map.51 = (f32[3,768]{1,0:T(4,128)S(1)}, f32[6,768]{1,0:T(8,128)S(1)}, f32[3,768]{1,0:T(4,128)S(1)}, f32[3,768]{1,0:T(4,128)S(1)}, f32[3,768]{1,0:T(4,128)S(1)}) custom-call(bf16[528,768]{1,0:T(8,128)(2,1)S(1)} %collective-permute-done.far_ref, bf16[528,768]{1,0:T(8,128)(2,1)S(1)} %shard_map.49.unit_ref, ...), custom_call_target="tpu_custom_call" | custom-call | bytes 4882432 | tf_op jit(solution)/shard_map/pallas_call | solution.py:30
  56.7 1.9 %collective-permute-start.5 = (f32[6,768]{1,0:T(8,128)S(1)}, f32[6,768]{1,0:T(8,128)S(1)}, u32[]{:S(2)}, u32[]{:S(2)}) collective-permute-start(f32[6,768]{1,0:T(8,128)S(1)} %get-tuple-element.12), channel_id=1, source_target_pairs={{0,1},{1,0},{2,3},{3,2},{4,5},{5,4},{6,7},{7,6},{8,9},{9,8},{10,11... | collective-permute-start | bytes 55304 | tf_op jit(solution)/shard_map/ppermute | solution.py:47
  58.7 3.9 %collective-permute-start.6 = (f32[3,768]{1,0:T(4,128)S(1)}, f32[3,768]{1,0:T(4,128)S(1)}, u32[]{:S(2)}, u32[]{:S(2)}) collective-permute-start(f32[3,768]{1,0:T(4,128)S(1)} %get-tuple-element.13), channel_id=1, source_target_pairs={{0,4},{1,5},{2,6},{3,7},{4,8},{5,9},{6,10},{7,11},{8,12},{9,13},{1... | collective-permute-start | bytes 27656 | tf_op jit(solution)/shard_map/ppermute | solution.py:43
  62.5 11.0 %collective-permute-start.7 = (f32[3,768]{1,0:T(4,128)S(1)}, f32[3,768]{1,0:T(4,128)S(1)}, u32[]{:S(2)}, u32[]{:S(2)}) collective-permute-start(f32[3,768]{1,0:T(4,128)S(1)} %get-tuple-element.14), channel_id=1, source_target_pairs={{4,1},{6,3},{8,5},{10,7},{12,9},{14,11},{16,13},{18,15},{20,17},{2... | collective-permute-start | bytes 27656 | tf_op jit(solution)/shard_map/ppermute | solution.py:43
  73.6 0.0 collective-permute-done.5.swap_ref
  73.6 3.7 %collective-permute-start.8 = (f32[3,768]{1,0:T(4,128)S(1)}, f32[3,768]{1,0:T(4,128)S(1)}, u32[]{:S(2)}, u32[]{:S(2)}) collective-permute-start(f32[3,768]{1,0:T(4,128)S(1)} %shard_map.52), channel_id=1, source_target_pairs={{2,0},{3,1},{4,2},{5,3},{6,4},{7,5},{8,6},{9,7},{10,8},{11,9},{12,... | collective-permute-start | bytes 27656 | tf_op jit(solution)/shard_map/ppermute | solution.py:43
  77.3 0.0 collective-permute-done.6.far_ref
  77.3 0.0 collective-permute-done.7.back_ref
  77.3 1.9 %collective-permute-done.8.near_ref = f32[3,768]{1,0:T(4,128)S(1)} collective-permute-done((f32[3,768]{1,0:T(4,128)S(1)}, f32[3,768]{1,0:T(4,128)S(1)}, u32[]{:S(2)}, u32[]{:S(2)}) %collective-permute-start.8) | collective-permute-done | bytes 9248 | tf_op jit(solution)/shard_map/ppermute | solution.py:43
  79.2 1.4 %shard_map.53 = (f32[1,512]{1,0:T(1,128)}, f32[1,512]{1,0:T(1,128)}, f32[1,512]{1,0:T(1,128)}) custom-call(bf16[528,768]{1,0:T(8,128)(2,1)S(1)} %shard_map.49.unit_ref, f32[3,768]{1,0:T(4,128)S(1)} %get-tuple-element.11.mine_ref, f32[6,768]{1,0:T(8,128)S(1)} %collective-permute-done.5.swap_ref, f32[3,768]{1,0:T(4,128)S(1)} %collective-permute-done.6.far_ref, ...), custom_call_target="tpu_custom_call" | custom-call | bytes 866304 | tf_op jit(solution)/shard_map/pallas_call | solution.py:30
  (1 shorter events, 0.0 us)
Async XLA Ops:
  1.3 1.1 %copy-start = (bf16[512,768]{1,0:T(8,128)(2,1)S(1)}, bf16[512,768]{1,0:T(8,128)(2,1)}, u32[]{:S(2)}) copy-start(bf16[512,768]{1,0:T(8,128)(2,1)} %emb_ref.1) | copy-start | bytes 2359300
  2.9 31.1 %collective-permute-start.2 = (bf16[528,768]{1,0:T(8,128)(2,1)S(1)}, bf16[528,768]{1,0:T(8,128)(2,1)S(1)}, u32[]{:S(2)}, u32[]{:S(2)}) collective-permute-start(bf16[528,768]{1,0:T(8,128)(2,1)S(1)} %shard_map.49.unit_ref), channel_id=1, source_target_pairs={{0,2},{1,3},{2,4},{3,5},{4,6},{5,7},{6,8},{7,9},{8,10},{9,11},{10,... | collective-permute-start | bytes 2433032 | tf_op jit(solution)/shard_map/ppermute | solution.py:43
  7.2 30.0 %collective-permute-start.1 = (bf16[528,768]{1,0:T(8,128)(2,1)S(1)}, bf16[528,768]{1,0:T(8,128)(2,1)S(1)}, u32[]{:S(2)}, u32[]{:S(2)}) collective-permute-start(bf16[528,768]{1,0:T(8,128)(2,1)S(1)} %shard_map.49.unit_ref), channel_id=1, source_target_pairs={{0,1},{1,0},{2,3},{3,2},{4,5},{5,4},{6,7},{7,6},{8,9},{9,8},{10,11... | collective-permute-start | bytes 2433032 | tf_op jit(solution)/shard_map/ppermute | solution.py:47
  9.1 44.7 %collective-permute-start = (bf16[528,768]{1,0:T(8,128)(2,1)S(1)}, bf16[528,768]{1,0:T(8,128)(2,1)S(1)}, u32[]{:S(2)}, u32[]{:S(2)}) collective-permute-start(bf16[528,768]{1,0:T(8,128)(2,1)S(1)} %shard_map.49.unit_ref), channel_id=1, source_target_pairs={{4,0},{5,1},{6,2},{7,3},{8,4},{9,5},{10,6},{11,7},{12,8},{13,9},{1... | collective-permute-start | bytes 2433032 | tf_op jit(solution)/shard_map/ppermute | solution.py:43
  34.0 19.8 %collective-permute-start.4 = (bf16[528,768]{1,0:T(8,128)(2,1)S(1)}, bf16[528,768]{1,0:T(8,128)(2,1)S(1)}, u32[]{:S(2)}, u32[]{:S(2)}) collective-permute-start(bf16[528,768]{1,0:T(8,128)(2,1)S(1)} %collective-permute-done.2.near_ref), channel_id=1, source_target_pairs={{1,2},{3,4},{5,6},{7,8},{9,10},{11,12},{13,14},{15,16},{17,18},{19... | collective-permute-start | bytes 2433032 | tf_op jit(solution)/shard_map/ppermute | solution.py:43
  35.2 18.6 %collective-permute-start.3 = (bf16[528,768]{1,0:T(8,128)(2,1)S(1)}, bf16[528,768]{1,0:T(8,128)(2,1)S(1)}, u32[]{:S(2)}, u32[]{:S(2)}) collective-permute-start(bf16[528,768]{1,0:T(8,128)(2,1)S(1)} %collective-permute-done.2.near_ref), channel_id=1, source_target_pairs={{0,1},{1,0},{2,3},{3,2},{4,5},{5,4},{6,7},{7,6},{8,9},{9,8},{10,11... | collective-permute-start | bytes 2433032 | tf_op jit(solution)/shard_map/ppermute | solution.py:47
  56.7 16.9 %collective-permute-start.5 = (f32[6,768]{1,0:T(8,128)S(1)}, f32[6,768]{1,0:T(8,128)S(1)}, u32[]{:S(2)}, u32[]{:S(2)}) collective-permute-start(f32[6,768]{1,0:T(8,128)S(1)} %get-tuple-element.12), channel_id=1, source_target_pairs={{0,1},{1,0},{2,3},{3,2},{4,5},{5,4},{6,7},{7,6},{8,9},{9,8},{10,11... | collective-permute-start | bytes 55304 | tf_op jit(solution)/shard_map/ppermute | solution.py:47
  58.7 18.6 %collective-permute-start.6 = (f32[3,768]{1,0:T(4,128)S(1)}, f32[3,768]{1,0:T(4,128)S(1)}, u32[]{:S(2)}, u32[]{:S(2)}) collective-permute-start(f32[3,768]{1,0:T(4,128)S(1)} %get-tuple-element.13), channel_id=1, source_target_pairs={{0,4},{1,5},{2,6},{3,7},{4,8},{5,9},{6,10},{7,11},{8,12},{9,13},{1... | collective-permute-start | bytes 27656 | tf_op jit(solution)/shard_map/ppermute | solution.py:43
  62.5 14.8 %collective-permute-start.7 = (f32[3,768]{1,0:T(4,128)S(1)}, f32[3,768]{1,0:T(4,128)S(1)}, u32[]{:S(2)}, u32[]{:S(2)}) collective-permute-start(f32[3,768]{1,0:T(4,128)S(1)} %get-tuple-element.14), channel_id=1, source_target_pairs={{4,1},{6,3},{8,5},{10,7},{12,9},{14,11},{16,13},{18,15},{20,17},{2... | collective-permute-start | bytes 27656 | tf_op jit(solution)/shard_map/ppermute | solution.py:43
  73.6 5.6 %collective-permute-start.8 = (f32[3,768]{1,0:T(4,128)S(1)}, f32[3,768]{1,0:T(4,128)S(1)}, u32[]{:S(2)}, u32[]{:S(2)}) collective-permute-start(f32[3,768]{1,0:T(4,128)S(1)} %shard_map.52), channel_id=1, source_target_pairs={{2,0},{3,1},{4,2},{5,3},{6,4},{7,5},{8,6},{9,7},{10,8},{11,9},{12,... | collective-permute-start | bytes 27656 | tf_op jit(solution)/shard_map/ppermute | solution.py:43

commit v3 on v2

--- a/solution.py
+++ b/solution.py
@@ -24,7 +24,7 @@
     return jax.ShapeDtypeStruct(dims, dtype)
 
 
-def call(kernel, outs, *args, flops=0, limit=16):
+def call(kernel, outs, *args, limit=16):
     single = not isinstance(outs, (list, tuple))
     size = sum(a.size * a.dtype.itemsize for a in args)
     return pl.pallas_call(
@@ -33,7 +33,7 @@
         in_specs=[VMEM] * len(args),
         out_specs=VMEM if single else [VMEM] * len(outs),
         compiler_params=pltpu.CompilerParams(vmem_limit_bytes=limit << 20),
-        cost_estimate=pl.CostEstimate(flops=flops, bytes_accessed=size, transcendentals=0),
+        cost_estimate=pl.CostEstimate(flops=0, bytes_accessed=size, transcendentals=0),
     )(*args)
 
 
@@ -161,11 +161,11 @@
     return [jnp.concatenate([part[which] for part in parts], axis=1) for which in range(2)]
 
 
-def near_kernel(unit_ref, other_ref, near_ref, out_ref):
-    unit, other = rows_of(unit_ref), rows_of(other_ref)
+def near_kernel(unit_ref, near_ref, out_ref):
+    unit = rows_of(unit_ref)
     rows = unit.shape[0]
-    (_, tag), (_, tag_other), (_, tag_near) = [tail_of(ref) for ref in (unit_ref, other_ref, near_ref)]
-    mine, across, near, parts = Columns(rows), Columns(rows), Columns(rows), []
+    flag = tail_of(unit_ref)[1] == tail_of(near_ref)[1]
+    mine, near, parts = Columns(rows), Columns(rows), []
     for at in range(0, rows, STRIP):
         sims = tile(unit_ref[at : at + STRIP, :], unit)
         row = lax.broadcasted_iota(jnp.int32, sims.shape, 0) + at
@@ -173,11 +173,10 @@
         weights = jnp.where(same, 0.0, jnp.exp2(sims * TO_EXP2))
         sims = jnp.where(same, LOW, sims)
         mine.add(jnp.max(sims, axis=0, keepdims=True), jnp.sum(weights, axis=0, keepdims=True))
-        strip(near_ref[at : at + STRIP, :], (unit, other), (tag_near == tag, tag_near == tag_other), (mine, across), parts)
+        strip(near_ref[at : at + STRIP, :], (unit,), (flag,), (mine,), parts)
     near.add(*whole(parts))
-    for at, columns in ((0, mine), (2, across), (4, near)):
-        columns.store(out_ref, at)
-    out_ref[6:8, :] = jnp.zeros((2, rows), F32)
+    mine.store(out_ref, 0)
+    near.store(out_ref, 2)
 
 
 def far_kernel(
@@ -195,10 +194,12 @@
     last_block = jnp.where(second, other, rows_of(back_ref))
     last_flag = jnp.where(second, tails[0][1], far_tail[1]) == jnp.where(second, tails[1][1], back_tail[1])
     flags = [tag == far_tail[1] for _, tag in tails]
-    far, extra = [], []
+    near_flag = tails[1][1] == tails[2][1]
+    far, extra, back_by = [], [], []
     for at in range(0, rows, STRIP):
         far_rows = far_ref[at : at + STRIP, :]
         strip(far_rows, blocks, flags, columns, far)
+        strip(near_ref[at : at + STRIP, :], (other,), (near_flag,), (across,), back_by)
         last_rows = jnp.where(second, unit_ref[at : at + STRIP, :], far_rows)
         strip(last_rows, (last_block,), (last_flag,), (last,), extra)
     mine.meet(tails[0][0])
@@ -220,9 +221,9 @@
     mine.add(*extra, on[:, :rows])
     across.add(last.top, last.mass, on[:, :rows])
     beyond.add(last.top, last.mass, off[:, :rows])
+    near.add(*whole(back_by))
     mine.load(stats_ref, 0)
-    across.load(stats_ref, 2)
-    near.load(stats_ref, 4)
+    near.load(stats_ref, 2)
     mine.store(mine_ref, 0)
     across.store(swap_ref, 0)
     near_x.store(swap_ref, 3)
@@ -248,10 +249,9 @@
     log_ref[...] = jnp.log(mine.mass)
     mean = jnp.sum(mine.total * mine.total, axis=1, keepdims=True) / width
     centre = mine.total * (lax.rsqrt(mean + 1e-06) / math.sqrt(width))
-    cosines = jnp.zeros((8, rows), F32)
-    for part in parts_of(centre)[::-1]:
-        cosines += tile(jnp.broadcast_to(part, (8, width)), unit)
-    cos_ref[...] = cosines[0:1, :]
+    parts = [part.astype(F32) for part in parts_of(centre)]
+    cosines = tile(jnp.concatenate(parts + [jnp.zeros((5, width), F32)]).astype(BF16), unit)
+    cos_ref[...] = cosines[0:1, :] + (cosines[1:2, :] + cosines[2:3, :])
 
 
 def per_device(embeddings, cluster_ids):
@@ -260,10 +260,10 @@
 
     near = blocks_moved(block, 2)
     far = blocks_moved(block, -4)
-    other = cores_swapped(block)
     back = blocks_moved(near, 1, core=1)
     near_x = cores_swapped(near)
-    stats = call(near_kernel, shape(8, rows), block, other, near)
+    other = cores_swapped(after(block, near))
+    stats = call(near_kernel, shape(4, rows), block, near)
     mine, swap, near_out, far_out, back_out = call(
         far_kernel,
         [shape(3, width), shape(6, width), shape(3, width), shape(3, width), shape(3, width)],

time: 80.9 us -> 78.9 us (0.975)
  starting transfers between devices: 42 us -> 38.9 us
  waiting for transfers between devices: 29.6 us -> 31.4 us
    ppermute x6, starting transfers between devices: 36.3 us -> 32.6 us  [blocks_moved(): return lax.ppermute(value, AXES, pairs)]
    ppermute x6, waiting for transfers between devices: 29.6 us -> 31.3 us  [blocks_moved(): return lax.ppermute(value, AXES, pairs)]
  transfers between devices with their start and end apart: 9 -> 9, of which waited for: 3 -> 4; matrix products, arithmetic and copies ran while one was open for 0% -> 0% of each run, Pallas kernels for 2% -> 2%
where the time goes in v3:
time: 78.9 us; the launch traced here: 78.6 us
  starting transfers between devices  38.9 us (49%)
  waiting for transfers between devices  31.4 us (40%)
  Pallas kernels  5.78 us (7%)
  between operations  1.4 us (2%)
  local copies, waits for them, and re-layouts  1.13 us (1%)
    ppermute x6, starting transfers between devices, blocks_moved(): return lax.ppermute(value, AXES, pairs)  32.6 us
    ppermute x6, waiting for transfers between devices, blocks_moved(): return lax.ppermute(value, AXES, pairs)  31.3 us
    ppermute x3, starting transfers between devices, cores_swapped(): lax.ppermute(value, AXES, [(i, i ^ 1) for i in range(lax.axis_size(AXES))])  6.28 us
    pallas_call x4, Pallas kernels, call(): pl.pallas_call(kernel, out_shape=outs, in_specs=[VMEM] * len(args), out_s...  5.34 us
  transfers between devices with their start and end apart: 9, of which 4 were waited for; matrix products, arithmetic and copies ran while one was open for 0% of the time, Pallas kernels for 2%

profile of v3, /device:TPU:32, one launch (start us, length us, event | category | flops | bytes accessed | tf_op | source)
XLA Modules:
  0.0 78.6 jit_solution(1268523876803332119)
XLA Ops:
  1.3 0.0 copy-start
  1.3 1.1 %copy-done = bf16[512,768]{1,0:T(8,128)(2,1)S(1)} copy-done((bf16[512,768]{1,0:T(8,128)(2,1)S(1)}, bf16[512,768]{1,0:T(8,128)(2,1)}, u32[]{:S(2)}) %copy-start) | copy-done | bytes 786456
  2.4 0.4 shard_map.49.unit_ref
  2.9 4.3 %collective-permute-start.1 = (bf16[528,768]{1,0:T(8,128)(2,1)S(1)}, bf16[528,768]{1,0:T(8,128)(2,1)S(1)}, u32[]{:S(2)}, u32[]{:S(2)}) collective-permute-start(bf16[528,768]{1,0:T(8,128)(2,1)S(1)} %shard_map.49.unit_ref), channel_id=1, source_target_pairs={{0,2},{1,3},{2,4},{3,5},{4,6},{5,7},{6,8},{7,9},{8,10},{9,11},{10,... | collective-permute-start | bytes 2433032 | tf_op jit(solution)/shard_map/ppermute | solution.py:43
  7.2 12.1 %collective-permute-start = (bf16[528,768]{1,0:T(8,128)(2,1)S(1)}, bf16[528,768]{1,0:T(8,128)(2,1)S(1)}, u32[]{:S(2)}, u32[]{:S(2)}) collective-permute-start(bf16[528,768]{1,0:T(8,128)(2,1)S(1)} %shard_map.49.unit_ref), channel_id=1, source_target_pairs={{4,0},{5,1},{6,2},{7,3},{8,4},{9,5},{10,6},{11,7},{12,8},{13,9},{1... | collective-permute-start | bytes 2433032 | tf_op jit(solution)/shard_map/ppermute | solution.py:43
  19.3 14.7 %collective-permute-done.1.near_ref = bf16[528,768]{1,0:T(8,128)(2,1)S(1)} collective-permute-done((bf16[528,768]{1,0:T(8,128)(2,1)S(1)}, bf16[528,768]{1,0:T(8,128)(2,1)S(1)}, u32[]{:S(2)}, u32[]{:S(2)}) %collective-permute-start.1) | collective-permute-done | bytes 811040 | tf_op jit(solution)/shard_map/ppermute | solution.py:43
  34.0 1.9 %collective-permute-start.2 = (bf16[528,768]{1,0:T(8,128)(2,1)S(1)}, bf16[528,768]{1,0:T(8,128)(2,1)S(1)}, u32[]{:S(2)}, u32[]{:S(2)}) collective-permute-start(bf16[528,768]{1,0:T(8,128)(2,1)S(1)} %shard_map.49.unit_ref), channel_id=1, source_target_pairs={{0,1},{1,0},{2,3},{3,2},{4,5},{5,4},{6,7},{7,6},{8,9},{9,8},{10,11... | collective-permute-start | bytes 2433032 | tf_op jit(solution)/shard_map/ppermute | solution.py:47
  35.9 1.3 %collective-permute-start.4 = (bf16[528,768]{1,0:T(8,128)(2,1)S(1)}, bf16[528,768]{1,0:T(8,128)(2,1)S(1)}, u32[]{:S(2)}, u32[]{:S(2)}) collective-permute-start(bf16[528,768]{1,0:T(8,128)(2,1)S(1)} %collective-permute-done.1.near_ref), channel_id=1, source_target_pairs={{1,2},{3,4},{5,6},{7,8},{9,10},{11,12},{13,14},{15,16},{17,18},{19... | collective-permute-start | bytes 2433032 | tf_op jit(solution)/shard_map/ppermute | solution.py:43
  37.2 2.5 %collective-permute-start.3 = (bf16[528,768]{1,0:T(8,128)(2,1)S(1)}, bf16[528,768]{1,0:T(8,128)(2,1)S(1)}, u32[]{:S(2)}, u32[]{:S(2)}) collective-permute-start(bf16[528,768]{1,0:T(8,128)(2,1)S(1)} %collective-permute-done.1.near_ref), channel_id=1, source_target_pairs={{0,1},{1,0},{2,3},{3,2},{4,5},{5,4},{6,7},{7,6},{8,9},{9,8},{10,11... | collective-permute-start | bytes 2433032 | tf_op jit(solution)/shard_map/ppermute | solution.py:47
  39.6 1.2 %shard_map.50.stats_ref = f32[4,512]{1,0:T(4,128)S(1)} custom-call(bf16[528,768]{1,0:T(8,128)(2,1)S(1)} %shard_map.49.unit_ref, bf16[528,768]{1,0:T(8,128)(2,1)S(1)} %collective-permute-done.1.near_ref), custom_call_target="tpu_custom_call" | custom-call | bytes 1622016 | tf_op jit(solution)/shard_map/pallas_call | solution.py:30
  40.8 10.1 %collective-permute-done.far_ref = bf16[528,768]{1,0:T(8,128)(2,1)S(1)} collective-permute-done((bf16[528,768]{1,0:T(8,128)(2,1)S(1)}, bf16[528,768]{1,0:T(8,128)(2,1)S(1)}, u32[]{:S(2)}, u32[]{:S(2)}) %collective-permute-start) | collective-permute-done | bytes 811040 | tf_op jit(solution)/shard_map/ppermute | solution.py:43
  50.9 0.0 collective-permute-done.2.other_ref
  50.9 3.9 %collective-permute-done.4.back_ref = bf16[528,768]{1,0:T(8,128)(2,1)S(1)} collective-permute-done((bf16[528,768]{1,0:T(8,128)(2,1)S(1)}, bf16[528,768]{1,0:T(8,128)(2,1)S(1)}, u32[]{:S(2)}, u32[]{:S(2)}) %collective-permute-start.4) | collective-permute-done | bytes 811040 | tf_op jit(solution)/shard_map/ppermute | solution.py:43
  54.9 0.0 collective-permute-done.3.near_x_ref
  54.9 3.2 %shard_map.51 = (f32[3,768]{1,0:T(4,128)S(1)}, f32[6,768]{1,0:T(8,128)S(1)}, f32[3,768]{1,0:T(4,128)S(1)}, f32[3,768]{1,0:T(4,128)S(1)}, f32[3,768]{1,0:T(4,128)S(1)}) custom-call(bf16[528,768]{1,0:T(8,128)(2,1)S(1)} %collective-permute-done.far_ref, bf16[528,768]{1,0:T(8,128)(2,1)S(1)} %shard_map.49.unit_ref, ...), custom_call_target="tpu_custom_call" | custom-call | bytes 4874240 | tf_op jit(solution)/shard_map/pallas_call | solution.py:30
  58.1 1.9 %collective-permute-start.5 = (f32[6,768]{1,0:T(8,128)S(1)}, f32[6,768]{1,0:T(8,128)S(1)}, u32[]{:S(2)}, u32[]{:S(2)}) collective-permute-start(f32[6,768]{1,0:T(8,128)S(1)} %get-tuple-element.14), channel_id=1, source_target_pairs={{0,1},{1,0},{2,3},{3,2},{4,5},{5,4},{6,7},{7,6},{8,9},{9,8},{10,11... | collective-permute-start | bytes 55304 | tf_op jit(solution)/shard_map/ppermute | solution.py:47
  60.0 1.9 %collective-permute-start.6 = (f32[3,768]{1,0:T(4,128)S(1)}, f32[3,768]{1,0:T(4,128)S(1)}, u32[]{:S(2)}, u32[]{:S(2)}) collective-permute-start(f32[3,768]{1,0:T(4,128)S(1)} %get-tuple-element.15), channel_id=1, source_target_pairs={{0,4},{1,5},{2,6},{3,7},{4,8},{5,9},{6,10},{7,11},{8,12},{9,13},{1... | collective-permute-start | bytes 27656 | tf_op jit(solution)/shard_map/ppermute | solution.py:43
  61.9 10.1 %collective-permute-start.7 = (f32[3,768]{1,0:T(4,128)S(1)}, f32[3,768]{1,0:T(4,128)S(1)}, u32[]{:S(2)}, u32[]{:S(2)}) collective-permute-start(f32[3,768]{1,0:T(4,128)S(1)} %get-tuple-element.16), channel_id=1, source_target_pairs={{4,1},{6,3},{8,5},{10,7},{12,9},{14,11},{16,13},{18,15},{20,17},{2... | collective-permute-start | bytes 27656 | tf_op jit(solution)/shard_map/ppermute | solution.py:43
  72.0 0.0 collective-permute-done.5.swap_ref
  72.0 2.9 %collective-permute-start.8 = (f32[3,768]{1,0:T(4,128)S(1)}, f32[3,768]{1,0:T(4,128)S(1)}, u32[]{:S(2)}, u32[]{:S(2)}) collective-permute-start(f32[3,768]{1,0:T(4,128)S(1)} %shard_map.52), channel_id=1, source_target_pairs={{2,0},{3,1},{4,2},{5,3},{6,4},{7,5},{8,6},{9,7},{10,8},{11,9},{12,... | collective-permute-start | bytes 27656 | tf_op jit(solution)/shard_map/ppermute | solution.py:43
  75.0 0.0 collective-permute-done.6.far_ref
  75.0 0.0 collective-permute-done.7.back_ref
  75.0 2.6 %collective-permute-done.8.near_ref = f32[3,768]{1,0:T(4,128)S(1)} collective-permute-done((f32[3,768]{1,0:T(4,128)S(1)}, f32[3,768]{1,0:T(4,128)S(1)}, u32[]{:S(2)}, u32[]{:S(2)}) %collective-permute-start.8) | collective-permute-done | bytes 9248 | tf_op jit(solution)/shard_map/ppermute | solution.py:43
  77.6 1.0 %shard_map.53 = (f32[1,512]{1,0:T(1,128)}, f32[1,512]{1,0:T(1,128)}, f32[1,512]{1,0:T(1,128)}) custom-call(bf16[528,768]{1,0:T(8,128)(2,1)S(1)} %shard_map.49.unit_ref, f32[3,768]{1,0:T(4,128)S(1)} %get-tuple-element.13.mine_ref, f32[6,768]{1,0:T(8,128)S(1)} %collective-permute-done.5.swap_ref, f32[3,768]{1,0:T(4,128)S(1)} %collective-permute-done.6.far_ref, ...), custom_call_target="tpu_custom_call" | custom-call | bytes 866304 | tf_op jit(solution)/shard_map/pallas_call | solution.py:30
  (1 shorter events, 0.0 us)
Async XLA Ops:
  1.3 1.1 %copy-start = (bf16[512,768]{1,0:T(8,128)(2,1)S(1)}, bf16[512,768]{1,0:T(8,128)(2,1)}, u32[]{:S(2)}) copy-start(bf16[512,768]{1,0:T(8,128)(2,1)} %emb_ref.1) | copy-start | bytes 2359300
  2.9 31.1 %collective-permute-start.1 = (bf16[528,768]{1,0:T(8,128)(2,1)S(1)}, bf16[528,768]{1,0:T(8,128)(2,1)S(1)}, u32[]{:S(2)}, u32[]{:S(2)}) collective-permute-start(bf16[528,768]{1,0:T(8,128)(2,1)S(1)} %shard_map.49.unit_ref), channel_id=1, source_target_pairs={{0,2},{1,3},{2,4},{3,5},{4,6},{5,7},{6,8},{7,9},{8,10},{9,11},{10,... | collective-permute-start | bytes 2433032 | tf_op jit(solution)/shard_map/ppermute | solution.py:43
  7.2 43.8 %collective-permute-start = (bf16[528,768]{1,0:T(8,128)(2,1)S(1)}, bf16[528,768]{1,0:T(8,128)(2,1)S(1)}, u32[]{:S(2)}, u32[]{:S(2)}) collective-permute-start(bf16[528,768]{1,0:T(8,128)(2,1)S(1)} %shard_map.49.unit_ref), channel_id=1, source_target_pairs={{4,0},{5,1},{6,2},{7,3},{8,4},{9,5},{10,6},{11,7},{12,8},{13,9},{1... | collective-permute-start | bytes 2433032 | tf_op jit(solution)/shard_map/ppermute | solution.py:43
  34.0 17.0 %collective-permute-start.2 = (bf16[528,768]{1,0:T(8,128)(2,1)S(1)}, bf16[528,768]{1,0:T(8,128)(2,1)S(1)}, u32[]{:S(2)}, u32[]{:S(2)}) collective-permute-start(bf16[528,768]{1,0:T(8,128)(2,1)S(1)} %shard_map.49.unit_ref), channel_id=1, source_target_pairs={{0,1},{1,0},{2,3},{3,2},{4,5},{5,4},{6,7},{7,6},{8,9},{9,8},{10,11... | collective-permute-start | bytes 2433032 | tf_op jit(solution)/shard_map/ppermute | solution.py:47
  35.9 19.0 %collective-permute-start.4 = (bf16[528,768]{1,0:T(8,128)(2,1)S(1)}, bf16[528,768]{1,0:T(8,128)(2,1)S(1)}, u32[]{:S(2)}, u32[]{:S(2)}) collective-permute-start(bf16[528,768]{1,0:T(8,128)(2,1)S(1)} %collective-permute-done.1.near_ref), channel_id=1, source_target_pairs={{1,2},{3,4},{5,6},{7,8},{9,10},{11,12},{13,14},{15,16},{17,18},{19... | collective-permute-start | bytes 2433032 | tf_op jit(solution)/shard_map/ppermute | solution.py:43
  37.2 17.7 %collective-permute-start.3 = (bf16[528,768]{1,0:T(8,128)(2,1)S(1)}, bf16[528,768]{1,0:T(8,128)(2,1)S(1)}, u32[]{:S(2)}, u32[]{:S(2)}) collective-permute-start(bf16[528,768]{1,0:T(8,128)(2,1)S(1)} %collective-permute-done.1.near_ref), channel_id=1, source_target_pairs={{0,1},{1,0},{2,3},{3,2},{4,5},{5,4},{6,7},{7,6},{8,9},{9,8},{10,11... | collective-permute-start | bytes 2433032 | tf_op jit(solution)/shard_map/ppermute | solution.py:47
  58.1 13.9 %collective-permute-start.5 = (f32[6,768]{1,0:T(8,128)S(1)}, f32[6,768]{1,0:T(8,128)S(1)}, u32[]{:S(2)}, u32[]{:S(2)}) collective-permute-start(f32[6,768]{1,0:T(8,128)S(1)} %get-tuple-element.14), channel_id=1, source_target_pairs={{0,1},{1,0},{2,3},{3,2},{4,5},{5,4},{6,7},{7,6},{8,9},{9,8},{10,11... | collective-permute-start | bytes 55304 | tf_op jit(solution)/shard_map/ppermute | solution.py:47
  60.0 15.0 %collective-permute-start.6 = (f32[3,768]{1,0:T(4,128)S(1)}, f32[3,768]{1,0:T(4,128)S(1)}, u32[]{:S(2)}, u32[]{:S(2)}) collective-permute-start(f32[3,768]{1,0:T(4,128)S(1)} %get-tuple-element.15), channel_id=1, source_target_pairs={{0,4},{1,5},{2,6},{3,7},{4,8},{5,9},{6,10},{7,11},{8,12},{9,13},{1... | collective-permute-start | bytes 27656 | tf_op jit(solution)/shard_map/ppermute | solution.py:43
  61.9 13.1 %collective-permute-start.7 = (f32[3,768]{1,0:T(4,128)S(1)}, f32[3,768]{1,0:T(4,128)S(1)}, u32[]{:S(2)}, u32[]{:S(2)}) collective-permute-start(f32[3,768]{1,0:T(4,128)S(1)} %get-tuple-element.16), channel_id=1, source_target_pairs={{4,1},{6,3},{8,5},{10,7},{12,9},{14,11},{16,13},{18,15},{20,17},{2... | collective-permute-start | bytes 27656 | tf_op jit(solution)/shard_map/ppermute | solution.py:43
  72.0 5.6 %collective-permute-start.8 = (f32[3,768]{1,0:T(4,128)S(1)}, f32[3,768]{1,0:T(4,128)S(1)}, u32[]{:S(2)}, u32[]{:S(2)}) collective-permute-start(f32[3,768]{1,0:T(4,128)S(1)} %shard_map.52), channel_id=1, source_target_pairs={{2,0},{3,1},{4,2},{5,3},{6,4},{7,5},{8,6},{9,7},{10,8},{11,9},{12,... | collective-permute-start | bytes 27656 | tf_op jit(solution)/shard_map/ppermute | solution.py:43

commit v4 on v3

--- a/solution.py
+++ b/solution.py
@@ -232,18 +232,18 @@
     beyond.store(back_out_ref, 0)
 
 
-def near_sum_kernel(near_ref, swap_ref, out_ref, *, rows):
-    near = Columns(rows, near_ref.shape[1])
-    near.receive(near_ref, 0)
-    near.receive(swap_ref, 3)
-    near.store(out_ref, 0)
-
-
-def final_kernel(unit_ref, mine_ref, swap_ref, far_ref, back_ref, near_ref, top_ref, log_ref, cos_ref):
+def sum_kernel(*refs, rows, places):
+    found = Columns(rows, refs[-1].shape[1])
+    for ref, place in zip(refs, places):
+        found.receive(ref, place)
+    found.store(refs[-1], 0)
+
+
+def final_kernel(unit_ref, most_ref, back_ref, top_ref, log_ref, cos_ref):
     unit = rows_of(unit_ref)
     rows, width = unit.shape
     mine = Columns(rows, width)
-    for ref in (mine_ref, swap_ref, far_ref, back_ref, near_ref):
+    for ref in (most_ref, back_ref):
         mine.receive(ref, 0)
     top_ref[...] = mine.top
     log_ref[...] = jnp.log(mine.mass)
@@ -271,10 +271,11 @@
     )
     swap_in = cores_swapped(swap)
     far_in = blocks_moved(far_out, 4)
-    back_in = blocks_moved(back_out, -3, core=0)
-    near_all = call(functools.partial(near_sum_kernel, rows=rows), shape(3, width), near_out, swap_in)
+    near_all = call(functools.partial(sum_kernel, rows=rows, places=(0, 3)), shape(3, width), near_out, swap_in)
     near_in = blocks_moved(near_all, -2)
-    outs = call(final_kernel, [shape(1, rows)] * 3, block, mine, swap_in, far_in, back_in, near_in)
+    back_in = blocks_moved(after(back_out, near_all), -3, core=0)
+    most = call(functools.partial(sum_kernel, rows=rows, places=(0, 0, 0, 0)), shape(3, width), mine, swap_in, far_in, near_in)
+    outs = call(final_kernel, [shape(1, rows)] * 3, block, most, back_in)
     return tuple(out.reshape(rows) for out in outs)
 
 

time: 78.9 us -> 78 us (0.989)
  waiting for transfers between devices: 31.4 us -> 30.1 us
    ppermute x6, waiting for transfers between devices: 31.3 us -> 30.1 us  [blocks_moved(): return lax.ppermute(value, AXES, pairs)]
    pallas_call x4 -> x5, Pallas kernels: 5.34 us -> 5.34 us  [call(): pl.pallas_call(kernel, out_shape=outs, in_specs=[VMEM] * len(args), out_s...]
where the time goes in v4:
time: 78 us; the launch traced here: 77 us
  starting transfers between devices  38.6 us (49%)
  waiting for transfers between devices  30.1 us (39%)
  Pallas kernels  5.79 us (7%)
  between operations  1.41 us (2%)
  local copies, waits for them, and re-layouts  1.13 us (1%)
    ppermute x6, starting transfers between devices, blocks_moved(): return lax.ppermute(value, AXES, pairs)  32.3 us
    ppermute x6, waiting for transfers between devices, blocks_moved(): return lax.ppermute(value, AXES, pairs)  30.1 us
    ppermute x3, starting transfers between devices, cores_swapped(): lax.ppermute(value, AXES, [(i, i ^ 1) for i in range(lax.axis_size(AXES))])  6.28 us
    pallas_call x5, Pallas kernels, call(): pl.pallas_call(kernel, out_shape=outs, in_specs=[VMEM] * len(args), out_s...  5.34 us
  transfers between devices with their start and end apart: 9, of which 4 were waited for; matrix products, arithmetic and copies ran while one was open for 0% of the time, Pallas kernels for 2%

profile of v4, /device:TPU:32, one launch (start us, length us, event | category | flops | bytes accessed | tf_op | source)
XLA Modules:
  0.0 77.0 jit_solution(17505932032360753903)
XLA Ops:
  1.3 0.0 copy-start
  1.3 1.1 %copy-done = bf16[512,768]{1,0:T(8,128)(2,1)S(1)} copy-done((bf16[512,768]{1,0:T(8,128)(2,1)S(1)}, bf16[512,768]{1,0:T(8,128)(2,1)}, u32[]{:S(2)}) %copy-start) | copy-done | bytes 786456
  2.4 0.4 shard_map.49.unit_ref
  2.9 4.3 %collective-permute-start.1 = (bf16[528,768]{1,0:T(8,128)(2,1)S(1)}, bf16[528,768]{1,0:T(8,128)(2,1)S(1)}, u32[]{:S(2)}, u32[]{:S(2)}) collective-permute-start(bf16[528,768]{1,0:T(8,128)(2,1)S(1)} %shard_map.49.unit_ref), channel_id=1, source_target_pairs={{0,2},{1,3},{2,4},{3,5},{4,6},{5,7},{6,8},{7,9},{8,10},{9,11},{10,... | collective-permute-start | bytes 2433032 | tf_op jit(solution)/shard_map/ppermute | solution.py:43
  7.2 12.1 %collective-permute-start = (bf16[528,768]{1,0:T(8,128)(2,1)S(1)}, bf16[528,768]{1,0:T(8,128)(2,1)S(1)}, u32[]{:S(2)}, u32[]{:S(2)}) collective-permute-start(bf16[528,768]{1,0:T(8,128)(2,1)S(1)} %shard_map.49.unit_ref), channel_id=1, source_target_pairs={{4,0},{5,1},{6,2},{7,3},{8,4},{9,5},{10,6},{11,7},{12,8},{13,9},{1... | collective-permute-start | bytes 2433032 | tf_op jit(solution)/shard_map/ppermute | solution.py:43
  19.3 14.7 %collective-permute-done.1.near_ref = bf16[528,768]{1,0:T(8,128)(2,1)S(1)} collective-permute-done((bf16[528,768]{1,0:T(8,128)(2,1)S(1)}, bf16[528,768]{1,0:T(8,128)(2,1)S(1)}, u32[]{:S(2)}, u32[]{:S(2)}) %collective-permute-start.1) | collective-permute-done | bytes 811040 | tf_op jit(solution)/shard_map/ppermute | solution.py:43
  34.0 1.9 %collective-permute-start.2 = (bf16[528,768]{1,0:T(8,128)(2,1)S(1)}, bf16[528,768]{1,0:T(8,128)(2,1)S(1)}, u32[]{:S(2)}, u32[]{:S(2)}) collective-permute-start(bf16[528,768]{1,0:T(8,128)(2,1)S(1)} %shard_map.49.unit_ref), channel_id=1, source_target_pairs={{0,1},{1,0},{2,3},{3,2},{4,5},{5,4},{6,7},{7,6},{8,9},{9,8},{10,11... | collective-permute-start | bytes 2433032 | tf_op jit(solution)/shard_map/ppermute | solution.py:47
  35.9 1.3 %collective-permute-start.4 = (bf16[528,768]{1,0:T(8,128)(2,1)S(1)}, bf16[528,768]{1,0:T(8,128)(2,1)S(1)}, u32[]{:S(2)}, u32[]{:S(2)}) collective-permute-start(bf16[528,768]{1,0:T(8,128)(2,1)S(1)} %collective-permute-done.1.near_ref), channel_id=1, source_target_pairs={{1,2},{3,4},{5,6},{7,8},{9,10},{11,12},{13,14},{15,16},{17,18},{19... | collective-permute-start | bytes 2433032 | tf_op jit(solution)/shard_map/ppermute | solution.py:43
  37.2 2.5 %collective-permute-start.3 = (bf16[528,768]{1,0:T(8,128)(2,1)S(1)}, bf16[528,768]{1,0:T(8,128)(2,1)S(1)}, u32[]{:S(2)}, u32[]{:S(2)}) collective-permute-start(bf16[528,768]{1,0:T(8,128)(2,1)S(1)} %collective-permute-done.1.near_ref), channel_id=1, source_target_pairs={{0,1},{1,0},{2,3},{3,2},{4,5},{5,4},{6,7},{7,6},{8,9},{9,8},{10,11... | collective-permute-start | bytes 2433032 | tf_op jit(solution)/shard_map/ppermute | solution.py:47
  39.6 1.2 %shard_map.50.stats_ref = f32[4,512]{1,0:T(4,128)S(1)} custom-call(bf16[528,768]{1,0:T(8,128)(2,1)S(1)} %shard_map.49.unit_ref, bf16[528,768]{1,0:T(8,128)(2,1)S(1)} %collective-permute-done.1.near_ref), custom_call_target="tpu_custom_call" | custom-call | bytes 1622016 | tf_op jit(solution)/shard_map/pallas_call | solution.py:30
  40.8 10.1 %collective-permute-done.far_ref = bf16[528,768]{1,0:T(8,128)(2,1)S(1)} collective-permute-done((bf16[528,768]{1,0:T(8,128)(2,1)S(1)}, bf16[528,768]{1,0:T(8,128)(2,1)S(1)}, u32[]{:S(2)}, u32[]{:S(2)}) %collective-permute-start) | collective-permute-done | bytes 811040 | tf_op jit(solution)/shard_map/ppermute | solution.py:43
  50.9 0.0 collective-permute-done.2.other_ref
  50.9 3.9 %collective-permute-done.4.back_ref = bf16[528,768]{1,0:T(8,128)(2,1)S(1)} collective-permute-done((bf16[528,768]{1,0:T(8,128)(2,1)S(1)}, bf16[528,768]{1,0:T(8,128)(2,1)S(1)}, u32[]{:S(2)}, u32[]{:S(2)}) %collective-permute-start.4) | collective-permute-done | bytes 811040 | tf_op jit(solution)/shard_map/ppermute | solution.py:43
  54.9 0.0 collective-permute-done.3.near_x_ref
  54.9 3.2 %shard_map.51 = (f32[3,768]{1,0:T(4,128)S(1)}, f32[6,768]{1,0:T(8,128)S(1)}, f32[3,768]{1,0:T(4,128)S(1)}, f32[3,768]{1,0:T(4,128)S(1)}, f32[3,768]{1,0:T(4,128)S(1)}) custom-call(bf16[528,768]{1,0:T(8,128)(2,1)S(1)} %collective-permute-done.far_ref, bf16[528,768]{1,0:T(8,128)(2,1)S(1)} %shard_map.49.unit_ref, ...), custom_call_target="tpu_custom_call" | custom-call | bytes 4874240 | tf_op jit(solution)/shard_map/pallas_call | solution.py:30
  58.1 1.9 %collective-permute-start.5 = (f32[6,768]{1,0:T(8,128)S(1)}, f32[6,768]{1,0:T(8,128)S(1)}, u32[]{:S(2)}, u32[]{:S(2)}) collective-permute-start(f32[6,768]{1,0:T(8,128)S(1)} %get-tuple-element.15), channel_id=1, source_target_pairs={{0,1},{1,0},{2,3},{3,2},{4,5},{5,4},{6,7},{7,6},{8,9},{9,8},{10,11... | collective-permute-start | bytes 55304 | tf_op jit(solution)/shard_map/ppermute | solution.py:47
  60.0 1.9 %collective-permute-start.6 = (f32[3,768]{1,0:T(4,128)S(1)}, f32[3,768]{1,0:T(4,128)S(1)}, u32[]{:S(2)}, u32[]{:S(2)}) collective-permute-start(f32[3,768]{1,0:T(4,128)S(1)} %get-tuple-element.16), channel_id=1, source_target_pairs={{0,4},{1,5},{2,6},{3,7},{4,8},{5,9},{6,10},{7,11},{8,12},{9,13},{1... | collective-permute-start | bytes 27656 | tf_op jit(solution)/shard_map/ppermute | solution.py:43
  61.9 0.0 collective-permute-done.5.refs_1_
  61.9 8.4 %collective-permute-start.7 = (f32[3,768]{1,0:T(4,128)S(1)}, f32[3,768]{1,0:T(4,128)S(1)}, u32[]{:S(2)}, u32[]{:S(2)}) collective-permute-start(f32[3,768]{1,0:T(4,128)S(1)} %shard_map.52), channel_id=1, source_target_pairs={{2,0},{3,1},{4,2},{5,3},{6,4},{7,5},{8,6},{9,7},{10,8},{11,9},{12,... | collective-permute-start | bytes 27656 | tf_op jit(solution)/shard_map/ppermute | solution.py:43
  70.3 4.4 %collective-permute-start.8 = (f32[3,768]{1,0:T(4,128)S(1)}, f32[3,768]{1,0:T(4,128)S(1)}, u32[]{:S(2)}, u32[]{:S(2)}) collective-permute-start(f32[3,768]{1,0:T(4,128)S(1)} %get-tuple-element.19), channel_id=1, source_target_pairs={{4,1},{6,3},{8,5},{10,7},{12,9},{14,11},{16,13},{18,15},{20,17},{2... | collective-permute-start | bytes 27656 | tf_op jit(solution)/shard_map/ppermute | solution.py:43
  74.7 0.0 collective-permute-done.6.refs_2_
  74.7 0.0 collective-permute-done.7.refs_3_
  74.7 1.3 %collective-permute-done.8.back_ref = f32[3,768]{1,0:T(4,128)S(1)} collective-permute-done((f32[3,768]{1,0:T(4,128)S(1)}, f32[3,768]{1,0:T(4,128)S(1)}, u32[]{:S(2)}, u32[]{:S(2)}) %collective-permute-start.8) | collective-permute-done | bytes 9248 | tf_op jit(solution)/shard_map/ppermute | solution.py:43
  76.1 1.0 %shard_map.54 = (f32[1,512]{1,0:T(1,128)}, f32[1,512]{1,0:T(1,128)}, f32[1,512]{1,0:T(1,128)}) custom-call(bf16[528,768]{1,0:T(8,128)(2,1)S(1)} %shard_map.49.unit_ref, f32[3,768]{1,0:T(4,128)S(1)} %shard_map.53.most_ref, f32[3,768]{1,0:T(4,128)S(1)} %collective-permute-done.8.back_ref), custom_call_target="tpu_custom_call" | custom-call | bytes 829440 | tf_op jit(solution)/shard_map/pallas_call | solution.py:30
  (2 shorter events, 0.0 us)
Async XLA Ops:
  1.3 1.1 %copy-start = (bf16[512,768]{1,0:T(8,128)(2,1)S(1)}, bf16[512,768]{1,0:T(8,128)(2,1)}, u32[]{:S(2)}) copy-start(bf16[512,768]{1,0:T(8,128)(2,1)} %emb_ref.1) | copy-start | bytes 2359300
  2.9 31.1 %collective-permute-start.1 = (bf16[528,768]{1,0:T(8,128)(2,1)S(1)}, bf16[528,768]{1,0:T(8,128)(2,1)S(1)}, u32[]{:S(2)}, u32[]{:S(2)}) collective-permute-start(bf16[528,768]{1,0:T(8,128)(2,1)S(1)} %shard_map.49.unit_ref), channel_id=1, source_target_pairs={{0,2},{1,3},{2,4},{3,5},{4,6},{5,7},{6,8},{7,9},{8,10},{9,11},{10,... | collective-permute-start | bytes 2433032 | tf_op jit(solution)/shard_map/ppermute | solution.py:43
  7.2 43.8 %collective-permute-start = (bf16[528,768]{1,0:T(8,128)(2,1)S(1)}, bf16[528,768]{1,0:T(8,128)(2,1)S(1)}, u32[]{:S(2)}, u32[]{:S(2)}) collective-permute-start(bf16[528,768]{1,0:T(8,128)(2,1)S(1)} %shard_map.49.unit_ref), channel_id=1, source_target_pairs={{4,0},{5,1},{6,2},{7,3},{8,4},{9,5},{10,6},{11,7},{12,8},{13,9},{1... | collective-permute-start | bytes 2433032 | tf_op jit(solution)/shard_map/ppermute | solution.py:43
  34.0 17.0 %collective-permute-start.2 = (bf16[528,768]{1,0:T(8,128)(2,1)S(1)}, bf16[528,768]{1,0:T(8,128)(2,1)S(1)}, u32[]{:S(2)}, u32[]{:S(2)}) collective-permute-start(bf16[528,768]{1,0:T(8,128)(2,1)S(1)} %shard_map.49.unit_ref), channel_id=1, source_target_pairs={{0,1},{1,0},{2,3},{3,2},{4,5},{5,4},{6,7},{7,6},{8,9},{9,8},{10,11... | collective-permute-start | bytes 2433032 | tf_op jit(solution)/shard_map/ppermute | solution.py:47
  35.9 19.0 %collective-permute-start.4 = (bf16[528,768]{1,0:T(8,128)(2,1)S(1)}, bf16[528,768]{1,0:T(8,128)(2,1)S(1)}, u32[]{:S(2)}, u32[]{:S(2)}) collective-permute-start(bf16[528,768]{1,0:T(8,128)(2,1)S(1)} %collective-permute-done.1.near_ref), channel_id=1, source_target_pairs={{1,2},{3,4},{5,6},{7,8},{9,10},{11,12},{13,14},{15,16},{17,18},{19... | collective-permute-start | bytes 2433032 | tf_op jit(solution)/shard_map/ppermute | solution.py:43
  37.2 17.7 %collective-permute-start.3 = (bf16[528,768]{1,0:T(8,128)(2,1)S(1)}, bf16[528,768]{1,0:T(8,128)(2,1)S(1)}, u32[]{:S(2)}, u32[]{:S(2)}) collective-permute-start(bf16[528,768]{1,0:T(8,128)(2,1)S(1)} %collective-permute-done.1.near_ref), channel_id=1, source_target_pairs={{0,1},{1,0},{2,3},{3,2},{4,5},{5,4},{6,7},{7,6},{8,9},{9,8},{10,11... | collective-permute-start | bytes 2433032 | tf_op jit(solution)/shard_map/ppermute | solution.py:47
  58.1 3.9 %collective-permute-start.5 = (f32[6,768]{1,0:T(8,128)S(1)}, f32[6,768]{1,0:T(8,128)S(1)}, u32[]{:S(2)}, u32[]{:S(2)}) collective-permute-start(f32[6,768]{1,0:T(8,128)S(1)} %get-tuple-element.15), channel_id=1, source_target_pairs={{0,1},{1,0},{2,3},{3,2},{4,5},{5,4},{6,7},{7,6},{8,9},{9,8},{10,11... | collective-permute-start | bytes 55304 | tf_op jit(solution)/shard_map/ppermute | solution.py:47
  60.0 14.7 %collective-permute-start.6 = (f32[3,768]{1,0:T(4,128)S(1)}, f32[3,768]{1,0:T(4,128)S(1)}, u32[]{:S(2)}, u32[]{:S(2)}) collective-permute-start(f32[3,768]{1,0:T(4,128)S(1)} %get-tuple-element.16), channel_id=1, source_target_pairs={{0,4},{1,5},{2,6},{3,7},{4,8},{5,9},{6,10},{7,11},{8,12},{9,13},{1... | collective-permute-start | bytes 27656 | tf_op jit(solution)/shard_map/ppermute | solution.py:43
  61.9 12.8 %collective-permute-start.7 = (f32[3,768]{1,0:T(4,128)S(1)}, f32[3,768]{1,0:T(4,128)S(1)}, u32[]{:S(2)}, u32[]{:S(2)}) collective-permute-start(f32[3,768]{1,0:T(4,128)S(1)} %shard_map.52), channel_id=1, source_target_pairs={{2,0},{3,1},{4,2},{5,3},{6,4},{7,5},{8,6},{9,7},{10,8},{11,9},{12,... | collective-permute-start | bytes 27656 | tf_op jit(solution)/shard_map/ppermute | solution.py:43
  70.3 5.8 %collective-permute-start.8 = (f32[3,768]{1,0:T(4,128)S(1)}, f32[3,768]{1,0:T(4,128)S(1)}, u32[]{:S(2)}, u32[]{:S(2)}) collective-permute-start(f32[3,768]{1,0:T(4,128)S(1)} %get-tuple-element.19), channel_id=1, source_target_pairs={{4,1},{6,3},{8,5},{10,7},{12,9},{14,11},{16,13},{18,15},{20,17},{2... | collective-permute-start | bytes 27656 | tf_op jit(solution)/shard_map/ppermute | solution.py:43

commit v5 on v4

--- a/solution.py
+++ b/solution.py
@@ -195,13 +195,40 @@
     last_flag = jnp.where(second, tails[0][1], far_tail[1]) == jnp.where(second, tails[1][1], back_tail[1])
     flags = [tag == far_tail[1] for _, tag in tails]
     near_flag = tails[1][1] == tails[2][1]
-    far, extra, back_by = [], [], []
-    for at in range(0, rows, STRIP):
-        far_rows = far_ref[at : at + STRIP, :]
-        strip(far_rows, blocks, flags, columns, far)
-        strip(near_ref[at : at + STRIP, :], (other,), (near_flag,), (across,), back_by)
-        last_rows = jnp.where(second, unit_ref[at : at + STRIP, :], far_rows)
-        strip(last_rows, (last_block,), (last_flag,), (last,), extra)
+    def far_tiles():
+        found, parts = [Columns(rows) for _ in blocks], []
+        for at in range(0, rows, STRIP):
+            strip(far_ref[at : at + STRIP, :], blocks, flags, found, parts)
+        return [value for column in found for value in (column.top, column.mass)] + whole(parts)
+
+    def near_tiles():
+        found, parts = Columns(rows), []
+        for at in range(0, rows, STRIP):
+            strip(near_ref[at : at + STRIP, :], (other,), (near_flag,), (found,), parts)
+        return [found.top, found.mass] + whole(parts)
+
+    def last_tiles():
+        found, parts = Columns(rows), []
+        for at in range(0, rows, STRIP):
+            last_rows = jnp.where(second, unit_ref[at : at + STRIP, :], far_ref[at : at + STRIP, :])
+            strip(last_rows, (last_block,), (last_flag,), (found,), parts)
+        return [found.top, found.mass] + whole(parts)
+
+    def where_met(some, tiles, pairs):
+        met = jnp.max(functools.reduce(jnp.maximum, [jnp.where(flag[:, :LANES], 1.0, 0.0) for flag in some])) > 0.5
+        nothing = [jnp.full((1, rows), LOW, F32), jnp.zeros((1, rows), F32)] * pairs
+        return lax.cond(met, tiles, lambda: nothing)
+
+    found = where_met(flags, far_tiles, 5)
+    for at, column in enumerate(columns):
+        column.add(found[2 * at], found[2 * at + 1])
+    far = found[8:]
+    found = where_met((near_flag,), near_tiles, 2)
+    across.add(found[0], found[1])
+    back_by = found[2:]
+    found = where_met((last_flag,), last_tiles, 2)
+    last.add(found[0], found[1])
+    extra = found[2:]
     mine.meet(tails[0][0])
     for (total, tag), owner in zip(tails[:2], (mine, across)):
         near.meet(total, tag == tails[2][1])
@@ -215,13 +242,12 @@
     mine.meet(tails[1][0], on)
     beyond.meet(far_tail[0], off)
     theirs.meet(back_tail[0], off)
-    extra = whole(extra)
-    theirs.add(*whole(far))
+    theirs.add(*far)
     theirs.add(*extra, off[:, :rows])
     mine.add(*extra, on[:, :rows])
     across.add(last.top, last.mass, on[:, :rows])
     beyond.add(last.top, last.mass, off[:, :rows])
-    near.add(*whole(back_by))
+    near.add(*back_by)
     mine.load(stats_ref, 0)
     near.load(stats_ref, 2)
     mine.store(mine_ref, 0)

time: 78 us -> 78.5 us (level); the launches traced: 77 us -> 78.3 us
  starting transfers between devices: 38.6 us -> 41.6 us
  Pallas kernels: 5.79 us -> 4.11 us
    ppermute x6, starting transfers between devices: 32.3 us -> 35.3 us  [blocks_moved(): return lax.ppermute(value, AXES, pairs)]
    pallas_call x5, Pallas kernels: 5.34 us -> 3.66 us  [call(): pl.pallas_call(kernel, out_shape=outs, in_specs=[VMEM] * len(args), out_s...]
where the time goes in v5:
time: 78.5 us; the launch traced here: 78.3 us
  starting transfers between devices  41.6 us (53%)
  waiting for transfers between devices  30.1 us (38%)
  Pallas kernels  4.11 us (5%)
  between operations  1.41 us (2%)
  local copies, waits for them, and re-layouts  1.13 us (1%)
    ppermute x6, starting transfers between devices, blocks_moved(): return lax.ppermute(value, AXES, pairs)  35.3 us
    ppermute x6, waiting for transfers between devices, blocks_moved(): return lax.ppermute(value, AXES, pairs)  30.1 us
    ppermute x3, starting transfers between devices, cores_swapped(): lax.ppermute(value, AXES, [(i, i ^ 1) for i in range(lax.axis_size(AXES))])  6.28 us
    pallas_call x5, Pallas kernels, call(): pl.pallas_call(kernel, out_shape=outs, in_specs=[VMEM] * len(args), out_s...  3.66 us
  transfers between devices with their start and end apart: 9, of which 4 were waited for; matrix products, arithmetic and copies ran while one was open for 0% of the time, Pallas kernels for 2%

profile of v5, /device:TPU:32, one launch (start us, length us, event | category | flops | bytes accessed | tf_op | source)
XLA Modules:
  0.0 78.3 jit_solution(11006355471813958008)
XLA Ops:
  1.3 0.0 copy-start
  1.3 1.1 %copy-done = bf16[512,768]{1,0:T(8,128)(2,1)S(1)} copy-done((bf16[512,768]{1,0:T(8,128)(2,1)S(1)}, bf16[512,768]{1,0:T(8,128)(2,1)}, u32[]{:S(2)}) %copy-start) | copy-done | bytes 786456
  2.4 0.4 shard_map.49.unit_ref
  2.9 4.3 %collective-permute-start.1 = (bf16[528,768]{1,0:T(8,128)(2,1)S(1)}, bf16[528,768]{1,0:T(8,128)(2,1)S(1)}, u32[]{:S(2)}, u32[]{:S(2)}) collective-permute-start(bf16[528,768]{1,0:T(8,128)(2,1)S(1)} %shard_map.49.unit_ref), channel_id=1, source_target_pairs={{0,2},{1,3},{2,4},{3,5},{4,6},{5,7},{6,8},{7,9},{8,10},{9,11},{10,... | collective-permute-start | bytes 2433032 | tf_op jit(solution)/shard_map/ppermute | solution.py:43
  7.2 12.1 %collective-permute-start = (bf16[528,768]{1,0:T(8,128)(2,1)S(1)}, bf16[528,768]{1,0:T(8,128)(2,1)S(1)}, u32[]{:S(2)}, u32[]{:S(2)}) collective-permute-start(bf16[528,768]{1,0:T(8,128)(2,1)S(1)} %shard_map.49.unit_ref), channel_id=1, source_target_pairs={{4,0},{5,1},{6,2},{7,3},{8,4},{9,5},{10,6},{11,7},{12,8},{13,9},{1... | collective-permute-start | bytes 2433032 | tf_op jit(solution)/shard_map/ppermute | solution.py:43
  19.3 14.7 %collective-permute-done.1.near_ref = bf16[528,768]{1,0:T(8,128)(2,1)S(1)} collective-permute-done((bf16[528,768]{1,0:T(8,128)(2,1)S(1)}, bf16[528,768]{1,0:T(8,128)(2,1)S(1)}, u32[]{:S(2)}, u32[]{:S(2)}) %collective-permute-start.1) | collective-permute-done | bytes 811040 | tf_op jit(solution)/shard_map/ppermute | solution.py:43
  34.0 1.9 %collective-permute-start.2 = (bf16[528,768]{1,0:T(8,128)(2,1)S(1)}, bf16[528,768]{1,0:T(8,128)(2,1)S(1)}, u32[]{:S(2)}, u32[]{:S(2)}) collective-permute-start(bf16[528,768]{1,0:T(8,128)(2,1)S(1)} %shard_map.49.unit_ref), channel_id=1, source_target_pairs={{0,1},{1,0},{2,3},{3,2},{4,5},{5,4},{6,7},{7,6},{8,9},{9,8},{10,11... | collective-permute-start | bytes 2433032 | tf_op jit(solution)/shard_map/ppermute | solution.py:47
  35.9 1.3 %collective-permute-start.4 = (bf16[528,768]{1,0:T(8,128)(2,1)S(1)}, bf16[528,768]{1,0:T(8,128)(2,1)S(1)}, u32[]{:S(2)}, u32[]{:S(2)}) collective-permute-start(bf16[528,768]{1,0:T(8,128)(2,1)S(1)} %collective-permute-done.1.near_ref), channel_id=1, source_target_pairs={{1,2},{3,4},{5,6},{7,8},{9,10},{11,12},{13,14},{15,16},{17,18},{19... | collective-permute-start | bytes 2433032 | tf_op jit(solution)/shard_map/ppermute | solution.py:43
  37.2 2.5 %collective-permute-start.3 = (bf16[528,768]{1,0:T(8,128)(2,1)S(1)}, bf16[528,768]{1,0:T(8,128)(2,1)S(1)}, u32[]{:S(2)}, u32[]{:S(2)}) collective-permute-start(bf16[528,768]{1,0:T(8,128)(2,1)S(1)} %collective-permute-done.1.near_ref), channel_id=1, source_target_pairs={{0,1},{1,0},{2,3},{3,2},{4,5},{5,4},{6,7},{7,6},{8,9},{9,8},{10,11... | collective-permute-start | bytes 2433032 | tf_op jit(solution)/shard_map/ppermute | solution.py:47
  39.6 1.2 %shard_map.50.stats_ref = f32[4,512]{1,0:T(4,128)S(1)} custom-call(bf16[528,768]{1,0:T(8,128)(2,1)S(1)} %shard_map.49.unit_ref, bf16[528,768]{1,0:T(8,128)(2,1)S(1)} %collective-permute-done.1.near_ref), custom_call_target="tpu_custom_call" | custom-call | bytes 1622016 | tf_op jit(solution)/shard_map/pallas_call | solution.py:30
  40.8 10.1 %collective-permute-done.far_ref = bf16[528,768]{1,0:T(8,128)(2,1)S(1)} collective-permute-done((bf16[528,768]{1,0:T(8,128)(2,1)S(1)}, bf16[528,768]{1,0:T(8,128)(2,1)S(1)}, u32[]{:S(2)}, u32[]{:S(2)}) %collective-permute-start) | collective-permute-done | bytes 811040 | tf_op jit(solution)/shard_map/ppermute | solution.py:43
  50.9 0.0 collective-permute-done.2.other_ref
  50.9 3.9 %collective-permute-done.4.back_ref = bf16[528,768]{1,0:T(8,128)(2,1)S(1)} collective-permute-done((bf16[528,768]{1,0:T(8,128)(2,1)S(1)}, bf16[528,768]{1,0:T(8,128)(2,1)S(1)}, u32[]{:S(2)}, u32[]{:S(2)}) %collective-permute-start.4) | collective-permute-done | bytes 811040 | tf_op jit(solution)/shard_map/ppermute | solution.py:43
  54.9 0.0 collective-permute-done.3.near_x_ref
  54.9 1.5 %shard_map.51 = (f32[3,768]{1,0:T(4,128)S(1)}, f32[6,768]{1,0:T(8,128)S(1)}, f32[3,768]{1,0:T(4,128)S(1)}, f32[3,768]{1,0:T(4,128)S(1)}, f32[3,768]{1,0:T(4,128)S(1)}) custom-call(bf16[528,768]{1,0:T(8,128)(2,1)S(1)} %collective-permute-done.far_ref, bf16[528,768]{1,0:T(8,128)(2,1)S(1)} %shard_map.49.unit_ref, ...), custom_call_target="tpu_custom_call" | custom-call | bytes 4874240 | tf_op jit(solution)/shard_map/pallas_call | solution.py:30
  56.4 1.9 %collective-permute-start.5 = (f32[6,768]{1,0:T(8,128)S(1)}, f32[6,768]{1,0:T(8,128)S(1)}, u32[]{:S(2)}, u32[]{:S(2)}) collective-permute-start(f32[6,768]{1,0:T(8,128)S(1)} %get-tuple-element.15), channel_id=1, source_target_pairs={{0,1},{1,0},{2,3},{3,2},{4,5},{5,4},{6,7},{7,6},{8,9},{9,8},{10,11... | collective-permute-start | bytes 55304 | tf_op jit(solution)/shard_map/ppermute | solution.py:47
  58.3 1.9 %collective-permute-start.6 = (f32[3,768]{1,0:T(4,128)S(1)}, f32[3,768]{1,0:T(4,128)S(1)}, u32[]{:S(2)}, u32[]{:S(2)}) collective-permute-start(f32[3,768]{1,0:T(4,128)S(1)} %get-tuple-element.16), channel_id=1, source_target_pairs={{0,4},{1,5},{2,6},{3,7},{4,8},{5,9},{6,10},{7,11},{8,12},{9,13},{1... | collective-permute-start | bytes 27656 | tf_op jit(solution)/shard_map/ppermute | solution.py:43
  60.2 0.0 collective-permute-done.5.refs_1_
  60.3 11.4 %collective-permute-start.7 = (f32[3,768]{1,0:T(4,128)S(1)}, f32[3,768]{1,0:T(4,128)S(1)}, u32[]{:S(2)}, u32[]{:S(2)}) collective-permute-start(f32[3,768]{1,0:T(4,128)S(1)} %shard_map.52), channel_id=1, source_target_pairs={{2,0},{3,1},{4,2},{5,3},{6,4},{7,5},{8,6},{9,7},{10,8},{11,9},{12,... | collective-permute-start | bytes 27656 | tf_op jit(solution)/shard_map/ppermute | solution.py:43
  71.6 4.4 %collective-permute-start.8 = (f32[3,768]{1,0:T(4,128)S(1)}, f32[3,768]{1,0:T(4,128)S(1)}, u32[]{:S(2)}, u32[]{:S(2)}) collective-permute-start(f32[3,768]{1,0:T(4,128)S(1)} %get-tuple-element.19), channel_id=1, source_target_pairs={{4,1},{6,3},{8,5},{10,7},{12,9},{14,11},{16,13},{18,15},{20,17},{2... | collective-permute-start | bytes 27656 | tf_op jit(solution)/shard_map/ppermute | solution.py:43
  76.0 0.0 collective-permute-done.6.refs_2_
  76.0 0.0 collective-permute-done.7.refs_3_
  76.0 1.3 %collective-permute-done.8.back_ref = f32[3,768]{1,0:T(4,128)S(1)} collective-permute-done((f32[3,768]{1,0:T(4,128)S(1)}, f32[3,768]{1,0:T(4,128)S(1)}, u32[]{:S(2)}, u32[]{:S(2)}) %collective-permute-start.8) | collective-permute-done | bytes 9248 | tf_op jit(solution)/shard_map/ppermute | solution.py:43
  77.4 1.0 %shard_map.54 = (f32[1,512]{1,0:T(1,128)}, f32[1,512]{1,0:T(1,128)}, f32[1,512]{1,0:T(1,128)}) custom-call(bf16[528,768]{1,0:T(8,128)(2,1)S(1)} %shard_map.49.unit_ref, f32[3,768]{1,0:T(4,128)S(1)} %shard_map.53.most_ref, f32[3,768]{1,0:T(4,128)S(1)} %collective-permute-done.8.back_ref), custom_call_target="tpu_custom_call" | custom-call | bytes 829440 | tf_op jit(solution)/shard_map/pallas_call | solution.py:30
  (2 shorter events, 0.0 us)
Async XLA Ops:
  1.3 1.1 %copy-start = (bf16[512,768]{1,0:T(8,128)(2,1)S(1)}, bf16[512,768]{1,0:T(8,128)(2,1)}, u32[]{:S(2)}) copy-start(bf16[512,768]{1,0:T(8,128)(2,1)} %emb_ref.1) | copy-start | bytes 2359300
  2.9 31.1 %collective-permute-start.1 = (bf16[528,768]{1,0:T(8,128)(2,1)S(1)}, bf16[528,768]{1,0:T(8,128)(2,1)S(1)}, u32[]{:S(2)}, u32[]{:S(2)}) collective-permute-start(bf16[528,768]{1,0:T(8,128)(2,1)S(1)} %shard_map.49.unit_ref), channel_id=1, source_target_pairs={{0,2},{1,3},{2,4},{3,5},{4,6},{5,7},{6,8},{7,9},{8,10},{9,11},{10,... | collective-permute-start | bytes 2433032 | tf_op jit(solution)/shard_map/ppermute | solution.py:43
  7.2 43.8 %collective-permute-start = (bf16[528,768]{1,0:T(8,128)(2,1)S(1)}, bf16[528,768]{1,0:T(8,128)(2,1)S(1)}, u32[]{:S(2)}, u32[]{:S(2)}) collective-permute-start(bf16[528,768]{1,0:T(8,128)(2,1)S(1)} %shard_map.49.unit_ref), channel_id=1, source_target_pairs={{4,0},{5,1},{6,2},{7,3},{8,4},{9,5},{10,6},{11,7},{12,8},{13,9},{1... | collective-permute-start | bytes 2433032 | tf_op jit(solution)/shard_map/ppermute | solution.py:43
  34.0 17.0 %collective-permute-start.2 = (bf16[528,768]{1,0:T(8,128)(2,1)S(1)}, bf16[528,768]{1,0:T(8,128)(2,1)S(1)}, u32[]{:S(2)}, u32[]{:S(2)}) collective-permute-start(bf16[528,768]{1,0:T(8,128)(2,1)S(1)} %shard_map.49.unit_ref), channel_id=1, source_target_pairs={{0,1},{1,0},{2,3},{3,2},{4,5},{5,4},{6,7},{7,6},{8,9},{9,8},{10,11... | collective-permute-start | bytes 2433032 | tf_op jit(solution)/shard_map/ppermute | solution.py:47
  35.9 19.0 %collective-permute-start.4 = (bf16[528,768]{1,0:T(8,128)(2,1)S(1)}, bf16[528,768]{1,0:T(8,128)(2,1)S(1)}, u32[]{:S(2)}, u32[]{:S(2)}) collective-permute-start(bf16[528,768]{1,0:T(8,128)(2,1)S(1)} %collective-permute-done.1.near_ref), channel_id=1, source_target_pairs={{1,2},{3,4},{5,6},{7,8},{9,10},{11,12},{13,14},{15,16},{17,18},{19... | collective-permute-start | bytes 2433032 | tf_op jit(solution)/shard_map/ppermute | solution.py:43
  37.2 17.7 %collective-permute-start.3 = (bf16[528,768]{1,0:T(8,128)(2,1)S(1)}, bf16[528,768]{1,0:T(8,128)(2,1)S(1)}, u32[]{:S(2)}, u32[]{:S(2)}) collective-permute-start(bf16[528,768]{1,0:T(8,128)(2,1)S(1)} %collective-permute-done.1.near_ref), channel_id=1, source_target_pairs={{0,1},{1,0},{2,3},{3,2},{4,5},{5,4},{6,7},{7,6},{8,9},{9,8},{10,11... | collective-permute-start | bytes 2433032 | tf_op jit(solution)/shard_map/ppermute | solution.py:47
  56.4 3.9 %collective-permute-start.5 = (f32[6,768]{1,0:T(8,128)S(1)}, f32[6,768]{1,0:T(8,128)S(1)}, u32[]{:S(2)}, u32[]{:S(2)}) collective-permute-start(f32[6,768]{1,0:T(8,128)S(1)} %get-tuple-element.15), channel_id=1, source_target_pairs={{0,1},{1,0},{2,3},{3,2},{4,5},{5,4},{6,7},{7,6},{8,9},{9,8},{10,11... | collective-permute-start | bytes 55304 | tf_op jit(solution)/shard_map/ppermute | solution.py:47
  58.3 17.7 %collective-permute-start.6 = (f32[3,768]{1,0:T(4,128)S(1)}, f32[3,768]{1,0:T(4,128)S(1)}, u32[]{:S(2)}, u32[]{:S(2)}) collective-permute-start(f32[3,768]{1,0:T(4,128)S(1)} %get-tuple-element.16), channel_id=1, source_target_pairs={{0,4},{1,5},{2,6},{3,7},{4,8},{5,9},{6,10},{7,11},{8,12},{9,13},{1... | collective-permute-start | bytes 27656 | tf_op jit(solution)/shard_map/ppermute | solution.py:43
  60.3 15.8 %collective-permute-start.7 = (f32[3,768]{1,0:T(4,128)S(1)}, f32[3,768]{1,0:T(4,128)S(1)}, u32[]{:S(2)}, u32[]{:S(2)}) collective-permute-start(f32[3,768]{1,0:T(4,128)S(1)} %shard_map.52), channel_id=1, source_target_pairs={{2,0},{3,1},{4,2},{5,3},{6,4},{7,5},{8,6},{9,7},{10,8},{11,9},{12,... | collective-permute-start | bytes 27656 | tf_op jit(solution)/shard_map/ppermute | solution.py:43
  71.6 5.8 %collective-permute-start.8 = (f32[3,768]{1,0:T(4,128)S(1)}, f32[3,768]{1,0:T(4,128)S(1)}, u32[]{:S(2)}, u32[]{:S(2)}) collective-permute-start(f32[3,768]{1,0:T(4,128)S(1)} %get-tuple-element.19), channel_id=1, source_target_pairs={{4,1},{6,3},{8,5},{10,7},{12,9},{14,11},{16,13},{18,15},{20,17},{2... | collective-permute-start | bytes 27656 | tf_op jit(solution)/shard_map/ppermute | solution.py:43

commit v6 on v5

--- a/solution.py
+++ b/solution.py
@@ -195,10 +195,10 @@
     last_flag = jnp.where(second, tails[0][1], far_tail[1]) == jnp.where(second, tails[1][1], back_tail[1])
     flags = [tag == far_tail[1] for _, tag in tails]
     near_flag = tails[1][1] == tails[2][1]
-    def far_tiles():
-        found, parts = [Columns(rows) for _ in blocks], []
+    def far_tiles(pair):
+        found, parts = [Columns(rows) for _ in blocks[pair]], []
         for at in range(0, rows, STRIP):
-            strip(far_ref[at : at + STRIP, :], blocks, flags, found, parts)
+            strip(far_ref[at : at + STRIP, :], blocks[pair], flags[pair], found, parts)
         return [value for column in found for value in (column.top, column.mass)] + whole(parts)
 
     def near_tiles():
@@ -219,10 +219,10 @@
         nothing = [jnp.full((1, rows), LOW, F32), jnp.zeros((1, rows), F32)] * pairs
         return lax.cond(met, tiles, lambda: nothing)
 
-    found = where_met(flags, far_tiles, 5)
-    for at, column in enumerate(columns):
-        column.add(found[2 * at], found[2 * at + 1])
-    far = found[8:]
+    for pair in (slice(0, 2), slice(2, 4)):
+        found = where_met(flags[pair], functools.partial(far_tiles, pair), 3)
+        for at, column in enumerate((*columns[pair], theirs)):
+            column.add(found[2 * at], found[2 * at + 1])
     found = where_met((near_flag,), near_tiles, 2)
     across.add(found[0], found[1])
     back_by = found[2:]
@@ -242,7 +242,6 @@
     mine.meet(tails[1][0], on)
     beyond.meet(far_tail[0], off)
     theirs.meet(back_tail[0], off)
-    theirs.add(*far)
     theirs.add(*extra, off[:, :rows])
     mine.add(*extra, on[:, :rows])
     across.add(last.top, last.mass, on[:, :rows])

time: 78.5 us -> 78.2 us (level)
  no operation moved by 1% of the time
where the time goes in v6:
time: 78.2 us; the launch traced here: 78.8 us
  starting transfers between devices  42 us (54%)
  waiting for transfers between devices  30.1 us (38%)
  Pallas kernels  4.22 us (5%)
  between operations  1.41 us (2%)
  local copies, waits for them, and re-layouts  1.13 us (1%)
    ppermute x6, starting transfers between devices, blocks_moved(): return lax.ppermute(value, AXES, pairs)  35.7 us
    ppermute x6, waiting for transfers between devices, blocks_moved(): return lax.ppermute(value, AXES, pairs)  30.1 us
    ppermute x3, starting transfers between devices, cores_swapped(): lax.ppermute(value, AXES, [(i, i ^ 1) for i in range(lax.axis_size(AXES))])  6.28 us
    pallas_call x5, Pallas kernels, call(): pl.pallas_call(kernel, out_shape=outs, in_specs=[VMEM] * len(args), out_s...  3.78 us
  transfers between devices with their start and end apart: 9, of which 4 were waited for; matrix products, arithmetic and copies ran while one was open for 0% of the time, Pallas kernels for 2%

profile of v6, /device:TPU:32, one launch (start us, length us, event | category | flops | bytes accessed | tf_op | source)
XLA Modules:
  0.0 78.8 jit_solution(6305628462189095698)
XLA Ops:
  1.3 0.0 copy-start
  1.3 1.1 %copy-done = bf16[512,768]{1,0:T(8,128)(2,1)S(1)} copy-done((bf16[512,768]{1,0:T(8,128)(2,1)S(1)}, bf16[512,768]{1,0:T(8,128)(2,1)}, u32[]{:S(2)}) %copy-start) | copy-done | bytes 786456
  2.4 0.4 shard_map.49.unit_ref
  2.9 4.3 %collective-permute-start.1 = (bf16[528,768]{1,0:T(8,128)(2,1)S(1)}, bf16[528,768]{1,0:T(8,128)(2,1)S(1)}, u32[]{:S(2)}, u32[]{:S(2)}) collective-permute-start(bf16[528,768]{1,0:T(8,128)(2,1)S(1)} %shard_map.49.unit_ref), channel_id=1, source_target_pairs={{0,2},{1,3},{2,4},{3,5},{4,6},{5,7},{6,8},{7,9},{8,10},{9,11},{10,... | collective-permute-start | bytes 2433032 | tf_op jit(solution)/shard_map/ppermute | solution.py:43
  7.2 12.1 %collective-permute-start = (bf16[528,768]{1,0:T(8,128)(2,1)S(1)}, bf16[528,768]{1,0:T(8,128)(2,1)S(1)}, u32[]{:S(2)}, u32[]{:S(2)}) collective-permute-start(bf16[528,768]{1,0:T(8,128)(2,1)S(1)} %shard_map.49.unit_ref), channel_id=1, source_target_pairs={{4,0},{5,1},{6,2},{7,3},{8,4},{9,5},{10,6},{11,7},{12,8},{13,9},{1... | collective-permute-start | bytes 2433032 | tf_op jit(solution)/shard_map/ppermute | solution.py:43
  19.3 14.7 %collective-permute-done.1.near_ref = bf16[528,768]{1,0:T(8,128)(2,1)S(1)} collective-permute-done((bf16[528,768]{1,0:T(8,128)(2,1)S(1)}, bf16[528,768]{1,0:T(8,128)(2,1)S(1)}, u32[]{:S(2)}, u32[]{:S(2)}) %collective-permute-start.1) | collective-permute-done | bytes 811040 | tf_op jit(solution)/shard_map/ppermute | solution.py:43
  34.0 1.9 %collective-permute-start.2 = (bf16[528,768]{1,0:T(8,128)(2,1)S(1)}, bf16[528,768]{1,0:T(8,128)(2,1)S(1)}, u32[]{:S(2)}, u32[]{:S(2)}) collective-permute-start(bf16[528,768]{1,0:T(8,128)(2,1)S(1)} %shard_map.49.unit_ref), channel_id=1, source_target_pairs={{0,1},{1,0},{2,3},{3,2},{4,5},{5,4},{6,7},{7,6},{8,9},{9,8},{10,11... | collective-permute-start | bytes 2433032 | tf_op jit(solution)/shard_map/ppermute | solution.py:47
  35.9 1.3 %collective-permute-start.4 = (bf16[528,768]{1,0:T(8,128)(2,1)S(1)}, bf16[528,768]{1,0:T(8,128)(2,1)S(1)}, u32[]{:S(2)}, u32[]{:S(2)}) collective-permute-start(bf16[528,768]{1,0:T(8,128)(2,1)S(1)} %collective-permute-done.1.near_ref), channel_id=1, source_target_pairs={{1,2},{3,4},{5,6},{7,8},{9,10},{11,12},{13,14},{15,16},{17,18},{19... | collective-permute-start | bytes 2433032 | tf_op jit(solution)/shard_map/ppermute | solution.py:43
  37.2 2.5 %collective-permute-start.3 = (bf16[528,768]{1,0:T(8,128)(2,1)S(1)}, bf16[528,768]{1,0:T(8,128)(2,1)S(1)}, u32[]{:S(2)}, u32[]{:S(2)}) collective-permute-start(bf16[528,768]{1,0:T(8,128)(2,1)S(1)} %collective-permute-done.1.near_ref), channel_id=1, source_target_pairs={{0,1},{1,0},{2,3},{3,2},{4,5},{5,4},{6,7},{7,6},{8,9},{9,8},{10,11... | collective-permute-start | bytes 2433032 | tf_op jit(solution)/shard_map/ppermute | solution.py:47
  39.6 1.2 %shard_map.50.stats_ref = f32[4,512]{1,0:T(4,128)S(1)} custom-call(bf16[528,768]{1,0:T(8,128)(2,1)S(1)} %shard_map.49.unit_ref, bf16[528,768]{1,0:T(8,128)(2,1)S(1)} %collective-permute-done.1.near_ref), custom_call_target="tpu_custom_call" | custom-call | bytes 1622016 | tf_op jit(solution)/shard_map/pallas_call | solution.py:30
  40.8 10.1 %collective-permute-done.far_ref = bf16[528,768]{1,0:T(8,128)(2,1)S(1)} collective-permute-done((bf16[528,768]{1,0:T(8,128)(2,1)S(1)}, bf16[528,768]{1,0:T(8,128)(2,1)S(1)}, u32[]{:S(2)}, u32[]{:S(2)}) %collective-permute-start) | collective-permute-done | bytes 811040 | tf_op jit(solution)/shard_map/ppermute | solution.py:43
  50.9 0.0 collective-permute-done.2.other_ref
  50.9 3.9 %collective-permute-done.4.back_ref = bf16[528,768]{1,0:T(8,128)(2,1)S(1)} collective-permute-done((bf16[528,768]{1,0:T(8,128)(2,1)S(1)}, bf16[528,768]{1,0:T(8,128)(2,1)S(1)}, u32[]{:S(2)}, u32[]{:S(2)}) %collective-permute-start.4) | collective-permute-done | bytes 811040 | tf_op jit(solution)/shard_map/ppermute | solution.py:43
  54.9 0.0 collective-permute-done.3.near_x_ref
  54.9 1.6 %shard_map.51 = (f32[3,768]{1,0:T(4,128)S(1)}, f32[6,768]{1,0:T(8,128)S(1)}, f32[3,768]{1,0:T(4,128)S(1)}, f32[3,768]{1,0:T(4,128)S(1)}, f32[3,768]{1,0:T(4,128)S(1)}) custom-call(bf16[528,768]{1,0:T(8,128)(2,1)S(1)} %collective-permute-done.far_ref, bf16[528,768]{1,0:T(8,128)(2,1)S(1)} %shard_map.49.unit_ref, ...), custom_call_target="tpu_custom_call" | custom-call | bytes 4874240 | tf_op jit(solution)/shard_map/pallas_call | solution.py:30
  56.5 1.9 %collective-permute-start.5 = (f32[6,768]{1,0:T(8,128)S(1)}, f32[6,768]{1,0:T(8,128)S(1)}, u32[]{:S(2)}, u32[]{:S(2)}) collective-permute-start(f32[6,768]{1,0:T(8,128)S(1)} %get-tuple-element.15), channel_id=1, source_target_pairs={{0,1},{1,0},{2,3},{3,2},{4,5},{5,4},{6,7},{7,6},{8,9},{9,8},{10,11... | collective-permute-start | bytes 55304 | tf_op jit(solution)/shard_map/ppermute | solution.py:47
  58.4 2.2 %collective-permute-start.6 = (f32[3,768]{1,0:T(4,128)S(1)}, f32[3,768]{1,0:T(4,128)S(1)}, u32[]{:S(2)}, u32[]{:S(2)}) collective-permute-start(f32[3,768]{1,0:T(4,128)S(1)} %get-tuple-element.16), channel_id=1, source_target_pairs={{0,4},{1,5},{2,6},{3,7},{4,8},{5,9},{6,10},{7,11},{8,12},{9,13},{1... | collective-permute-start | bytes 27656 | tf_op jit(solution)/shard_map/ppermute | solution.py:43
  60.7 0.0 collective-permute-done.5.refs_1_
  60.7 11.4 %collective-permute-start.7 = (f32[3,768]{1,0:T(4,128)S(1)}, f32[3,768]{1,0:T(4,128)S(1)}, u32[]{:S(2)}, u32[]{:S(2)}) collective-permute-start(f32[3,768]{1,0:T(4,128)S(1)} %shard_map.52), channel_id=1, source_target_pairs={{2,0},{3,1},{4,2},{5,3},{6,4},{7,5},{8,6},{9,7},{10,8},{11,9},{12,... | collective-permute-start | bytes 27656 | tf_op jit(solution)/shard_map/ppermute | solution.py:43
  72.1 4.4 %collective-permute-start.8 = (f32[3,768]{1,0:T(4,128)S(1)}, f32[3,768]{1,0:T(4,128)S(1)}, u32[]{:S(2)}, u32[]{:S(2)}) collective-permute-start(f32[3,768]{1,0:T(4,128)S(1)} %get-tuple-element.19), channel_id=1, source_target_pairs={{4,1},{6,3},{8,5},{10,7},{12,9},{14,11},{16,13},{18,15},{20,17},{2... | collective-permute-start | bytes 27656 | tf_op jit(solution)/shard_map/ppermute | solution.py:43
  76.5 0.0 collective-permute-done.6.refs_2_
  76.5 0.0 collective-permute-done.7.refs_3_
  76.5 1.3 %collective-permute-done.8.back_ref = f32[3,768]{1,0:T(4,128)S(1)} collective-permute-done((f32[3,768]{1,0:T(4,128)S(1)}, f32[3,768]{1,0:T(4,128)S(1)}, u32[]{:S(2)}, u32[]{:S(2)}) %collective-permute-start.8) | collective-permute-done | bytes 9248 | tf_op jit(solution)/shard_map/ppermute | solution.py:43
  77.8 1.0 %shard_map.54 = (f32[1,512]{1,0:T(1,128)}, f32[1,512]{1,0:T(1,128)}, f32[1,512]{1,0:T(1,128)}) custom-call(bf16[528,768]{1,0:T(8,128)(2,1)S(1)} %shard_map.49.unit_ref, f32[3,768]{1,0:T(4,128)S(1)} %shard_map.53.most_ref, f32[3,768]{1,0:T(4,128)S(1)} %collective-permute-done.8.back_ref), custom_call_target="tpu_custom_call" | custom-call | bytes 829440 | tf_op jit(solution)/shard_map/pallas_call | solution.py:30
  (2 shorter events, 0.0 us)
Async XLA Ops:
  1.3 1.1 %copy-start = (bf16[512,768]{1,0:T(8,128)(2,1)S(1)}, bf16[512,768]{1,0:T(8,128)(2,1)}, u32[]{:S(2)}) copy-start(bf16[512,768]{1,0:T(8,128)(2,1)} %emb_ref.1) | copy-start | bytes 2359300
  2.9 31.1 %collective-permute-start.1 = (bf16[528,768]{1,0:T(8,128)(2,1)S(1)}, bf16[528,768]{1,0:T(8,128)(2,1)S(1)}, u32[]{:S(2)}, u32[]{:S(2)}) collective-permute-start(bf16[528,768]{1,0:T(8,128)(2,1)S(1)} %shard_map.49.unit_ref), channel_id=1, source_target_pairs={{0,2},{1,3},{2,4},{3,5},{4,6},{5,7},{6,8},{7,9},{8,10},{9,11},{10,... | collective-permute-start | bytes 2433032 | tf_op jit(solution)/shard_map/ppermute | solution.py:43
  7.2 43.8 %collective-permute-start = (bf16[528,768]{1,0:T(8,128)(2,1)S(1)}, bf16[528,768]{1,0:T(8,128)(2,1)S(1)}, u32[]{:S(2)}, u32[]{:S(2)}) collective-permute-start(bf16[528,768]{1,0:T(8,128)(2,1)S(1)} %shard_map.49.unit_ref), channel_id=1, source_target_pairs={{4,0},{5,1},{6,2},{7,3},{8,4},{9,5},{10,6},{11,7},{12,8},{13,9},{1... | collective-permute-start | bytes 2433032 | tf_op jit(solution)/shard_map/ppermute | solution.py:43
  34.0 17.0 %collective-permute-start.2 = (bf16[528,768]{1,0:T(8,128)(2,1)S(1)}, bf16[528,768]{1,0:T(8,128)(2,1)S(1)}, u32[]{:S(2)}, u32[]{:S(2)}) collective-permute-start(bf16[528,768]{1,0:T(8,128)(2,1)S(1)} %shard_map.49.unit_ref), channel_id=1, source_target_pairs={{0,1},{1,0},{2,3},{3,2},{4,5},{5,4},{6,7},{7,6},{8,9},{9,8},{10,11... | collective-permute-start | bytes 2433032 | tf_op jit(solution)/shard_map/ppermute | solution.py:47
  35.9 19.0 %collective-permute-start.4 = (bf16[528,768]{1,0:T(8,128)(2,1)S(1)}, bf16[528,768]{1,0:T(8,128)(2,1)S(1)}, u32[]{:S(2)}, u32[]{:S(2)}) collective-permute-start(bf16[528,768]{1,0:T(8,128)(2,1)S(1)} %collective-permute-done.1.near_ref), channel_id=1, source_target_pairs={{1,2},{3,4},{5,6},{7,8},{9,10},{11,12},{13,14},{15,16},{17,18},{19... | collective-permute-start | bytes 2433032 | tf_op jit(solution)/shard_map/ppermute | solution.py:43
  37.2 17.7 %collective-permute-start.3 = (bf16[528,768]{1,0:T(8,128)(2,1)S(1)}, bf16[528,768]{1,0:T(8,128)(2,1)S(1)}, u32[]{:S(2)}, u32[]{:S(2)}) collective-permute-start(bf16[528,768]{1,0:T(8,128)(2,1)S(1)} %collective-permute-done.1.near_ref), channel_id=1, source_target_pairs={{0,1},{1,0},{2,3},{3,2},{4,5},{5,4},{6,7},{7,6},{8,9},{9,8},{10,11... | collective-permute-start | bytes 2433032 | tf_op jit(solution)/shard_map/ppermute | solution.py:47
  56.5 4.2 %collective-permute-start.5 = (f32[6,768]{1,0:T(8,128)S(1)}, f32[6,768]{1,0:T(8,128)S(1)}, u32[]{:S(2)}, u32[]{:S(2)}) collective-permute-start(f32[6,768]{1,0:T(8,128)S(1)} %get-tuple-element.15), channel_id=1, source_target_pairs={{0,1},{1,0},{2,3},{3,2},{4,5},{5,4},{6,7},{7,6},{8,9},{9,8},{10,11... | collective-permute-start | bytes 55304 | tf_op jit(solution)/shard_map/ppermute | solution.py:47
  58.4 18.0 %collective-permute-start.6 = (f32[3,768]{1,0:T(4,128)S(1)}, f32[3,768]{1,0:T(4,128)S(1)}, u32[]{:S(2)}, u32[]{:S(2)}) collective-permute-start(f32[3,768]{1,0:T(4,128)S(1)} %get-tuple-element.16), channel_id=1, source_target_pairs={{0,4},{1,5},{2,6},{3,7},{4,8},{5,9},{6,10},{7,11},{8,12},{9,13},{1... | collective-permute-start | bytes 27656 | tf_op jit(solution)/shard_map/ppermute | solution.py:43
  60.7 15.8 %collective-permute-start.7 = (f32[3,768]{1,0:T(4,128)S(1)}, f32[3,768]{1,0:T(4,128)S(1)}, u32[]{:S(2)}, u32[]{:S(2)}) collective-permute-start(f32[3,768]{1,0:T(4,128)S(1)} %shard_map.52), channel_id=1, source_target_pairs={{2,0},{3,1},{4,2},{5,3},{6,4},{7,5},{8,6},{9,7},{10,8},{11,9},{12,... | collective-permute-start | bytes 27656 | tf_op jit(solution)/shard_map/ppermute | solution.py:43
  72.1 5.8 %collective-permute-start.8 = (f32[3,768]{1,0:T(4,128)S(1)}, f32[3,768]{1,0:T(4,128)S(1)}, u32[]{:S(2)}, u32[]{:S(2)}) collective-permute-start(f32[3,768]{1,0:T(4,128)S(1)} %get-tuple-element.19), channel_id=1, source_target_pairs={{4,1},{6,3},{8,5},{10,7},{12,9},{14,11},{16,13},{18,15},{20,17},{2... | collective-permute-start | bytes 27656 | tf_op jit(solution)/shard_map/ppermute | solution.py:43
